TPU v7x, 32 devices: a whole 2x2x4 slice. The times are simulated.
32 devices in a mesh: dp: 8 (over y, x, core), tensor: 4 (over z).
Axes of the slice: x: 2, y: 2, z: 4, core: 2. Of those that a mesh axis runs over, the one named last changes fastest.
Arguments:
- tokens: bfloat16 [8192, 2048], P(('dp', 'tensor')), may hold values from -6 to 6
- seq_lengths: int32 [8, 2], P('dp'), may hold values from 1 to 768, 1024 in all within a row
- attn_gain: float32 [2048], replicated, may hold values from 0.1 to 1.9
- mlp_gain: float32 [2048], replicated, may hold values from 0.1 to 1.9
- q_gain: float32 [128], replicated, may hold values from 0.1 to 1.9
- k_gain: float32 [128], replicated, may hold values from 0.1 to 1.9
- w_query: bfloat16 [2048, 2048], P(None, 'tensor'), may hold values from -0.125 to 0.125
- key_weight: bfloat16 [2048, 1024], P(None, 'tensor'), may hold values from -0.125 to 0.125
- value_weight: bfloat16 [2048, 1024], P(None, 'tensor'), may hold values from -0.125 to 0.125
- w_out: bfloat16 [2048, 2048], P('tensor'), may hold values from -0.5 to 0.5
- w_gate: bfloat16 [2048, 6144], P(None, 'tensor'), may hold values from -0.125 to 0.125
- w_up: bfloat16 [2048, 6144], P(None, 'tensor'), may hold values from -0.125 to 0.125
- w_down: bfloat16 [6144, 2048], P('tensor'), may hold values from -0.078125 to 0.078125
- out_grad: bfloat16 [8192, 2048], P(('dp', 'tensor')), may hold values from -6 to 6
Outputs:
- output: bfloat16 [8192, 2048], P(('dp', 'tensor'))
- token_grad: bfloat16 [8192, 2048], P(('dp', 'tensor'))
- attn_gain_grad: float32 [2048], replicated
- mlp_gain_grad: float32 [2048], replicated
- q_gain_grad: float32 [128], replicated
- k_gain_grad: float32 [128], replicated
- w_query_grad: float32 [2048, 2048], P('dp', 'tensor')
- w_key_grad: float32 [2048, 1024], P('dp', 'tensor')
- w_value_grad: float32 [2048, 1024], P('dp', 'tensor')
- w_out_grad: float32 [2048, 2048], P('tensor', 'dp')
- w_gate_grad: float32 [2048, 6144], P('dp', 'tensor')
- w_up_grad: float32 [2048, 6144], P('dp', 'tensor')
- w_down_grad: float32 [6144, 2048], P('tensor', 'dp')
Inputs may be any that keep to these rules, and one draw needn't show every extreme that they name: `seq_lengths`: row d lists in order the lengths of the 2 sequences packed one after another into the 1024 tokens of index d of dp; each row sums to 1024 and its longest is at most 768.
All inputs are finite; a program needn't handle non-finite values.
Results may differ from a plain program's by a relative error of at most 0.02.
Values may be sent and summed in bfloat16 or wider, within the bound.
No kernel may reach another device: no remote copies, remote signals or barrier semaphores. Data moves between devices by JAX's collectives and lax.ppermute only.
A program may use at most 192 MiB of HBM per device.

v0:
```python
import jax
import jax.numpy as jnp
from jax import lax
from jax.sharding import PartitionSpec as P

NORM_EPSILON = 1e-06
ROPE_BASE = 1000000.0
MASK_FILL = -1e30


def normed_with_scale(values):
    inv_root = lax.rsqrt(jnp.mean(values * values, axis=-1, keepdims=True) + NORM_EPSILON)
    return (values * inv_root, inv_root)


def norm_back(grad_normed, normal, inv_root):
    return inv_root * (
        grad_normed - normal * jnp.mean(grad_normed * normal, axis=-1, keepdims=True)
    )


def product(first_operand, second_operand):
    return jnp.dot(first_operand, second_operand, preferred_element_type=jnp.float32)


def product_by_transpose(first_operand, second_operand):
    return lax.dot_general(
        first_operand, second_operand, (((1,), (1,)), ((), ())), preferred_element_type=jnp.float32
    )


def transpose_product(first_operand, second_operand):
    return lax.dot_general(
        first_operand, second_operand, (((0,), (0,)), ((), ())), preferred_element_type=jnp.float32
    )


def positions_of(lengths, count_of_rows):
    seq_ends = jnp.cumsum(lengths, dtype=jnp.int32)
    starts = seq_ends - lengths
    place_index = jnp.arange(count_of_rows, dtype=jnp.int32)
    segment = jnp.sum(
        (place_index[:, None] >= seq_ends[None, :]).astype(jnp.int32), axis=1, dtype=jnp.int32
    )
    belongs = segment[:, None] == jnp.arange(lengths.shape[0], dtype=jnp.int32)[None, :]
    offset = jnp.sum(jnp.where(belongs, starts[None, :], 0), axis=1, dtype=jnp.int32)
    return (segment, place_index - offset)


def rope_tables(position, head_width):
    half_width = head_width // 2
    frequency = ROPE_BASE ** (-2.0 * jnp.arange(half_width, dtype=jnp.float32) / head_width)
    angles = position.astype(jnp.float32)[:, None] * frequency[None, :]
    cosine_table = jnp.concatenate([jnp.cos(angles), jnp.cos(angles)], axis=1)
    sine_table = jnp.concatenate([jnp.sin(angles), jnp.sin(angles)], axis=1)
    return (cosine_table[:, None, :], sine_table[:, None, :])


def rotate(values):
    half_width = values.shape[-1] // 2
    return jnp.concatenate([-values[..., half_width:], values[..., :half_width]], axis=-1)


def rotate_backward(values):
    half_width = values.shape[-1] // 2
    return jnp.concatenate([values[..., half_width:], -values[..., :half_width]], axis=-1)


def apply_rope(values, cosine_table, sine_table):
    return values * cosine_table + rotate(values) * sine_table


def rope_backward(grads, cosine_table, sine_table):
    return grads * cosine_table + rotate_backward(grads * sine_table)


def tile_mask(segment, first_row, tile_rows):
    row_place = first_row + jnp.arange(tile_rows, dtype=jnp.int32)
    row_segment = lax.dynamic_slice_in_dim(segment, first_row, tile_rows, 0)
    columns = jnp.arange(segment.shape[0], dtype=jnp.int32)
    return (row_segment[:, None] == segment[None, :]) & (row_place[:, None] >= columns[None, :])


def local(
    tokens,
    seq_lengths,
    attn_gain,
    mlp_gain,
    q_gain,
    k_gain,
    w_query,
    key_weight,
    value_weight,
    w_out,
    w_gate,
    w_up,
    w_down,
    out_grad,
):
    shard_rows = tokens.shape[0]
    block_rows = shard_rows * lax.axis_size("tensor")
    head_dim = q_gain.shape[0]
    query_heads = w_query.shape[1] // head_dim
    kv_heads = key_weight.shape[1] // head_dim
    group_width = query_heads // kv_heads
    tile_rows = min(512, block_rows)
    tile_count = block_rows // tile_rows
    segment, position = positions_of(seq_lengths[0], block_rows)
    cosine_table, sine_table = rope_tables(position, head_dim)
    resid_in = tokens.astype(jnp.float32)
    normal_one, scale_one = normed_with_scale(resid_in)
    attention_start = (normal_one * attn_gain).astype(jnp.bfloat16)
    entry_all = lax.all_gather(attention_start, "tensor", axis=0, tiled=True)
    query_raw = product(entry_all, w_query).reshape(block_rows, query_heads, head_dim)
    key_unnormed = product(entry_all, key_weight).reshape(block_rows, kv_heads, head_dim)
    value_operand = (
        product(entry_all, value_weight)
        .astype(jnp.bfloat16)
        .reshape(block_rows, kv_heads, head_dim)
    )
    query_normal, query_scale = normed_with_scale(query_raw)
    key_normal, key_scale = normed_with_scale(key_unnormed)
    query_operand = (
        apply_rope(query_normal * q_gain, cosine_table, sine_table) * head_dim ** (-0.5)
    ).astype(jnp.bfloat16)
    key_side = apply_rope(key_normal * k_gain, cosine_table, sine_table).astype(jnp.bfloat16)
    query_tiles = query_operand.reshape(tile_count, tile_rows, kv_heads, group_width, head_dim)
    tile_index = jnp.arange(tile_count, dtype=jnp.int32)

    def forward_tile(operands):
        query_rows, number = operands
        visible = tile_mask(segment, number * tile_rows, tile_rows)
        scores = jnp.einsum(
            "qhgd,shd->hgqs", query_rows, key_side, preferred_element_type=jnp.float32
        )
        scores = jnp.where(visible, scores, MASK_FILL)
        row_peak = jnp.max(scores, axis=-1, keepdims=True)
        spread = jnp.exp(scores - row_peak)
        exp_total = jnp.sum(spread, axis=-1, keepdims=True)
        weights_low = (spread / exp_total).astype(jnp.bfloat16)
        mixed_rows = jnp.einsum(
            "hgqs,shd->qhgd", weights_low, value_operand, preferred_element_type=jnp.float32
        )
        return (mixed_rows, row_peak + jnp.log(exp_total))

    mixed_tiles, log_totals = lax.map(forward_tile, (query_tiles, tile_index))
    attn_mixed = mixed_tiles.reshape(block_rows, query_heads * head_dim).astype(jnp.bfloat16)
    hidden = resid_in + lax.psum_scatter(
        product(attn_mixed, w_out).astype(jnp.bfloat16), "tensor", scatter_dimension=0, tiled=True
    ).astype(jnp.float32)
    normal_two, scale_two = normed_with_scale(hidden)
    mlp_entry = (normal_two * mlp_gain).astype(jnp.bfloat16)
    mlp_all = lax.all_gather(mlp_entry, "tensor", axis=0, tiled=True)
    gate_proj = product(mlp_all, w_gate)
    up_proj = product(mlp_all, w_up)
    active = (gate_proj * jax.nn.sigmoid(gate_proj) * up_proj).astype(jnp.bfloat16)
    result = hidden + lax.psum_scatter(
        product(active, w_down).astype(jnp.bfloat16), "tensor", scatter_dimension=0, tiled=True
    ).astype(jnp.float32)
    output = result.astype(jnp.bfloat16)
    grad_all = lax.all_gather(out_grad, "tensor", axis=0, tiled=True)
    w_down_grad = transpose_product(active, grad_all)
    grad_active = product_by_transpose(grad_all, w_down)
    sigmoid_gate = jax.nn.sigmoid(gate_proj)
    grad_gate = (
        grad_active * up_proj * sigmoid_gate * (1.0 + gate_proj * (1.0 - sigmoid_gate))
    ).astype(jnp.bfloat16)
    grad_up = (grad_active * (gate_proj * sigmoid_gate)).astype(jnp.bfloat16)
    w_gate_grad = transpose_product(mlp_all, grad_gate)
    w_up_grad = transpose_product(mlp_all, grad_up)
    grad_inner = lax.psum_scatter(
        (product_by_transpose(grad_gate, w_gate) + product_by_transpose(grad_up, w_up)).astype(
            jnp.bfloat16
        ),
        "tensor",
        scatter_dimension=0,
        tiled=True,
    ).astype(jnp.float32)
    mlp_gain_part = jnp.sum(grad_inner * normal_two, axis=0)
    grad_hidden = out_grad.astype(jnp.float32) + norm_back(
        grad_inner * mlp_gain, normal_two, scale_two
    )
    grad_mid = lax.all_gather(grad_hidden.astype(jnp.bfloat16), "tensor", axis=0, tiled=True)
    w_out_grad = transpose_product(attn_mixed, grad_mid)
    grad_mixed = product_by_transpose(grad_mid, w_out).astype(jnp.bfloat16)
    grad_tiles = grad_mixed.reshape(tile_count, tile_rows, kv_heads, group_width, head_dim)

    def backward_tile(accumulated, operands):
        key_acc, value_acc = accumulated
        query_rows, grad_rows, log_total, number = operands
        visible = tile_mask(segment, number * tile_rows, tile_rows)
        scores = jnp.einsum(
            "qhgd,shd->hgqs", query_rows, key_side, preferred_element_type=jnp.float32
        )
        scores = jnp.where(visible, scores, MASK_FILL)
        soft_weights = jnp.exp(scores - log_total)
        grad_weights = jnp.einsum(
            "qhgd,shd->hgqs", grad_rows, value_operand, preferred_element_type=jnp.float32
        )
        inner_sum = jnp.sum(soft_weights * grad_weights, axis=-1, keepdims=True)
        grad_scores = (soft_weights * (grad_weights - inner_sum)).astype(jnp.bfloat16)
        grad_query_rows = jnp.einsum(
            "hgqs,shd->qhgd", grad_scores, key_side, preferred_element_type=jnp.float32
        )
        key_acc = key_acc + jnp.einsum(
            "hgqs,qhgd->shd", grad_scores, query_rows, preferred_element_type=jnp.float32
        )
        value_acc = value_acc + jnp.einsum(
            "hgqs,qhgd->shd",
            soft_weights.astype(jnp.bfloat16),
            grad_rows,
            preferred_element_type=jnp.float32,
        )
        return ((key_acc, value_acc), grad_query_rows)

    zeros_kv = jnp.zeros((block_rows, kv_heads, head_dim), jnp.float32)
    (grad_key_side, grad_value), grad_query_tiles = lax.scan(
        backward_tile, (zeros_kv, zeros_kv), (query_tiles, grad_tiles, log_totals, tile_index)
    )
    grad_query_side = grad_query_tiles.reshape(block_rows, query_heads, head_dim) * head_dim ** (
        -0.5
    )
    grad_query_normal = rope_backward(grad_query_side, cosine_table, sine_table)
    grad_key_normal = rope_backward(grad_key_side, cosine_table, sine_table)
    q_gain_part = jnp.sum(grad_query_normal * query_normal, axis=(0, 1))
    k_gain_part = jnp.sum(grad_key_normal * key_normal, axis=(0, 1))
    grad_query = (
        norm_back(grad_query_normal * q_gain, query_normal, query_scale)
        .astype(jnp.bfloat16)
        .reshape(block_rows, query_heads * head_dim)
    )
    grad_key = (
        norm_back(grad_key_normal * k_gain, key_normal, key_scale)
        .astype(jnp.bfloat16)
        .reshape(block_rows, kv_heads * head_dim)
    )
    grad_value_low = grad_value.astype(jnp.bfloat16).reshape(block_rows, kv_heads * head_dim)
    w_query_grad = transpose_product(entry_all, grad_query)
    w_key_grad = transpose_product(entry_all, grad_key)
    w_value_grad = transpose_product(entry_all, grad_value_low)
    query_part = product_by_transpose(grad_query, w_query)
    key_part = product_by_transpose(grad_key, key_weight)
    value_part = product_by_transpose(grad_value_low, value_weight)
    grad_entry = lax.psum_scatter(
        (query_part + key_part + value_part).astype(jnp.bfloat16),
        "tensor",
        scatter_dimension=0,
        tiled=True,
    ).astype(jnp.float32)
    attn_gain_part = jnp.sum(grad_entry * normal_one, axis=0)
    token_grad = (grad_hidden + norm_back(grad_entry * attn_gain, normal_one, scale_one)).astype(
        jnp.bfloat16
    )
    attn_gain_grad, mlp_gain_grad, q_gain_grad, k_gain_grad = lax.psum(
        (attn_gain_part, mlp_gain_part, q_gain_part, k_gain_part), ("dp", "tensor")
    )
    w_query_grad, w_key_grad, w_value_grad, w_out_grad, w_gate_grad, w_up_grad, w_down_grad = (
        lax.psum_scatter(
            w_query_grad.astype(jnp.bfloat16), "dp", scatter_dimension=0, tiled=True
        ).astype(jnp.float32),
        lax.psum_scatter(
            w_key_grad.astype(jnp.bfloat16), "dp", scatter_dimension=0, tiled=True
        ).astype(jnp.float32),
        lax.psum_scatter(
            w_value_grad.astype(jnp.bfloat16), "dp", scatter_dimension=0, tiled=True
        ).astype(jnp.float32),
        lax.psum_scatter(
            w_out_grad.astype(jnp.bfloat16), "dp", scatter_dimension=1, tiled=True
        ).astype(jnp.float32),
        lax.psum_scatter(
            w_gate_grad.astype(jnp.bfloat16), "dp", scatter_dimension=0, tiled=True
        ).astype(jnp.float32),
        lax.psum_scatter(
            w_up_grad.astype(jnp.bfloat16), "dp", scatter_dimension=0, tiled=True
        ).astype(jnp.float32),
        lax.psum_scatter(
            w_down_grad.astype(jnp.bfloat16), "dp", scatter_dimension=1, tiled=True
        ).astype(jnp.float32),
    )
    return (
        output,
        token_grad,
        attn_gain_grad,
        mlp_gain_grad,
        q_gain_grad,
        k_gain_grad,
        w_query_grad,
        w_key_grad,
        w_value_grad,
        w_out_grad,
        w_gate_grad,
        w_up_grad,
        w_down_grad,
    )


def solution(mesh):
    return jax.shard_map(
        local,
        mesh=mesh,
        in_specs=(
            P(("dp", "tensor"), None),
            P("dp", None),
            P(),
            P(),
            P(),
            P(),
            P(None, "tensor"),
            P(None, "tensor"),
            P(None, "tensor"),
            P("tensor", None),
            P(None, "tensor"),
            P(None, "tensor"),
            P("tensor", None),
            P(("dp", "tensor"), None),
        ),
        out_specs=(
            P(("dp", "tensor"), None),
            P(("dp", "tensor"), None),
            P(),
            P(),
            P(),
            P(),
            P("dp", "tensor"),
            P("dp", "tensor"),
            P("dp", "tensor"),
            P("tensor", "dp"),
            P("dp", "tensor"),
            P("dp", "tensor"),
            P("tensor", "dp"),
        ),
        check_vma=False,
    )
```

profile of v0, /device:TPU:0, one launch (start us, length us, event | category | flops | bytes accessed | tf_op | source)
XLA Modules:
  0.0 1147.6 jit_solution(3853062584959068873)
XLA Ops:
  17.0 4.2 multiply_cosine_fusion.1
  24.5 71.2 %all-gather.5.cloned.1.call-done = bf16[1024,2048]{1,0:T(8,128)(2,1)} async-done(((bf16[256,2048]{1,0:T(8,128)(2,1)}), bf16[1024,2048]{1,0:T(8,128)(2,1)}) %all-gather.5.cloned.1.call-update) | async-done | bytes 4194320 | tf_op jit(solution)/shard_map/all_gather | solution.py:113
  95.7 4.6 convolution_convert_fusion.10
  101.6 3.8 multiply_reduce_fusion.6
  109.3 5.9 multiply_reduce_fusion.3
  115.3 4.0 reshape.263
  122.7 3.1 concatenate.41
  128.9 5.0 fusion.69
  133.9 3.7 copy.59
  137.5 20.6 %while.29 = (s32[]{:T(128)}, bf16[2,512,2,2,128]{4,1,3,2,0:T(8,128)(2,1)}, f32[2,2,2,512,1]{3,2,1,4,0:T(2,128)S(1)}, s32[2]{0:T(128)S(1)}, s32[1024]{0:T(1024)S(...) while((s32[]{:T(128)}, ...), condition=%wide.region_9.10_spmd.clone, body=%wide.region_6.9_spmd.sunk.clone | while | flops 1094187520 | bytes 38353128 | solution.py:146
  158.2 3.6 copy.62
  164.1 6.2 convolution_convert_fusion.4
  170.4 75.5 %reduce-scatter.12.cloned.1.call-done = bf16[256,2048]{1,0:T(8,128)(2,1)} async-done(((bf16[1024,2048]{1,0:T(8,128)(2,1)}), bf16[256,2048]{1,0:T(8,128)(2,1)}) %reduce-scatter.12.cloned.1.call-update) | async-done | bytes 1048592 | tf_op jit(solution)/shard_map/reduce_scatter | solution.py:148
  250.8 80.8 %all-gather.7.cloned.1.call-done = bf16[1024,2048]{1,0:T(8,128)(2,1)} async-done(((bf16[256,2048]{1,0:T(8,128)(2,1)}), bf16[1024,2048]{1,0:T(8,128)(2,1)}) %all-gather.7.cloned.1.call-update) | async-done | bytes 4194320 | tf_op jit(solution)/shard_map/all_gather | solution.py:153
  331.6 12.9 %fusion.80 = f32[1024,1536]{1,0:T(8,128)} fusion(bf16[1024,2048]{1,0:T(8,128)(2,1)} %all-gather.7.cloned.1.call-done, bf16[2048,1536]{1,0:T(8,128)(2,1)} %param.29), kind=kOutput, calls=%fused_computation.168 | convolution fusion | flops 6442450944 | bytes 16777216 | tf_op jit(solution)/shard_map/dot_general | solution.py:23
  344.5 10.4 fusion.79
  354.9 57.5 %all-gather.9.cloned.1.call-done = bf16[1024,2048]{1,0:T(8,128)(2,1)} async-done(((bf16[256,2048]{1,0:T(8,128)(2,1)}), bf16[1024,2048]{1,0:T(8,128)(2,1)}) %all-gather.9.cloned.1.call-update) | async-done | bytes 4194320 | tf_op jit(solution)/shard_map/all_gather | solution.py:161
  412.4 15.9 %multiply_convert_fusion = (bf16[1024,1536]{1,0:T(8,128)(2,1)S(1)}, bf16[1024,1536]{1,0:T(8,128)(2,1)S(1)}, bf16[1024,1536]{1,0:T(8,128)(2,1)}) fusion(f32[1024,1536]{1,0:T(8,128)} %fusion.79, f32[1024,1536]{1,0:T(8,128)} %fusion.80, bf16[1024,2048]{1,0:T(8,128)(2,1)} %all-gather.9.cloned.1.call-done, bf16[1536,2048]{1,0:T(8,128)(2,1)} %param.30), kind=kOutput, calls=%fused_computation.60 | convolution fusion | flops 6466043904 | bytes 32505856 | tf_op jit(solution)/shard_map/dot_general | solution.py:27
  428.4 11.1 fusion.81
  439.5 11.4 add_convert_fusion.1
  450.9 75.4 %reduce-scatter.16.cloned.1.call-done = bf16[256,2048]{1,0:T(8,128)(2,1)} async-done(((bf16[1024,2048]{1,0:T(8,128)(2,1)}), bf16[256,2048]{1,0:T(8,128)(2,1)}) %reduce-scatter.16.cloned.1.call-update) | async-done | bytes 1048592 | tf_op jit(solution)/shard_map/reduce_scatter | solution.py:171
  526.3 3.2 fusion.58
  531.7 11.3 convolution_convert_fusion
  543.1 11.5 %convolution_convert_fusion.1 = bf16[2048,1536]{1,0:T(8,128)(2,1)} fusion(bf16[1024,2048]{1,0:T(8,128)(2,1)} %all-gather.7.cloned.1.call-done, bf16[1024,1536]{1,0:T(8,128)(2,1)} %copy-done.61), kind=kOutput, calls=%fused_computation.58 | convolution fusion | flops 6445596672 | bytes 13631488 | tf_op jit(solution)/shard_map/dot_general | solution.py:33
  554.7 11.6 %convolution_convert_fusion.2 = bf16[2048,1536]{1,0:T(8,128)(2,1)} fusion(bf16[1024,2048]{1,0:T(8,128)(2,1)} %all-gather.7.cloned.1.call-done, bf16[1024,1536]{1,0:T(8,128)(2,1)} %copy-done.60), kind=kOutput, calls=%fused_computation.59 | convolution fusion | flops 6445596672 | bytes 13631488 | tf_op jit(solution)/shard_map/dot_general | solution.py:33
  566.4 46.7 %all-gather.11.cloned.1.call-done = bf16[1024,2048]{1,0:T(8,128)(2,1)} async-done(((bf16[256,2048]{1,0:T(8,128)(2,1)}), bf16[1024,2048]{1,0:T(8,128)(2,1)}) %all-gather.11.cloned.1.call-update) | async-done | bytes 4194320 | tf_op jit(solution)/shard_map/all_gather | solution.py:183
  613.1 6.2 convolution_convert_fusion.9
  622.1 36.3 %while.30 = (s32[]{:T(128)}, f32[1024,2,128]{0,2,1:T(8,128)S(1)}, f32[1024,2,128]{0,2,1:T(8,128)}, f32[2,512,2,2,128]{4,1,3,2,0:T(8,128)}, bf16[2,512,2,2,128]{4...) while((s32[]{:T(128)}, f32[1024,2,128]{0,2,1:T(8,128)S(1)}, ...), condition=%wide.region_17.18_spmd.clone.clone, body=%wide.region_15.17_spmd.clone.sunk.clone | while | flops 2712140288 | bytes 108599728 | solution.py:217
  630.6 3.2 fusion.177
  648.7 3.2 fusion.177
  665.7 4.5 convolution_convert_fusion.7
  670.5 6.3 convolution_convert_fusion.5
  677.9 4.2 copy.67
  694.1 6.2 multiply_reduce_fusion
  705.4 3.6 fusion.65
  710.0 3.7 convolution_convert_fusion.6
  719.1 3.4 add_convert_fusion
  722.5 11.1 convolution_convert_fusion.3
  736.1 6.2 reduce-scatter.30.cloned.1.call-done
  744.8 62.7 %reduce-scatter.28.cloned.1.call-done = bf16[256,1536]{1,0:T(8,128)(2,1)} async-done(((bf16[2048,1536]{1,0:T(8,128)(2,1)}), bf16[256,1536]{1,0:T(8,128)(2,1)}) %reduce-scatter.28.cloned.1.call-update) | async-done | bytes 786448 | tf_op jit(solution)/shard_map/reduce_scatter | solution.py:270
  810.0 36.9 %reduce-scatter.22.cloned.1.call-done = bf16[256,256]{1,0:T(8,128)(2,1)} async-done(((bf16[2048,256]{1,0:T(8,128)(2,1)}), bf16[256,256]{1,0:T(8,128)(2,1)}) %reduce-scatter.22.cloned.1.call-update) | async-done | bytes 131088 | tf_op jit(solution)/shard_map/reduce_scatter | solution.py:261
  848.5 37.9 %reduce-scatter.24.cloned.1.call-done = bf16[256,256]{1,0:T(8,128)(2,1)} async-done(((bf16[2048,256]{1,0:T(8,128)(2,1)}), bf16[256,256]{1,0:T(8,128)(2,1)}) %reduce-scatter.24.cloned.1.call-update) | async-done | bytes 131088 | tf_op jit(solution)/shard_map/reduce_scatter | solution.py:264
  888.1 43.2 %reduce-scatter.26.cloned.1.call-done = bf16[512,256]{1,0:T(8,128)(2,1)} async-done(((bf16[512,2048]{1,0:T(8,128)(2,1)}), bf16[512,256]{1,0:T(8,128)(2,1)}) %reduce-scatter.26.cloned.1.call-update) | async-done | bytes 262160 | tf_op jit(solution)/shard_map/reduce_scatter | solution.py:267
  933.0 42.8 %reduce-scatter.20.cloned.1.call-done = bf16[256,512]{1,0:T(8,128)(2,1)} async-done(((bf16[2048,512]{1,0:T(8,128)(2,1)}), bf16[256,512]{1,0:T(8,128)(2,1)}) %reduce-scatter.20.cloned.1.call-update) | async-done | bytes 262160 | tf_op jit(solution)/shard_map/reduce_scatter | solution.py:258
  977.6 77.2 %reduce-scatter.18.cloned.1.call-done = bf16[256,2048]{1,0:T(8,128)(2,1)} async-done(((bf16[1024,2048]{1,0:T(8,128)(2,1)}), bf16[256,2048]{1,0:T(8,128)(2,1)}) %reduce-scatter.18.cloned.1.call-update) | async-done | bytes 1048592 | tf_op jit(solution)/shard_map/reduce_scatter | solution.py:244
  1056.9 46.5 %all-reduce = (f32[2048]{0:T(1024)}, f32[2048]{0:T(1024)}, f32[128]{0:T(128)}, f32[128]{0:T(128)}) all-reduce(f32[2048]{0:T(1024)S(1)} %get-tuple-element.217, f32[2048]{0:T(1024)S(1)} %copy-done.45, f32[128]{0:T(128)S(1)} %get-tuple-element.213, f32[128]{0:T(128)S(1)} %get-tuple-element.219), channel_id=1, replica_groups=mesh['dp'=8,'tensor'=4] {'dp','tensor'}, use_global_device_ids=true, to_apply=%region_23.24 | all-reduce | flops 4352 | bytes 34816 | tf_op jit(solution)/shard_map/psum | solution.py:254
  1103.4 31.9 %reduce-scatter.14.cloned.1.call-done = bf16[256,2048]{1,0:T(8,128)(2,1)} async-done(((bf16[1024,2048]{1,0:T(8,128)(2,1)}), bf16[256,2048]{1,0:T(8,128)(2,1)}) %reduce-scatter.14.cloned.1.call-update) | async-done | bytes 1048592 | tf_op jit(solution)/shard_map/reduce_scatter | solution.py:157
  1135.3 5.5 fusion.54
  (283 shorter events, 132.9 us)
Async XLA Ops:
  7.2 102.1 %copy-start = (bf16[2048,512]{1,0:T(8,128)(2,1)S(1)}, bf16[2048,512]{1,0:T(8,128)(2,1)}, u32[]{:S(2)}) copy-start(bf16[2048,512]{1,0:T(8,128)(2,1)} %param.24) | copy-start | bytes 6291460
  7.2 4.9 copy-start.59
  7.2 88.5 %all-gather.5.cloned.1.call-start = ((), (), s32[]{:S(2)}) async-start(), calls=%async_computation.11 | async-start | bytes 5242880 | tf_op jit(solution)/shard_map/all_gather | solution.py:113
  12.0 233.8 %reduce-scatter.12.cloned.1.call-start = ((), (), s32[]{:S(2)}) async-start(), calls=%async_computation.12 | async-start | bytes 5242880 | tf_op jit(solution)/shard_map/reduce_scatter | solution.py:148
  16.9 88.8 %copy-start.18 = (f32[1024,128]{0,1:T(8,128)}, f32[1024,128]{0,1:T(8,128)S(1)}, u32[]{:S(2)}) copy-start(f32[1024,128]{0,1:T(8,128)S(1)} %copy.57) | copy-start | bytes 1572868
  101.6 3.9 copy-start.54
  115.2 4.0 copy-start.52
  115.2 6.0 copy-start.36
  115.3 13.6 %copy-start.40 = (f32[2,512,2,2]{1,0,3,2:T(2,128)}, f32[2,512,2,2]{1,0,3,2:T(2,128)S(1)}, u32[]{:S(2)}) copy-start(f32[2,512,2,2]{1,0,3,2:T(2,128)S(1)} %rsqrt.38) | copy-start | bytes 49156
  158.2 12.1 %copy-start.1 = (bf16[1024,2,128]{2,0,1:T(8,128)(2,1)}, bf16[1024,2,128]{2,0,1:T(8,128)(2,1)S(1)}, u32[]{:S(2)}) copy-start(bf16[1024,2,128]{2,0,1:T(8,128)(2,1)S(1)} %get-tuple-element.555) | copy-start | bytes 1572868
  158.2 12.1 %copy-start.9 = (bf16[1024,2,128]{2,0,1:T(8,128)(2,1)}, bf16[1024,2,128]{2,0,1:T(8,128)(2,1)S(1)}, u32[]{:S(2)}) copy-start(bf16[1024,2,128]{2,0,1:T(8,128)(2,1)S(1)} %get-tuple-element.558) | copy-start | bytes 1572868
  170.3 75.6 %copy-start.4 = (bf16[256,2048]{1,0:T(8,128)(2,1)S(1)}, bf16[256,2048]{1,0:T(8,128)(2,1)}, u32[]{:S(2)}) copy-start(bf16[256,2048]{1,0:T(8,128)(2,1)} %param.18) | copy-start | bytes 3145732
  170.3 77.2 %copy-start.42 = (f32[2048]{0:T(1024)S(1)}, f32[2048]{0:T(1024)}, u32[]{:S(2)}) copy-start(f32[2048]{0:T(1024)} %param.21) | copy-start | bytes 24580
  170.4 161.2 %all-gather.7.cloned.1.call-start = ((), (), s32[]{:S(2)}) async-start(), calls=%async_computation.13 | async-start | bytes 5242880 | tf_op jit(solution)/shard_map/all_gather | solution.py:153
  247.5 282.0 %copy-start.46 = (f32[256]{0:T(256)}, f32[256]{0:T(256)S(1)}, u32[]{:S(2)}) copy-start(f32[256]{0:T(256)S(1)} %add_rsqrt_fusion.2) | copy-start | bytes 3076
  250.2 162.2 %all-gather.9.cloned.1.call-start = ((), (), s32[]{:S(2)}) async-start(), calls=%async_computation.15 | async-start | bytes 5242880 | tf_op jit(solution)/shard_map/all_gather | solution.py:161
  250.7 275.6 %reduce-scatter.16.cloned.1.call-start = ((), (), s32[]{:S(2)}) async-start(), calls=%async_computation.16 | async-start | bytes 5242880 | tf_op jit(solution)/shard_map/reduce_scatter | solution.py:171
  331.6 12.9 %copy-start.58 = (bf16[1024,2048]{1,0:T(8,128)(2,1)S(1)}, bf16[1024,2048]{1,0:T(8,128)(2,1)}, u32[]{:S(2)}) copy-start(bf16[1024,2048]{1,0:T(8,128)(2,1)} %all-gather.7.cloned.1.call-done) | copy-start | bytes 12582916
  428.4 11.1 copy-start.60
  428.4 11.1 copy-start.61
  450.9 162.2 %all-gather.11.cloned.1.call-start = ((), (), s32[]{:S(2)}) async-start(), calls=%async_computation.17 | async-start | bytes 5242880 | tf_op jit(solution)/shard_map/all_gather | solution.py:183
  526.3 3.2 copy-start.8
  526.3 3.2 copy-start.14
  526.3 3.2 copy-start.15
  531.7 202.0 %reduce-scatter.32.cloned.1.call-start = ((), (), s32[]{:S(2)}) async-start(), calls=%async_computation.25 | async-start | bytes 7077888 | tf_op jit(solution)/shard_map/reduce_scatter | solution.py:276
  543.1 199.2 %reduce-scatter.30.cloned.1.call-start = ((), (), s32[]{:S(2)}) async-start(), calls=%async_computation.24 | async-start | bytes 7077888 | tf_op jit(solution)/shard_map/reduce_scatter | solution.py:273
  554.6 252.9 %reduce-scatter.28.cloned.1.call-start = ((), (), s32[]{:S(2)}) async-start(), calls=%async_computation.23 | async-start | bytes 7077888 | tf_op jit(solution)/shard_map/reduce_scatter | solution.py:270
  566.3 280.6 %reduce-scatter.22.cloned.1.call-start = ((), (), s32[]{:S(2)}) async-start(), calls=%async_computation.20 | async-start | bytes 1179648 | tf_op jit(solution)/shard_map/reduce_scatter | solution.py:261
  630.6 3.2 copy-start.34
  648.7 3.2 copy-start.34
  664.8 221.7 %reduce-scatter.24.cloned.1.call-start = ((), (), s32[]{:S(2)}) async-start(), calls=%async_computation.21 | async-start | bytes 1179648 | tf_op jit(solution)/shard_map/reduce_scatter | solution.py:264
  670.3 6.6 copy-start.29
  670.3 261.0 %reduce-scatter.26.cloned.1.call-start = ((), (), s32[]{:S(2)}) async-start(), calls=%async_computation.22 | async-start | bytes 2359296 | tf_op jit(solution)/shard_map/reduce_scatter | solution.py:267
  676.8 299.0 %reduce-scatter.20.cloned.1.call-start = ((), (), s32[]{:S(2)}) async-start(), calls=%async_computation.19 | async-start | bytes 2359296 | tf_op jit(solution)/shard_map/reduce_scatter | solution.py:258
  688.9 5.2 copy-start.41
  694.1 6.2 copy-start.12
  694.1 6.2 copy-start.13
  705.4 4.5 copy-start.57
  709.9 4.0 copy-start.24
  713.7 341.2 %reduce-scatter.18.cloned.1.call-start = ((), (), s32[]{:S(2)}) async-start(), calls=%async_computation.18 | async-start | bytes 5242880 | tf_op jit(solution)/shard_map/reduce_scatter | solution.py:244
  722.5 412.9 %reduce-scatter.14.cloned.1.call-start = ((), (), s32[]{:S(2)}) async-start(), calls=%async_computation.14 | async-start | bytes 5242880 | tf_op jit(solution)/shard_map/reduce_scatter | solution.py:157
  736.1 318.7 %copy-start.5 = (bf16[256,2048]{1,0:T(8,128)(2,1)S(1)}, bf16[256,2048]{1,0:T(8,128)(2,1)}, u32[]{:S(2)}) copy-start(bf16[256,2048]{1,0:T(8,128)(2,1)} %param.18) | copy-start | bytes 3145732
  736.1 318.7 %copy-start.44 = (f32[2048]{0:T(1024)S(1)}, f32[2048]{0:T(1024)}, u32[]{:S(2)}) copy-start(f32[2048]{0:T(1024)} %param.20) | copy-start | bytes 24580
  736.1 318.7 %copy-start.49 = (f32[256]{0:T(256)S(1)}, f32[256]{0:T(256)}, u32[]{:S(2)}) copy-start(f32[256]{0:T(256)} %copy-done.48) | copy-start | bytes 3076
  744.8 312.1 %copy-start.45 = (f32[2048]{0:T(1024)S(1)}, f32[2048]{0:T(1024)}, u32[]{:S(2)}) copy-start(f32[2048]{0:T(1024)} %get-tuple-element.215) | copy-start | bytes 24580
  744.8 390.5 %copy-start.43 = (f32[2048]{0:T(1024)S(1)}, f32[2048]{0:T(1024)}, u32[]{:S(2)}) copy-start(f32[2048]{0:T(1024)} %param.21) | copy-start | bytes 24580
  744.8 390.5 %copy-start.47 = (f32[256]{0:T(256)S(1)}, f32[256]{0:T(256)}, u32[]{:S(2)}) copy-start(f32[256]{0:T(256)} %copy-done.46) | copy-start | bytes 3076
  744.8 390.5 %copy-start.51 = (f32[256]{0:T(256)S(1)}, f32[256]{0:T(256)}, u32[]{:S(2)}) copy-start(f32[256]{0:T(256)} %copy-done.50) | copy-start | bytes 3076
  (38 other events, 67.9 us)
Sparse Core Ops, SparseCore 0:
  12.2 83.4 all-gather.4
  170.5 75.3 reduce-scatter.11
  250.3 81.2 all-gather.6
  333.1 79.2 all-gather.8
  451.0 75.2 reduce-scatter.15
  531.8 81.2 all-gather.10
  616.5 60.3 reduce-scatter.31
  680.6 61.7 reduce-scatter.29
  745.7 61.7 reduce-scatter.27
  810.8 36.0 reduce-scatter.21
  850.4 36.0 reduce-scatter.23
  890.0 41.2 reduce-scatter.25
  934.5 41.2 reduce-scatter.19
  978.1 76.7 reduce-scatter.17
  1057.0 78.2 reduce-scatter.13
where the time goes:
time: 1150 us
  waiting for transfers between devices  747 us (65%)
  matrix products  190 us (17%)
  other arithmetic  84.5 us (7%)
  local copies, waits for them, and re-layouts  60.7 us (5%)
  blocking collectives  46.5 us (4%)
  between operations  14.8 us (1%)
    all_gather x1, waiting for transfers between devices, local(): mlp_all = lax.all_gather(mlp_entry, 'tensor', axis=0, tiled=True)  80.8 us
    reduce_scatter x1, waiting for transfers between devices, local(): lax.psum_scatter((query_part + key_part + value_part).astype(jnp.bfloat16...  77.2 us
    reduce_scatter x1, waiting for transfers between devices, local(): lax.psum_scatter(product(attn_mixed, w_out).astype(jnp.bfloat16), 'tensor...  75.5 us
    reduce_scatter x1, waiting for transfers between devices, local(): lax.psum_scatter((product_by_transpose(grad_gate, w_gate) + product_by_tr...  75.4 us
    all_gather x1, waiting for transfers between devices, local(): entry_all = lax.all_gather(attention_start, 'tensor', axis=0, tiled=True)  71.2 us
    reduce_scatter x1, waiting for transfers between devices, local(): lax.psum_scatter(w_gate_grad.astype(jnp.bfloat16), 'dp', scatter_dimensio...  62.7 us
    all_gather x1, waiting for transfers between devices, local(): grad_all = lax.all_gather(out_grad, 'tensor', axis=0, tiled=True)  57.5 us
    dot_general x7, matrix products, product(): jnp.dot(first_operand, second_operand, preferred_element_type=jnp.float32)  54.9 us
  transfers between devices with their start and end apart: 15, of which 14 were waited for; matrix products, arithmetic and copies ran while one was open for 17% of the time, Pallas kernels for 0%

commit v1 on v0

v1 whole, which is shorter than its diff:
```python
import functools

import jax
import jax.numpy as jnp
from jax import lax
from jax.experimental import pallas as pl
from jax.experimental.pallas import tpu as pltpu
from jax.sharding import PartitionSpec as P

NORM_EPSILON = 1e-06
ROPE_BASE = 1000000.0
MASK_FILL = -1e30
VMEM_BYTES = 52 * 1024 * 1024
F32 = jnp.float32
BF16 = jnp.bfloat16

NT = (((1,), (1,)), ((), ()))
TN = (((0,), (0,)), ((), ()))


def mm(a, b):
    return jnp.dot(a, b, preferred_element_type=F32)


def mm_nt(a, b):
    return lax.dot_general(a, b, NT, preferred_element_type=F32)


def mm_tn(a, b):
    return lax.dot_general(a, b, TN, preferred_element_type=F32)


def inv_root_of(values):
    return lax.rsqrt(jnp.mean(values * values, axis=-1, keepdims=True) + NORM_EPSILON)


def norm_back(grad_normed, normal, inv_root):
    return inv_root * (
        grad_normed - normal * jnp.mean(grad_normed * normal, axis=-1, keepdims=True)
    )


def call(kernel, grid_spec, out_shape, flops, nbytes, aliases=None):
    return pl.pallas_call(
        kernel,
        grid_spec=grid_spec,
        out_shape=out_shape,
        input_output_aliases=aliases or {},
        compiler_params=pltpu.CompilerParams(vmem_limit_bytes=VMEM_BYTES),
        cost_estimate=pl.CostEstimate(flops=flops, bytes_accessed=nbytes, transcendentals=0),
    )


def shape(dims, dtype):
    return jax.ShapeDtypeStruct(dims, dtype)


def positions_of(lengths, count_of_rows):
    seq_ends = jnp.cumsum(lengths, dtype=jnp.int32)
    starts = seq_ends - lengths
    place_index = jnp.arange(count_of_rows, dtype=jnp.int32)
    segment = jnp.sum(
        (place_index[:, None] >= seq_ends[None, :]).astype(jnp.int32), axis=1, dtype=jnp.int32
    )
    belongs = segment[:, None] == jnp.arange(lengths.shape[0], dtype=jnp.int32)[None, :]
    offset = jnp.sum(jnp.where(belongs, starts[None, :], 0), axis=1, dtype=jnp.int32)
    return (offset, place_index - offset)


def rope_tables(position, head_width):
    half_width = head_width // 2
    frequency = ROPE_BASE ** (-2.0 * jnp.arange(half_width, dtype=F32) / head_width)
    angles = position.astype(F32)[:, None] * frequency[None, :]
    cosine, sine = jnp.cos(angles), jnp.sin(angles)
    return (
        jnp.concatenate([cosine, cosine], axis=1),
        jnp.concatenate([-sine, sine], axis=1),
    )


def qkv_kernel(heads, kv_heads, dim, sid_ref, x_ref, gain_ref, w_ref, cos_ref, sin_ref, qg_ref, kg_ref, *refs):
    entry_ref, side_ref, raw_ref = refs[-3:]
    x = x_ref[...].astype(F32)
    entry = (x * inv_root_of(x) * gain_ref[...]).astype(BF16)
    entry_ref[...] = entry
    both = mm(entry, w_ref[...])
    cosine, sine = cos_ref[...], sin_ref[...]
    for h in range(heads + kv_heads):
        cols = slice(h * dim, (h + 1) * dim)
        raw = both[:, cols]
        raw_ref[:, cols] = raw.astype(BF16)
        gain = qg_ref[...] if h < heads else kg_ref[...]
        u = raw * inv_root_of(raw) * gain
        turned = u * cosine + pltpu.roll(u, dim // 2, 1) * sine
        if h < heads:
            turned = turned * dim ** (-0.5)
        side_ref[:, cols] = turned.astype(BF16)
    rest = slice((heads + kv_heads) * dim, (heads + 2 * kv_heads) * dim)
    side_ref[:, rest] = both[:, rest].astype(BF16)


def qkv_shard(sid, x, gain, w_qkv, cosine, sine, q_gain, k_gain, heads, kv_heads, dim, block_rows, kept):
    rows, width = x.shape
    cols = w_qkv.shape[1]
    raw_cols = (heads + kv_heads) * dim
    whole = lambda i, sid: (0, 0)
    mine = lambda i, sid: (sid[0], 0)
    in_specs = [
        pl.BlockSpec((rows, width), whole),
        pl.BlockSpec((1, width), whole),
        pl.BlockSpec((width, cols), whole),
        pl.BlockSpec((rows, dim), mine),
        pl.BlockSpec((rows, dim), mine),
        pl.BlockSpec((1, dim), whole),
        pl.BlockSpec((1, dim), whole),
    ]
    args = [sid, x, gain, w_qkv, cosine, sine, q_gain, k_gain]
    aliases = {}
    if kept is not None:
        for j, array in enumerate(kept):
            aliases[len(args)] = j
            args.append(array)
            in_specs.append(pl.BlockSpec(memory_space=pl.ANY))
    return call(
        functools.partial(qkv_kernel, heads, kv_heads, dim),
        pltpu.PrefetchScalarGridSpec(
            num_scalar_prefetch=1,
            grid=(1,),
            in_specs=in_specs,
            out_specs=[
                pl.BlockSpec((rows, width), mine),
                pl.BlockSpec((rows, cols), mine),
                pl.BlockSpec((rows, raw_cols), mine),
            ],
        ),
        [
            shape((block_rows, width), BF16),
            shape((block_rows, cols), BF16),
            shape((block_rows, raw_cols), BF16),
        ],
        2 * rows * width * cols,
        2 * (2 * rows * width + width * cols + 2 * rows * cols),
        aliases,
    )(*args)


def visible_keys(start_ref, first_row, rows, keys):
    row = first_row + lax.broadcasted_iota(jnp.int32, (rows, keys), 0)
    col = lax.broadcasted_iota(jnp.int32, (rows, keys), 1)
    return (col <= row) & (col >= start_ref[first_row : first_row + rows, :])


def attention_kernel(n, heads, kv_heads, dim, z_ref, side_ref, start_ref, mixed_ref, lse_ref):
    rows = side_ref.shape[0] // n
    group = heads // kv_heads
    for i in range(n):
        slot = lax.rem(i - z_ref[0] + n, n)
        keys = (i + 1) * rows
        here = slice(i * rows, (i + 1) * rows)
        visible = visible_keys(start_ref, i * rows, rows, keys)
        for h in range(heads):
            kv = h // group
            key = side_ref[:keys, (heads + kv) * dim : (heads + kv + 1) * dim]
            value = side_ref[
                :keys, (heads + kv_heads + kv) * dim : (heads + kv_heads + kv + 1) * dim
            ]
            cols = slice(h * dim, (h + 1) * dim)
            scores = jnp.where(visible, mm_nt(side_ref[here, cols], key), MASK_FILL)
            peak = jnp.max(scores, axis=-1, keepdims=True)
            spread = jnp.exp(scores - peak)
            total = jnp.sum(spread, axis=-1, keepdims=True)
            mixed = mm(spread.astype(BF16), value) / total
            mixed_ref[slot, :, cols] = mixed.astype(BF16)
            lse_ref[here, cols] = jnp.broadcast_to(peak + jnp.log(total), (rows, dim))


def attention_forward(z, side, start, n, heads, kv_heads, dim):
    block_rows = side.shape[0]
    rows = block_rows // n
    whole2 = lambda i, z: (0, 0)
    return call(
        functools.partial(attention_kernel, n, heads, kv_heads, dim),
        pltpu.PrefetchScalarGridSpec(
            num_scalar_prefetch=1,
            grid=(1,),
            in_specs=[
                pl.BlockSpec(side.shape, whole2),
                pl.BlockSpec((block_rows, 1), whole2),
            ],
            out_specs=[
                pl.BlockSpec((n, rows, heads * dim), lambda i, z: (0, 0, 0)),
                pl.BlockSpec((block_rows, heads * dim), whole2),
            ],
        ),
        [shape((n, rows, heads * dim), BF16), shape((block_rows, heads * dim), F32)],
        2 * block_rows * block_rows * heads * dim * 2,
        2 * side.size + 6 * block_rows * heads * dim,
    )(z, side, start)


def attention_back_kernel(
    n, heads, kv_heads, dim, z_ref, side_ref, raw_ref, gm_ref, lse_ref, start_ref, cos_ref, sin_ref,
    qg_ref, kg_ref, out_ref, gain_ref, key_acc, value_acc,
):
    block_rows = side_ref.shape[0]
    rows = block_rows // n
    group = heads // kv_heads
    q_sum = jnp.zeros((1, dim), F32)
    k_sum = jnp.zeros((1, dim), F32)
    for kv in range(kv_heads):
        key_cols = slice((heads + kv) * dim, (heads + kv + 1) * dim)
        value_cols = slice((heads + kv_heads + kv) * dim, (heads + kv_heads + kv + 1) * dim)
        key_acc[...] = jnp.zeros_like(key_acc)
        value_acc[...] = jnp.zeros_like(value_acc)
        for i in range(n):
            slot = lax.rem(z_ref[0] - i + n, n)
            keys = (i + 1) * rows
            here = slice(i * rows, (i + 1) * rows)
            key = side_ref[:keys, key_cols]
            value = side_ref[:keys, value_cols]
            visible = visible_keys(start_ref, i * rows, rows, keys)
            cosine, sine = cos_ref[here, :], sin_ref[here, :]
            for g in range(group):
                h = kv * group + g
                cols = slice(h * dim, (h + 1) * dim)
                query = side_ref[here, cols]
                grad = gm_ref[slot, :, cols]
                scores = jnp.where(visible, mm_nt(query, key), MASK_FILL)
                soft = jnp.exp(scores - lse_ref[here, cols][:, :1])
                grad_weights = mm_nt(grad, value)
                inner = jnp.sum(soft * grad_weights, axis=-1, keepdims=True)
                grad_scores = (soft * (grad_weights - inner)).astype(BF16)
                value_acc[:keys, :] += mm_tn(soft.astype(BF16), grad)
                key_acc[:keys, :] += mm_tn(grad_scores, query)
                turned = mm(grad_scores, key) * dim ** (-0.5)
                back = turned * cosine - pltpu.roll(turned, dim // 2, 1) * sine
                raw = raw_ref[here, cols].astype(F32)
                scale = inv_root_of(raw)
                normal = raw * scale
                q_sum = q_sum + jnp.sum(back * normal, axis=0, keepdims=True)
                out_ref[here, cols] = norm_back(back * qg_ref[...], normal, scale).astype(BF16)
        turned = key_acc[...]
        back = turned * cos_ref[...] - pltpu.roll(turned, dim // 2, 1) * sin_ref[...]
        raw = raw_ref[:, key_cols].astype(F32)
        scale = inv_root_of(raw)
        normal = raw * scale
        k_sum = k_sum + jnp.sum(back * normal, axis=0, keepdims=True)
        out_ref[:, key_cols] = norm_back(back * kg_ref[...], normal, scale).astype(BF16)
        out_ref[:, value_cols] = value_acc[...].astype(BF16)
    gain_ref[...] = jnp.concatenate([q_sum, k_sum, jnp.zeros((6, dim), F32)], axis=0)


def attention_backward(z, side, raw, gm, lse, start, cosine, sine, q_gain, k_gain, n, heads, kv_heads, dim):
    block_rows = side.shape[0]
    whole2 = lambda i, z: (0, 0)
    spec = lambda a: pl.BlockSpec(a.shape, (lambda i, z: (0, 0, 0)) if a.ndim == 3 else whole2)
    ins = (side, raw, gm, lse, start, cosine, sine, q_gain, k_gain)
    return call(
        functools.partial(attention_back_kernel, n, heads, kv_heads, dim),
        pltpu.PrefetchScalarGridSpec(
            num_scalar_prefetch=1,
            grid=(1,),
            in_specs=[spec(a) for a in ins],
            out_specs=[pl.BlockSpec(side.shape, whole2), pl.BlockSpec((8, dim), whole2)],
            scratch_shapes=[pltpu.VMEM((block_rows, dim), F32), pltpu.VMEM((block_rows, dim), F32)],
        ),
        [shape(side.shape, BF16), shape((8, dim), F32)],
        2 * block_rows * block_rows * heads * dim * 5,
        12 * side.size,
    )(z, *ins)


def out_kernel(n, z_ref, mixed_ref, w_ref, x_ref, gain_ref, hidden_ref, entry_ref, acc):
    k = pl.program_id(0)
    part = mm(mixed_ref[0], w_ref[...].reshape(mixed_ref.shape[2], -1))

    @pl.when(k == 0)
    def _():
        acc[...] = part + x_ref[...].astype(F32)

    @pl.when(k > 0)
    def _():
        acc[...] += part

    @pl.when(k == n - 1)
    def _():
        hidden = acc[...]
        hidden_ref[...] = hidden
        entry_ref[...] = (hidden * inv_root_of(hidden) * gain_ref[...]).astype(BF16)


def out_projection(z, mixed, w_full, x, gain, n):
    rows, width = x.shape
    cols = mixed.shape[2]
    whole = lambda k, z: (0, 0)
    return call(
        functools.partial(out_kernel, n),
        pltpu.PrefetchScalarGridSpec(
            num_scalar_prefetch=1,
            grid=(n,),
            in_specs=[
                pl.BlockSpec((1, rows, cols), lambda k, z: (k, 0, 0)),
                pl.BlockSpec(
                    (w_full.shape[0], 1, w_full.shape[2], width),
                    lambda k, z: (0, lax.rem(z[0] - k + n, n), 0, 0),
                ),
                pl.BlockSpec((rows, width), whole),
                pl.BlockSpec((1, width), whole),
            ],
            out_specs=[pl.BlockSpec((rows, width), whole), pl.BlockSpec((rows, width), whole)],
            scratch_shapes=[pltpu.VMEM((rows, width), F32)],
        ),
        [shape((rows, width), F32), shape((rows, width), BF16)],
        2 * rows * width * cols * n,
        2 * w_full.size + 10 * rows * width,
    )(z, mixed, w_full, x, gain)


def mlp_kernel(tiles, sid_ref, x_ref, go_ref, wg_ref, wu_ref, wd_ref, *refs):
    active_ref, gate_grad_ref, up_grad_ref, down_ref, inner_ref, down_acc, inner_acc = refs[-7:]
    j = pl.program_id(0)
    x = x_ref[...]
    gate = mm(x, wg_ref[...])
    up = mm(x, wu_ref[...])
    sigmoid = jax.nn.sigmoid(gate)
    silu = gate * sigmoid
    active = (silu * up).astype(BF16)
    active_ref[...] = active
    grad_active = mm_nt(go_ref[...], wd_ref[...])
    gate_grad = (grad_active * up * sigmoid * (1.0 + gate * (1.0 - sigmoid))).astype(BF16)
    up_grad = (grad_active * silu).astype(BF16)
    gate_grad_ref[...] = gate_grad
    up_grad_ref[...] = up_grad
    inner = mm_nt(gate_grad, wg_ref[...]) + mm_nt(up_grad, wu_ref[...])
    down = mm(active, wd_ref[...])

    @pl.when(j == 0)
    def _():
        inner_acc[...] = inner
        down_acc[...] = down

    @pl.when(j > 0)
    def _():
        inner_acc[...] += inner
        down_acc[...] += down

    @pl.when(j == tiles - 1)
    def _():
        inner_ref[...] = inner_acc[...].astype(BF16)
        down_ref[...] = down_acc[...].astype(BF16)


def mlp_shard(sid, x, grad_all, w_gate, w_up, w_down, kept):
    rows, width = x.shape
    block_rows = grad_all.shape[0]
    units = w_gate.shape[1]
    tile = next(t for t in (512, 384, 256, 128) if units % t == 0)
    tiles = units // tile
    whole = lambda j, sid: (0, 0)
    mine = lambda j, sid: (sid[0], 0)
    tiled = lambda j, sid: (sid[0], j)
    in_specs = [
        pl.BlockSpec((rows, width), whole),
        pl.BlockSpec((rows, width), mine),
        pl.BlockSpec((width, tile), lambda j, sid: (0, j)),
        pl.BlockSpec((width, tile), lambda j, sid: (0, j)),
        pl.BlockSpec((tile, width), lambda j, sid: (j, 0)),
    ]
    args = [sid, x, grad_all, w_gate, w_up, w_down]
    aliases = {}
    if kept is not None:
        for j, array in enumerate(kept):
            aliases[len(args)] = j
            args.append(array)
            in_specs.append(pl.BlockSpec(memory_space=pl.ANY))
    return call(
        functools.partial(mlp_kernel, tiles),
        pltpu.PrefetchScalarGridSpec(
            num_scalar_prefetch=1,
            grid=(tiles,),
            in_specs=in_specs,
            out_specs=[
                pl.BlockSpec((rows, tile), tiled),
                pl.BlockSpec((rows, tile), tiled),
                pl.BlockSpec((rows, tile), tiled),
                pl.BlockSpec((rows, width), mine),
                pl.BlockSpec((rows, width), whole),
            ],
            scratch_shapes=[pltpu.VMEM((rows, width), F32), pltpu.VMEM((rows, width), F32)],
        ),
        [
            shape((block_rows, units), BF16),
            shape((block_rows, units), BF16),
            shape((block_rows, units), BF16),
            shape((block_rows, width), BF16),
            shape((rows, width), BF16),
        ],
        2 * rows * width * units * 6,
        2 * (3 * width * units + 3 * rows * units + 4 * rows * width),
        aliases,
    )(*args)


def mid_kernel(n, z_ref, got_ref, own_ref, go_ref, hidden_ref, gain_ref, w_ref, gm_ref, gh_ref, mid_ref, part_ref):
    k = pl.program_id(0)

    @pl.when(k == 0)
    def _():
        hidden = hidden_ref[...]
        scale = inv_root_of(hidden)
        normal = hidden * scale
        inner = got_ref[...].astype(F32) + own_ref[...].astype(F32)
        part_ref[...] = jnp.sum(inner * normal, axis=0, keepdims=True)
        grad_hidden = go_ref[...].astype(F32) + norm_back(inner * gain_ref[...], normal, scale)
        gh_ref[...] = grad_hidden
        mid_ref[...] = grad_hidden.astype(BF16)

    gm_ref[0] = mm_nt(mid_ref[...], w_ref[...].reshape(gm_ref.shape[2], -1)).astype(BF16)


def mid_stage(z, got, own, go, hidden, gain, w_full, n):
    rows, width = go.shape
    cols = w_full.shape[0] * w_full.shape[2]
    whole = lambda k, z: (0, 0)
    return call(
        functools.partial(mid_kernel, n),
        pltpu.PrefetchScalarGridSpec(
            num_scalar_prefetch=1,
            grid=(n,),
            in_specs=[
                pl.BlockSpec((rows, width), whole),
                pl.BlockSpec((rows, width), whole),
                pl.BlockSpec((rows, width), whole),
                pl.BlockSpec((rows, width), whole),
                pl.BlockSpec((1, width), whole),
                pl.BlockSpec(
                    (w_full.shape[0], 1, w_full.shape[2], width),
                    lambda k, z: (0, lax.rem(z[0] + k, n), 0, 0),
                ),
            ],
            out_specs=[
                pl.BlockSpec((1, rows, cols), lambda k, z: (k, 0, 0)),
                pl.BlockSpec((rows, width), whole),
                pl.BlockSpec((rows, width), whole),
                pl.BlockSpec((1, width), whole),
            ],
        ),
        [
            shape((n, rows, cols), BF16),
            shape((rows, width), F32),
            shape((rows, width), BF16),
            shape((1, width), F32),
        ],
        2 * rows * width * cols * n,
        2 * w_full.size + 20 * rows * width,
    )(z, got, own, go, hidden, gain, w_full)


def out_weight_kernel(z_ref, mixed_ref, mid_ref, out_ref):
    grad = mm_tn(mixed_ref[0], mid_ref[...]).astype(BF16)
    cols = out_ref.shape[3]
    for b in range(out_ref.shape[0]):
        out_ref[b, 0] = grad[:, b * cols : (b + 1) * cols]


def out_weight_grad(z, mixed, mid, n, batches):
    rows, width = mid.shape
    cols = mixed.shape[2]
    return call(
        out_weight_kernel,
        pltpu.PrefetchScalarGridSpec(
            num_scalar_prefetch=1,
            grid=(n,),
            in_specs=[
                pl.BlockSpec((1, rows, cols), lambda k, z: (k, 0, 0)),
                pl.BlockSpec((rows, width), lambda k, z: (0, 0)),
            ],
            out_specs=pl.BlockSpec(
                (batches, 1, cols, width // batches),
                lambda k, z: (0, lax.rem(z[0] - k + n, n), 0, 0),
            ),
        ),
        shape((batches, n, cols, width // batches), BF16),
        2 * rows * width * cols * n,
        2 * n * cols * width,
    )(z, mixed, mid)


def qkv_weight_kernel(entry_ref, grad_ref, w_ref, out_ref, part_ref):
    grad = mm_tn(entry_ref[...], grad_ref[...])
    out_ref[...] = grad.astype(BF16)
    both = grad * w_ref[...].astype(F32)
    lanes = part_ref.shape[1]
    total = both[:, :lanes]
    for first in range(lanes, both.shape[1], lanes):
        total = total + both[:, first : first + lanes]

    @pl.when(pl.program_id(0) == 0)
    def _():
        part_ref[...] = total

    @pl.when(pl.program_id(0) > 0)
    def _():
        part_ref[...] += total


def qkv_weight_grad(entry, grads, w_qkv):
    block_rows, width = entry.shape
    cols = grads.shape[1]
    tile = 256
    return call(
        qkv_weight_kernel,
        pltpu.PrefetchScalarGridSpec(
            num_scalar_prefetch=0,
            grid=(cols // tile,),
            in_specs=[
                pl.BlockSpec((block_rows, width), lambda j: (0, 0)),
                pl.BlockSpec((block_rows, tile), lambda j: (0, j)),
                pl.BlockSpec((width, tile), lambda j: (0, j)),
            ],
            out_specs=[
                pl.BlockSpec((width, tile), lambda j: (0, j)),
                pl.BlockSpec((width, 128), lambda j: (0, 0)),
            ],
        ),
        [shape((width, cols), BF16), shape((width, 128), F32)],
        2 * block_rows * width * cols,
        2 * (block_rows * width + block_rows * cols + 2 * width * cols),
    )(entry, grads, w_qkv)


def exchange(value, axis, step):
    size = lax.axis_size(axis)
    return lax.ppermute(value, axis, [(i, i ^ step) for i in range(size)])


def total_over(value, axis):
    step = 1
    while step < lax.axis_size(axis):
        value = value + exchange(value, axis, step)
        step *= 2
    return value


def halve(value, axes, bits, bit):
    own = lax.rem(lax.div(lax.axis_index("dp"), 1 << bit), 2)
    at = axes.index(bit)
    sent = lax.dynamic_index_in_dim(value, 1 - own, at, False).astype(BF16)
    kept = lax.dynamic_index_in_dim(value, own, at, False)
    total = kept.astype(F32) + exchange(sent, "dp", 1 << bit).astype(F32)
    return total, axes[:at] + axes[at + 1 :]


def halved_over_dp(value):
    batches = value.shape[0]
    bits = batches.bit_length() - 1
    axes = list(range(bits))[::-1]
    value = value.reshape((2,) * bits + value.shape[1:])
    value, axes = halve(value, axes, bits, 0)
    middle = value.shape[-1] // 2
    results = []
    for part, order in ((value[..., :middle], axes[::-1]), (value[..., middle:], axes)):
        left = axes
        for bit in order:
            part, left = halve(part, left, bits, bit)
        results.append(part)
    return jnp.concatenate(results, axis=-1)


def line_sum(value, z, n):
    rows = value.shape[0] // n
    shard = lambda d: lax.dynamic_slice_in_dim(value, jnp.clip(z + d, 0, n - 1) * rows, rows, 0)
    right = left = None
    for s in range(1, n):
        far = n - s
        to_right, to_left = shard(far), shard(-far)
        if right is not None:
            to_right = (to_right.astype(F32) + right.astype(F32)).astype(BF16)
            to_left = (to_left.astype(F32) + left.astype(F32)).astype(BF16)
        right = lax.ppermute(to_right, "tensor", [(i, i + 1) for i in range(s)])
        left = lax.ppermute(to_left, "tensor", [(i, i - 1) for i in range(n - s, n)])
    return shard(0).astype(F32) + right.astype(F32) + left.astype(F32)


def local(
    tokens,
    seq_lengths,
    attn_gain,
    mlp_gain,
    q_gain,
    k_gain,
    w_query,
    key_weight,
    value_weight,
    w_out,
    w_gate,
    w_up,
    w_down,
    out_grad,
):
    n = lax.axis_size("tensor")
    batches = lax.axis_size("dp")
    rows, width = tokens.shape
    block_rows = rows * n
    dim = q_gain.shape[0]
    heads = w_query.shape[1] // dim
    kv_heads = key_weight.shape[1] // dim
    z = lax.axis_index("tensor").astype(jnp.int32)
    zs = z.reshape(1)
    ring = [(i, (i + 1) % n) for i in range(n)]
    shift = lambda v, d=1: lax.ppermute(v, "tensor", [(i, (i + d) % n) for i in range(n)])
    shard_of = lambda s: lax.rem(z - s + n, n).reshape(1)

    own_rows = w_out.shape[0] // batches
    piece = lax.dynamic_slice_in_dim(w_out, lax.axis_index("dp") * own_rows, own_rows, 0)
    piece = lax.all_gather(piece, "tensor", axis=0, tiled=False)
    w_out_full = lax.all_gather(piece, "dp", axis=0, tiled=False)

    offset, position = positions_of(seq_lengths[0], block_rows)
    start = offset[:, None]
    cosine, sine = rope_tables(position, dim)
    w_qkv = jnp.concatenate([w_query, key_weight, value_weight], axis=1)
    gain_one, gain_two = attn_gain[None, :], mlp_gain[None, :]
    qg, kg = q_gain[None, :], k_gain[None, :]

    kept = None
    block = tokens
    for s in range(n):
        later = shift(block) if s < n - 1 else None
        kept = qkv_shard(
            shard_of(s), block, gain_one, w_qkv, cosine, sine, qg, kg, heads, kv_heads, dim, block_rows, kept
        )
        last, block = block, later
    entry_all, side, raw = kept

    later_grad, _ = lax.optimization_barrier((out_grad, last))
    grad_all = lax.all_gather(later_grad, "tensor", axis=0, tiled=True)

    mixed, lse = attention_forward(zs, side, start, n, heads, kv_heads, dim)
    mixed = jnp.stack([mixed[0]] + [shift(mixed[d], d) for d in range(1, n)])
    hidden, mlp_entry = out_projection(zs, mixed, w_out_full, tokens, gain_two, n)

    kept = None
    block = mlp_entry
    blocks, partials = [], []
    for s in range(n):
        later = shift(block) if s < n - 1 else None
        *kept, partial = mlp_shard(shard_of(s), block, grad_all, w_gate, w_up, w_down, kept)
        blocks.append(block)
        partials.append(partial)
        block = later
    active, gate_grad, up_grad, down = kept

    moving = partials[1]
    for s in range(2, n + 1):
        moving = shift(moving)
        if s < n:
            moving = (moving.astype(F32) + partials[s].astype(F32)).astype(BF16)

    mlp_all = jnp.zeros((block_rows, width), BF16)
    for s in range(n):
        mlp_all = lax.dynamic_update_slice_in_dim(mlp_all, blocks[s], shard_of(s)[0] * rows, 0)
    w_down_grad = mm_tn(active, grad_all).astype(BF16)
    w_gate_grad = mm_tn(mlp_all, gate_grad).astype(BF16)
    w_up_grad = mm_tn(mlp_all, up_grad).astype(BF16)
    moving, w_down_grad, w_gate_grad, w_up_grad = lax.optimization_barrier(
        (moving, w_down_grad, w_gate_grad, w_up_grad)
    )

    gm, grad_hidden, grad_mid, mlp_part = mid_stage(
        zs, moving, partials[0], out_grad, hidden, gain_two, w_out_full, n
    )
    gm, down = lax.optimization_barrier((gm, down))
    ffn = line_sum(down, z, n)
    output = (hidden + ffn).astype(BF16)
    gm = jnp.stack([gm[0]] + [shift(gm[d], d) for d in range(1, n)])
    grads, gain_parts = attention_backward(
        zs, side, raw, gm, lse, start, cosine, sine, qg, kg, n, heads, kv_heads, dim
    )
    w_out_grad = out_weight_grad(zs, mixed, grad_mid, n, batches)

    def entry_part(s):
        mine = lax.dynamic_slice_in_dim(grads, shard_of(s)[0] * rows, rows, 0)
        return mm_nt(mine, w_qkv)

    moving = entry_part(1).astype(BF16)
    for s in range(2, n + 1):
        moving = shift(moving)
        if s < n:
            moving = (moving.astype(F32) + entry_part(s)).astype(BF16)
    grad_entry = moving.astype(F32) + entry_part(0)
    w_qkv_grad, attn_lanes = qkv_weight_grad(entry_all, grads, w_qkv)

    x = tokens.astype(F32)
    scale = inv_root_of(x)
    token_grad = (grad_hidden + norm_back(grad_entry * attn_gain, x * scale, scale)).astype(BF16)

    attn_part = jnp.sum(attn_lanes, axis=1) / attn_gain
    totals = jnp.concatenate([attn_part, mlp_part[0], gain_parts[0], gain_parts[1]])[None, :]
    totals = total_over(total_over(totals, "dp"), "tensor")[0]
    attn_gain_grad = totals[:width]
    mlp_gain_grad = totals[width : 2 * width]
    q_gain_grad = totals[2 * width : 2 * width + dim]
    k_gain_grad = totals[2 * width + dim :]

    over_dp = lambda g, d: lax.psum_scatter(g, "dp", scatter_dimension=d, tiled=True)
    w_down_grad = over_dp(w_down_grad, 1).astype(F32)
    w_gate_grad = over_dp(w_gate_grad, 0).astype(F32)
    w_up_grad = over_dp(w_up_grad, 0).astype(F32)
    w_out_grad = halved_over_dp(w_out_grad).astype(BF16)
    pieces = [lax.dynamic_index_in_dim(w_out_grad, lax.rem(z + d, n), 0, False) for d in range(n)]
    w_out_grad = pieces[0].astype(F32)
    for d in range(1, n):
        w_out_grad = w_out_grad + shift(pieces[d], d).astype(F32)
    w_qkv_grad = halved_over_dp(
        w_qkv_grad.reshape(batches, width // batches, w_qkv_grad.shape[1])
    )
    a, b = heads * dim, (heads + kv_heads) * dim
    return (
        output,
        token_grad,
        attn_gain_grad,
        mlp_gain_grad,
        q_gain_grad,
        k_gain_grad,
        w_qkv_grad[:, :a],
        w_qkv_grad[:, a:b],
        w_qkv_grad[:, b:],
        w_out_grad,
        w_gate_grad,
        w_up_grad,
        w_down_grad,
    )


def solution(mesh):
    return jax.shard_map(
        local,
        mesh=mesh,
        in_specs=(
            P(("dp", "tensor"), None),
            P("dp", None),
            P(),
            P(),
            P(),
            P(),
            P(None, "tensor"),
            P(None, "tensor"),
            P(None, "tensor"),
            P("tensor", None),
            P(None, "tensor"),
            P(None, "tensor"),
            P("tensor", None),
            P(("dp", "tensor"), None),
        ),
        out_specs=(
            P(("dp", "tensor"), None),
            P(("dp", "tensor"), None),
            P(),
            P(),
            P(),
            P(),
            P("dp", "tensor"),
            P("dp", "tensor"),
            P("dp", "tensor"),
            P("tensor", "dp"),
            P("dp", "tensor"),
            P("dp", "tensor"),
            P("tensor", "dp"),
        ),
        check_vma=False,
    )
```

time: 1150 us -> 702 us (0.61)
  waiting for transfers between devices: 747 us -> 345 us
  Pallas kernels: 0 us -> 156 us
  matrix products: 190 us -> 44.1 us
  starting transfers between devices: 1.01 us -> 57.2 us
  other arithmetic: 84.5 us -> 37.5 us
  blocking collectives: 46.5 us -> 0 us
  local copies, waits for them, and re-layouts: 60.7 us -> 37 us
    reduce_scatter x11 -> x3, waiting for transfers between devices: 490 us -> 0.01 us  [local(): lax.psum_scatter(g, 'dp', scatter_dimension=d, tiled=True)]
    ppermute x0 -> x42, waiting for transfers between devices: none -> 293 us  [the longest x21 200 us: local(): lax.ppermute(v, 'tensor', [(i, (i + d) % n) for i in range(n)])]
    all_gather x4 -> x3, waiting for transfers between devices: 256 us -> 51 us  [the longest x1 31.3 us: local(): piece = lax.all_gather(piece, 'tensor', axis=0, tiled=False)]
    pallas_call x0 -> x14, Pallas kernels: none -> 156 us  [the longest x4 70.4 us: mlp_shard(): call(functools.partial(mlp_kernel, tiles), pltpu.PrefetchScalarGridSpec(n...]
    dot_general x35 -> x7, matrix products: 190 us -> 44.1 us  [the longest x3 33.9 us: mm_tn(): return lax.dot_general(a, b, TN, preferred_element_type=F32)]
    ppermute x0 -> x42, starting transfers between devices: none -> 57 us  [the longest x15 20.5 us: exchange(): return lax.ppermute(value, axis, [(i, i ^ step) for i in range(size)])]
    psum x1 -> x0, blocking collectives: 46.5 us -> none  [local(): lax.psum((attn_gain_part, mlp_gain_part, q_gain_part, k_gain_part), ('dp'...]
    convert_element_type x20 -> x11, other arithmetic: 41.1 us -> 18.1 us  [the longest x2 5.28 us: line_sum(): to_right = (to_right.astype(F32) + right.astype(F32)).astype(BF16)]
  transfers between devices with their start and end apart: 15 -> 48, of which waited for: 14 -> 27; matrix products, arithmetic and copies ran while one was open for 17% -> 15% of each run, Pallas kernels for 0% -> 23%
where the time goes in v1:
time: 702 us; the launch traced here: 692 us
  waiting for transfers between devices  345 us (49%)
  Pallas kernels  156 us (22%)
  starting transfers between devices  57.2 us (8%)
  matrix products  44.1 us (6%)
  other arithmetic  37.5 us (5%)
  local copies, waits for them, and re-layouts  37 us (5%)
  between operations  15.2 us (2%)
    ppermute x21, waiting for transfers between devices, local(): lax.ppermute(v, 'tensor', [(i, (i + d) % n) for i in range(n)])  200 us
    ppermute x15, waiting for transfers between devices, exchange(): return lax.ppermute(value, axis, [(i, i ^ step) for i in range(size)])  72.2 us
    pallas_call x4, Pallas kernels, mlp_shard(): call(functools.partial(mlp_kernel, tiles), pltpu.PrefetchScalarGridSpec(n...  70.4 us
    dot_general x3, matrix products, mm_tn(): return lax.dot_general(a, b, TN, preferred_element_type=F32)  33.9 us
    all_gather x1, waiting for transfers between devices, local(): piece = lax.all_gather(piece, 'tensor', axis=0, tiled=False)  31.3 us
    ppermute x3, waiting for transfers between devices, line_sum(): right = lax.ppermute(to_right, 'tensor', [(i, i + 1) for i in range(s)])  20.8 us
    pallas_call x4, Pallas kernels, qkv_shard(): call(functools.partial(qkv_kernel, heads, kv_heads, dim), pltpu.PrefetchS...  20.6 us
    ppermute x15, starting transfers between devices, exchange(): return lax.ppermute(value, axis, [(i, i ^ step) for i in range(size)])  20.5 us
  transfers between devices with their start and end apart: 48, of which 27 were waited for; matrix products, arithmetic and copies ran while one was open for 15% of the time, Pallas kernels for 23%

profile of v1, /device:TPU:0, one launch (start us, length us, event | category | flops | bytes accessed | tf_op | source)
XLA Modules:
  0.0 691.7 jit_solution(8154133296280252456)
XLA Ops:
  9.6 31.3 %all-gather.8.cloned.1.call-done = bf16[256,2048]{1,0:T(8,128)(2,1)} async-done(((bf16[64,2048]{1,0:T(8,128)(2,1)}), bf16[256,2048]{1,0:T(8,128)(2,1)}) %all-gather.8.cloned.1.call-update) | async-done | bytes 1048592 | tf_op jit(solution)/shard_map/all_gather | solution.py:616
  42.4 25.3 %collective-permute-done.x_ref = bf16[256,2048]{1,0:T(8,128)(2,1)S(1)} collective-permute-done((bf16[256,2048]{1,0:T(8,128)(2,1)}, bf16[256,2048]{1,0:T(8,128)(2,1)S(1)}, u32[]{:S(2)}, u32[]{:S(2)}) %collective-permute-start) | collective-permute-done | bytes 1048608 | tf_op jit(solution)/shard_map/ppermute | solution.py:611
  67.7 25.7 %collective-permute-done.1.x_ref = bf16[256,2048]{1,0:T(8,128)(2,1)S(1)} collective-permute-done((bf16[256,2048]{1,0:T(8,128)(2,1)S(1)}, bf16[256,2048]{1,0:T(8,128)(2,1)S(1)}, u32[]{:S(2)}, u32[]{:S(2)}) %collective-permute-start.1) | collective-permute-done | bytes 1048608 | tf_op jit(solution)/shard_map/ppermute | solution.py:611
  93.4 24.7 %collective-permute-done.2.x_ref = bf16[256,2048]{1,0:T(8,128)(2,1)S(1)} collective-permute-done((bf16[256,2048]{1,0:T(8,128)(2,1)S(1)}, bf16[256,2048]{1,0:T(8,128)(2,1)S(1)}, u32[]{:S(2)}, u32[]{:S(2)}) %collective-permute-start.2) | collective-permute-done | bytes 1048608 | tf_op jit(solution)/shard_map/ppermute | solution.py:611
  127.0 5.1 shard_map.237
  132.2 5.2 shard_map.238
  137.3 5.2 shard_map.239
  142.5 5.2 shard_map.240
  147.7 9.5 %shard_map.241 = (bf16[4,256,512]{2,1,0:T(8,128)(2,1)S(1)}, f32[1024,512]{1,0:T(8,128)}) custom-call(s32[1]{0:T(128)} %bitcast.z_ref, bf16[1024,1024]{1,0:T(8,128)(2,1)} %get-tuple-element.73.side_ref, s32[1024,1]{1,0:T(8,128)S(1)} %copy.58.start_ref), custom_call_target="tpu_custom_call" | custom-call | flops 2147483648 | bytes 5242880 | tf_op jit(solution)/shard_map/pallas_call | solution.py:181
  159.3 15.3 %collective-permute-done.5 = bf16[256,512]{1,0:T(8,128)(2,1)S(1)} collective-permute-done((bf16[256,512]{1,0:T(8,128)(2,1)S(1)}, bf16[256,512]{1,0:T(8,128)(2,1)S(1)}, u32[]{:S(2)}, u32[]{:S(2)}) %collective-permute-start.5) | collective-permute-done | bytes 262176 | tf_op jit(solution)/shard_map/ppermute | solution.py:611
  174.6 33.7 %collective-permute-done.4 = bf16[256,512]{1,0:T(8,128)(2,1)S(1)} collective-permute-done((bf16[256,512]{1,0:T(8,128)(2,1)S(1)}, bf16[256,512]{1,0:T(8,128)(2,1)S(1)}, u32[]{:S(2)}, u32[]{:S(2)}) %collective-permute-start.4) | collective-permute-done | bytes 262176 | tf_op jit(solution)/shard_map/ppermute | solution.py:611
  210.4 8.3 %shard_map.242 = (f32[256,2048]{1,0:T(8,128)}, bf16[256,2048]{1,0:T(8,128)(2,1)S(1)}) custom-call(s32[1]{0:T(128)} %bitcast.z_ref, bf16[4,256,512]{2,1,0:T(8,128)(2,1)} %pad_maximum_fusion.mixed_ref, bf16[8,4,64,2048]{3,2,1,0:T(8,128)(2,1)} %bitcast.139, bf16[256,2048]{1,0:T(8,128)(2,1)} %x_ref.3, f32[1,2048]{1,0:T(1,128)S(1)} %bitcast.126), custom_call_target="tpu_custom_call" | custom-call | flops 2147483648 | bytes 13631488 | tf_op jit(solution)/shard_map/pallas_call | solution.py:296
  222.2 19.7 %all-gather.6.cloned.1.call-done.go_ref = bf16[1024,2048]{1,0:T(8,128)(2,1)} async-done(((bf16[256,2048]{1,0:T(8,128)(2,1)}), bf16[1024,2048]{1,0:T(8,128)(2,1)}) %all-gather.6.cloned.1.call-update) | async-done | bytes 4194320 | tf_op jit(solution)/shard_map/all_gather | solution.py:637
  241.9 17.6 %shard_map.243 = (bf16[1024,1536]{1,0:T(8,128)(2,1)}, bf16[1024,1536]{1,0:T(8,128)(2,1)}, bf16[1024,1536]{1,0:T(8,128)(2,1)}, bf16[1024,2048]{1,0:T(8,128)(2,1)}, bf16[256,2048]{1,0:T(8,128)(2,1)S(1)}) custom-call(s32[1]{0:T(128)} %bitcast.11.sid_ref, bf16[256,2048]{1,0:T(8,128)(2,1)} %copy-done.4, bf16[1024,2048]{1,0:T(8,128)(2,1)} %all-gather.6.cloned.1.call-done.go_ref, ...), custom_call_target="tpu_custom_call" | custom-call | flops 9663676416 | bytes 25427968 | tf_op jit(solution)/shard_map/pallas_call | solution.py:376
  260.9 17.6 %shard_map.244 = (bf16[1024,1536]{1,0:T(8,128)(2,1)}, bf16[1024,1536]{1,0:T(8,128)(2,1)}, bf16[1024,1536]{1,0:T(8,128)(2,1)}, bf16[1024,2048]{1,0:T(8,128)(2,1)}, bf16[256,2048]{1,0:T(8,128)(2,1)S(1)}) custom-call(s32[1]{0:T(128)} %bitcast.10.sid_ref, ...), custom_call_target="tpu_custom_call", output_to_operand_aliasing={{0}: (6, {}), {1}: (7, {}), {2}: (8, {}), {3}: (9, {})} | custom-call | flops 9663676416 | bytes 25427968 | tf_op jit(solution)/shard_map/pallas_call | solution.py:376
  280.8 8.1 %collective-permute-done.8.x_ref = bf16[256,2048]{1,0:T(8,128)(2,1)S(1)} collective-permute-done((bf16[256,2048]{1,0:T(8,128)(2,1)}, bf16[256,2048]{1,0:T(8,128)(2,1)S(1)}, u32[]{:S(2)}, u32[]{:S(2)}) %collective-permute-start.8) | collective-permute-done | bytes 1048608 | tf_op jit(solution)/shard_map/ppermute | solution.py:611
  289.9 17.5 %shard_map.245 = (bf16[1024,1536]{1,0:T(8,128)(2,1)}, bf16[1024,1536]{1,0:T(8,128)(2,1)}, bf16[1024,1536]{1,0:T(8,128)(2,1)}, bf16[1024,2048]{1,0:T(8,128)(2,1)}, bf16[256,2048]{1,0:T(8,128)(2,1)S(1)}) custom-call(s32[1]{0:T(128)} %bitcast.9.sid_ref, ...), custom_call_target="tpu_custom_call", output_to_operand_aliasing={{0}: (6, {}), {1}: (7, {}), {2}: (8, {}), {3}: (9, {})} | custom-call | flops 9663676416 | bytes 25427968 | tf_op jit(solution)/shard_map/pallas_call | solution.py:376
  307.5 4.0 collective-permute-done.7
  312.9 21.0 %collective-permute-done.10.x_ref = bf16[256,2048]{1,0:T(8,128)(2,1)S(1)} collective-permute-done((bf16[256,2048]{1,0:T(8,128)(2,1)S(1)}, bf16[256,2048]{1,0:T(8,128)(2,1)S(1)}, u32[]{:S(2)}, u32[]{:S(2)}) %collective-permute-start.10) | collective-permute-done | bytes 1048608 | tf_op jit(solution)/shard_map/ppermute | solution.py:611
  334.9 17.6 %shard_map.246 = (bf16[1024,1536]{1,0:T(8,128)(2,1)}, bf16[1024,1536]{1,0:T(8,128)(2,1)}, bf16[1024,1536]{1,0:T(8,128)(2,1)}, bf16[1024,2048]{1,0:T(8,128)(2,1)}, bf16[256,2048]{1,0:T(8,128)(2,1)S(1)}) custom-call(s32[1]{0:T(128)} %bitcast.1.sid_ref, ...), custom_call_target="tpu_custom_call", output_to_operand_aliasing={{0}: (6, {}), {1}: (7, {}), {2}: (8, {}), {3}: (9, {})} | custom-call | flops 9663676416 | bytes 25427968 | tf_op jit(solution)/shard_map/pallas_call | solution.py:376
  359.1 11.2 %convolution_convert_fusion.1 = bf16[2048,1536]{1,0:T(8,128)(2,1)} fusion(bf16[1024,2048]{1,0:T(8,128)(2,1)} %constant_dynamic-update-slice_fusion, bf16[1024,1536]{1,0:T(8,128)(2,1)S(1)} %copy-done.12), kind=kOutput, calls=%fused_computation.2 | convolution fusion | flops 6445596672 | bytes 13631488 | tf_op jit(solution)/shard_map/dot_general | solution.py:30
  370.3 11.3 %convolution_convert_fusion.2 = bf16[1536,2048]{1,0:T(8,128)(2,1)} fusion(bf16[1024,1536]{1,0:T(8,128)(2,1)} %get-tuple-element.93, bf16[1024,2048]{1,0:T(8,128)(2,1)} %all-gather.6.cloned.1.call-done.go_ref), kind=kOutput, calls=%fused_computation.3 | convolution fusion | flops 6445596672 | bytes 13631488 | tf_op jit(solution)/shard_map/dot_general | solution.py:30
  381.5 11.5 %convolution_convert_fusion = bf16[2048,1536]{1,0:T(8,128)(2,1)} fusion(bf16[1024,2048]{1,0:T(8,128)(2,1)} %constant_dynamic-update-slice_fusion, bf16[1024,1536]{1,0:T(8,128)(2,1)} %get-tuple-element.95), kind=kOutput, calls=%fused_computation.1 | convolution fusion | flops 6445596672 | bytes 13631488 | tf_op jit(solution)/shard_map/dot_general | solution.py:30
  394.6 10.5 %shard_map.247 = (bf16[4,256,512]{2,1,0:T(8,128)(2,1)S(1)}, f32[256,2048]{1,0:T(8,128)}, bf16[256,2048]{1,0:T(8,128)(2,1)}, f32[1,2048]{1,0:T(1,128)S(1)}) custom-call(s32[1]{0:T(128)} %bitcast.z_ref, bf16[256,2048]{1,0:T(8,128)(2,1)} %copy-done.21, bf16[256,2048]{1,0:T(8,128)(2,1)} %copy-done.3, bf16[256,2048]{1,0:T(8,128)(2,1)} %go_ref.1, ...), custom_call_target="tpu_custom_call" | custom-call | flops 2147483648 | bytes 18874368 | tf_op jit(solution)/shard_map/pallas_call | solution.py:425
  405.2 4.0 collective-permute-start.20
  410.6 5.4 collective-permute-done.20
  416.0 11.9 %collective-permute-done.19 = bf16[256,512]{1,0:T(8,128)(2,1)S(1)} collective-permute-done((bf16[256,512]{1,0:T(8,128)(2,1)S(1)}, bf16[256,512]{1,0:T(8,128)(2,1)S(1)}, u32[]{:S(2)}, u32[]{:S(2)}) %collective-permute-start.19) | collective-permute-done | bytes 262176 | tf_op jit(solution)/shard_map/ppermute | solution.py:611
  430.0 20.0 %shard_map.248 = (bf16[1024,1024]{1,0:T(8,128)(2,1)}, f32[8,128]{1,0:T(8,128)S(1)}) custom-call(s32[1]{0:T(128)} %bitcast.z_ref, bf16[1024,1024]{1,0:T(8,128)(2,1)} %get-tuple-element.73.side_ref, bf16[1024,768]{1,0:T(8,128)(2,1)} %get-tuple-element.102.raw_ref, bf16[4,256,512]{2,1,0:T(8,128)(2,1)} %pad_maximum_fusion.1.gm_ref, ...), custom_call_target="tpu_custom_call" | custom-call | flops 5368709120 | bytes 12582912 | tf_op jit(solution)/shard_map/pallas_call | solution.py:258
  449.9 10.5 %shard_map.249 = (bf16[2048,1024]{1,0:T(8,128)(2,1)}, f32[2048,128]{1,0:T(8,128)S(1)}) custom-call(bf16[1024,2048]{1,0:T(8,128)(2,1)} %get-tuple-element.106.entry_ref, bf16[1024,1024]{1,0:T(8,128)(2,1)} %get-tuple-element.105.grad_ref, bf16[2048,1024]{1,0:T(8,128)(2,1)} %copy-done.10), custom_call_target="tpu_custom_call" | custom-call | flops 4294967296 | bytes 14680064 | tf_op jit(solution)/shard_map/pallas_call | solution.py:511
  463.6 6.0 collective-permute-start.12
  472.8 6.3 shard_map.250
  480.8 4.6 dynamic-slice_bitcast_fusion
  485.6 3.8 convolution_convert_fusion.3
  492.7 6.1 collective-permute-start.28
  500.7 20.2 %collective-permute-done.28 = f32[1,4352]{1,0:T(1,128)S(1)} collective-permute-done((f32[1,4352]{1,0:T(1,128)S(1)}, f32[1,4352]{1,0:T(1,128)S(1)}, u32[]{:S(2)}, u32[]{:S(2)}) %collective-permute-start.28) | collective-permute-done | bytes 17440 | tf_op jit(solution)/shard_map/ppermute | solution.py:534
  527.5 20.8 %collective-permute-done.13 = bf16[256,2048]{1,0:T(8,128)(2,1)S(1)} collective-permute-done((bf16[256,2048]{1,0:T(8,128)(2,1)S(1)}, bf16[256,2048]{1,0:T(8,128)(2,1)S(1)}, u32[]{:S(2)}, u32[]{:S(2)}) %collective-permute-start.13) | collective-permute-done | bytes 1048608 | tf_op jit(solution)/shard_map/ppermute | solution.py:580
  552.6 5.1 collective-permute-start.14
  561.0 9.8 %collective-permute-done.22 = bf16[256,2048]{1,0:T(8,128)(2,1)S(1)} collective-permute-done((bf16[256,2048]{1,0:T(8,128)(2,1)S(1)}, bf16[256,2048]{1,0:T(8,128)(2,1)S(1)}, u32[]{:S(2)}, u32[]{:S(2)}) %collective-permute-start.22) | collective-permute-done | bytes 1048608 | tf_op jit(solution)/shard_map/ppermute | solution.py:611
  574.5 4.4 collective-permute-done.32
  585.6 12.0 %collective-permute-done.33 = bf16[256,512]{1,0:T(8,128)(2,1)S(1)} collective-permute-done((bf16[256,512]{1,0:T(8,128)(2,1)S(1)}, bf16[256,512]{1,0:T(8,128)(2,1)S(1)}, u32[]{:S(2)}, u32[]{:S(2)}) %collective-permute-start.33) | collective-permute-done | bytes 262176 | tf_op jit(solution)/shard_map/ppermute | solution.py:534
  600.2 3.9 collective-permute-done.31
  604.9 6.6 convert_add_fusion
  611.5 4.0 fusion.47
  623.6 13.7 %collective-permute-done.35 = bf16[2,4,512,128]{3,2,1,0:T(8,128)(2,1)S(1)} collective-permute-done((bf16[2,4,512,128]{3,2,1,0:T(8,128)(2,1)S(1)}, bf16[2,4,512,128]{3,2,1,0:T(8,128)(2,1)S(1)}, u32[]{:S(2)}, u32[]{:S(2)}) %collective-permute-start.35) | collective-permute-done | bytes 1048608 | tf_op jit(solution)/shard_map/ppermute | solution.py:534
  639.4 6.1 collective-permute-done.37
  647.6 4.3 collective-permute-done.36
  655.3 4.9 collective-permute-start.41
  667.2 9.1 %collective-permute-done.40 = bf16[512,256]{1,0:T(8,128)(2,1)S(1)} collective-permute-done((bf16[512,256]{1,0:T(8,128)(2,1)S(1)}, bf16[512,256]{1,0:T(8,128)(2,1)S(1)}, u32[]{:S(2)}, u32[]{:S(2)}) %collective-permute-start.40) | collective-permute-done | bytes 262176 | tf_op jit(solution)/shard_map/ppermute | solution.py:611
  (209 shorter events, 111.0 us)
Async XLA Ops:
  7.2 33.6 %all-gather.8.cloned.1.call-start = ((), (), s32[]{:S(2)}) async-start(), calls=%async_computation.7 | async-start | bytes 1310720 | tf_op jit(solution)/shard_map/all_gather | solution.py:616
  9.5 200.9 %all-gather.10.cloned.1.call-start = ((), (), s32[]{:S(2)}) async-start(), calls=%async_computation.8 | async-start | bytes 9437184 | tf_op jit(solution)/shard_map/all_gather | solution.py:617
  40.9 201.1 %all-gather.6.cloned.1.call-start = ((), (), s32[]{:S(2)}) async-start(), calls=%async_computation.3 | async-start | bytes 5242880 | tf_op jit(solution)/shard_map/all_gather | solution.py:637
  40.9 26.8 %collective-permute-start = (bf16[256,2048]{1,0:T(8,128)(2,1)}, bf16[256,2048]{1,0:T(8,128)(2,1)S(1)}, u32[]{:S(2)}, u32[]{:S(2)}) collective-permute-start(bf16[256,2048]{1,0:T(8,128)(2,1)} %x_ref.3), channel_id=1, source_target_pairs={{0,1},{1,2},{2,3},{3,0},{4,5},{5,6},{6,7},{7,4},{8,9},{9,10},{10,1... | collective-permute-start | bytes 3145736 | tf_op jit(solution)/shard_map/ppermute | solution.py:611
  67.7 25.7 %collective-permute-start.1 = (bf16[256,2048]{1,0:T(8,128)(2,1)S(1)}, bf16[256,2048]{1,0:T(8,128)(2,1)S(1)}, u32[]{:S(2)}, u32[]{:S(2)}) collective-permute-start(bf16[256,2048]{1,0:T(8,128)(2,1)S(1)} %collective-permute-done.x_ref), channel_id=1, source_target_pairs={{0,1},{1,2},{2,3},{3,0},{4,5},{5,6},{6,7},{7,4},{8,9},{9,10},{10,1... | collective-permute-start | bytes 3145736 | tf_op jit(solution)/shard_map/ppermute | solution.py:611
  93.4 24.7 %collective-permute-start.2 = (bf16[256,2048]{1,0:T(8,128)(2,1)S(1)}, bf16[256,2048]{1,0:T(8,128)(2,1)S(1)}, u32[]{:S(2)}, u32[]{:S(2)}) collective-permute-start(bf16[256,2048]{1,0:T(8,128)(2,1)S(1)} %collective-permute-done.1.x_ref), channel_id=1, source_target_pairs={{0,1},{1,2},{2,3},{3,0},{4,5},{5,6},{6,7},{7,4},{8,9},{9,10},{10,1... | collective-permute-start | bytes 3145736 | tf_op jit(solution)/shard_map/ppermute | solution.py:611
  118.2 559.1 %reduce-scatter.4.cloned.1.call-start = ((), (), s32[]{:S(2)}) async-start(), calls=%async_computation.4 | async-start | bytes 7077888 | tf_op jit(solution)/shard_map/reduce_scatter | solution.py:706
  157.3 17.4 %collective-permute-start.5 = (bf16[256,512]{1,0:T(8,128)(2,1)S(1)}, bf16[256,512]{1,0:T(8,128)(2,1)S(1)}, u32[]{:S(2)}, u32[]{:S(2)}) collective-permute-start(bf16[256,512]{1,0:T(8,128)(2,1)S(1)} %get-tuple-element.131), channel_id=1, source_target_pairs={{0,3},{1,0},{2,1},{3,2},{4,7},{5,4},{6,5},{7,6},{8,11},{9,8},{10,9... | collective-permute-start | bytes 786440 | tf_op jit(solution)/shard_map/ppermute | solution.py:611
  157.3 51.0 %collective-permute-start.4 = (bf16[256,512]{1,0:T(8,128)(2,1)S(1)}, bf16[256,512]{1,0:T(8,128)(2,1)S(1)}, u32[]{:S(2)}, u32[]{:S(2)}) collective-permute-start(bf16[256,512]{1,0:T(8,128)(2,1)S(1)} %get-tuple-element.132), channel_id=1, source_target_pairs={{0,2},{1,3},{2,0},{3,1},{4,6},{5,7},{6,4},{7,5},{8,10},{9,11},{10,... | collective-permute-start | bytes 786440 | tf_op jit(solution)/shard_map/ppermute | solution.py:611
  157.4 50.9 %collective-permute-start.3 = (bf16[256,512]{1,0:T(8,128)(2,1)S(1)}, bf16[256,512]{1,0:T(8,128)(2,1)}, u32[]{:S(2)}, u32[]{:S(2)}) collective-permute-start(bf16[256,512]{1,0:T(8,128)(2,1)S(1)} %get-tuple-element.133), channel_id=1, source_target_pairs={{0,1},{1,2},{2,3},{3,0},{4,5},{5,6},{6,7},{7,4},{8,9},{9,10},{10,1... | collective-permute-start | bytes 786440 | tf_op jit(solution)/shard_map/ppermute | solution.py:611
  218.7 41.9 %collective-permute-start.6 = (bf16[256,2048]{1,0:T(8,128)(2,1)S(1)}, bf16[256,2048]{1,0:T(8,128)(2,1)}, u32[]{:S(2)}, u32[]{:S(2)}) collective-permute-start(bf16[256,2048]{1,0:T(8,128)(2,1)S(1)} %get-tuple-element.76.x_ref), channel_id=1, source_target_pairs={{0,1},{1,2},{2,3},{3,0},{4,5},{5,6},{6,7},{7,4},{8,9},{9,10},{10,1... | collective-permute-start | bytes 3145736 | tf_op jit(solution)/shard_map/ppermute | solution.py:611
  260.5 28.4 %collective-permute-start.8 = (bf16[256,2048]{1,0:T(8,128)(2,1)}, bf16[256,2048]{1,0:T(8,128)(2,1)S(1)}, u32[]{:S(2)}, u32[]{:S(2)}) collective-permute-start(bf16[256,2048]{1,0:T(8,128)(2,1)} %collective-permute-done.6.x_ref), channel_id=1, source_target_pairs={{0,1},{1,2},{2,3},{3,0},{4,5},{5,6},{6,7},{7,4},{8,9},{9,10},{10,1... | collective-permute-start | bytes 3145736 | tf_op jit(solution)/shard_map/ppermute | solution.py:611
  278.5 32.9 %collective-permute-start.7 = (bf16[256,2048]{1,0:T(8,128)(2,1)S(1)}, bf16[256,2048]{1,0:T(8,128)(2,1)S(1)}, u32[]{:S(2)}, u32[]{:S(2)}) collective-permute-start(bf16[256,2048]{1,0:T(8,128)(2,1)S(1)} %get-tuple-element.82), channel_id=1, source_target_pairs={{0,1},{1,2},{2,3},{3,0},{4,5},{5,6},{6,7},{7,4},{8,9},{9,10},{10,1... | collective-permute-start | bytes 3145736 | tf_op jit(solution)/shard_map/ppermute | solution.py:611
  289.0 44.9 %collective-permute-start.10 = (bf16[256,2048]{1,0:T(8,128)(2,1)S(1)}, bf16[256,2048]{1,0:T(8,128)(2,1)S(1)}, u32[]{:S(2)}, u32[]{:S(2)}) collective-permute-start(bf16[256,2048]{1,0:T(8,128)(2,1)S(1)} %collective-permute-done.8.x_ref), channel_id=1, source_target_pairs={{0,1},{1,2},{2,3},{3,0},{4,5},{5,6},{6,7},{7,4},{8,9},{9,10},{10,1... | collective-permute-start | bytes 3145736 | tf_op jit(solution)/shard_map/ppermute | solution.py:611
  311.8 43.4 %collective-permute-start.9 = (bf16[256,2048]{1,0:T(8,128)(2,1)S(1)}, bf16[256,2048]{1,0:T(8,128)(2,1)S(1)}, u32[]{:S(2)}, u32[]{:S(2)}) collective-permute-start(bf16[256,2048]{1,0:T(8,128)(2,1)S(1)} %add_convert_fusion.8), channel_id=1, source_target_pairs={{0,1},{1,2},{2,3},{3,0},{4,5},{5,6},{6,7},{7,4},{8,9},{9,10},{10,1... | collective-permute-start | bytes 3145736 | tf_op jit(solution)/shard_map/ppermute | solution.py:611
  356.6 36.4 %collective-permute-start.11 = (bf16[256,2048]{1,0:T(8,128)(2,1)}, bf16[256,2048]{1,0:T(8,128)(2,1)S(1)}, u32[]{:S(2)}, u32[]{:S(2)}) collective-permute-start(bf16[256,2048]{1,0:T(8,128)(2,1)} %add_convert_fusion.7), channel_id=1, source_target_pairs={{0,1},{1,2},{2,3},{3,0},{4,5},{5,6},{6,7},{7,4},{8,9},{9,10},{10,1... | collective-permute-start | bytes 3145736 | tf_op jit(solution)/shard_map/ppermute | solution.py:611
  394.0 285.7 %reduce-scatter.6.cloned.1.call-start = ((), (), s32[]{:S(2)}) async-start(), calls=%async_computation.5 | async-start | bytes 7077888 | tf_op jit(solution)/shard_map/reduce_scatter | solution.py:706
  394.6 287.6 %reduce-scatter.8.cloned.1.call-start = ((), (), s32[]{:S(2)}) async-start(), calls=%async_computation.6 | async-start | bytes 7077888 | tf_op jit(solution)/shard_map/reduce_scatter | solution.py:706
  405.2 10.8 %collective-permute-start.20 = (bf16[256,512]{1,0:T(8,128)(2,1)S(1)}, bf16[256,512]{1,0:T(8,128)(2,1)S(1)}, u32[]{:S(2)}, u32[]{:S(2)}) collective-permute-start(bf16[256,512]{1,0:T(8,128)(2,1)S(1)} %get-tuple-element.127), channel_id=1, source_target_pairs={{0,3},{1,0},{2,1},{3,2},{4,7},{5,4},{6,5},{7,6},{8,11},{9,8},{10,9... | collective-permute-start | bytes 786440 | tf_op jit(solution)/shard_map/ppermute | solution.py:611
  409.2 18.7 %collective-permute-start.19 = (bf16[256,512]{1,0:T(8,128)(2,1)S(1)}, bf16[256,512]{1,0:T(8,128)(2,1)S(1)}, u32[]{:S(2)}, u32[]{:S(2)}) collective-permute-start(bf16[256,512]{1,0:T(8,128)(2,1)S(1)} %get-tuple-element.128), channel_id=1, source_target_pairs={{0,2},{1,3},{2,0},{3,1},{4,6},{5,7},{6,4},{7,5},{8,10},{9,11},{10,... | collective-permute-start | bytes 786440 | tf_op jit(solution)/shard_map/ppermute | solution.py:611
  409.2 18.7 %collective-permute-start.18 = (bf16[256,512]{1,0:T(8,128)(2,1)S(1)}, bf16[256,512]{1,0:T(8,128)(2,1)}, u32[]{:S(2)}, u32[]{:S(2)}) collective-permute-start(bf16[256,512]{1,0:T(8,128)(2,1)S(1)} %get-tuple-element.129), channel_id=1, source_target_pairs={{0,1},{1,2},{2,3},{3,0},{4,5},{5,6},{6,7},{7,4},{8,9},{9,10},{10,1... | collective-permute-start | bytes 786440 | tf_op jit(solution)/shard_map/ppermute | solution.py:611
  460.8 10.4 %collective-permute-start.24 = (f32[1,4352]{1,0:T(1,128)S(1)}, f32[1,4352]{1,0:T(1,128)S(1)}, u32[]{:S(2)}, u32[]{:S(2)}) collective-permute-start(f32[1,4352]{1,0:T(1,128)S(1)} %broadcast_in_dim.51), channel_id=1, source_target_pairs={{0,4},{4,0},{8,12},{12,8},{16,20},{20,16},{24,28},{28,24},{1,5},{5... | collective-permute-start | bytes 52232 | tf_op jit(solution)/shard_map/ppermute | solution.py:534
  463.6 57.4 %collective-permute-start.12 = (bf16[256,2048]{1,0:T(8,128)(2,1)}, bf16[256,2048]{1,0:T(8,128)(2,1)}, u32[]{:S(2)}, u32[]{:S(2)}) collective-permute-start(bf16[256,2048]{1,0:T(8,128)(2,1)} %get-tuple-element.121), channel_id=1, source_target_pairs={{0,1},{4,5},{8,9},{12,13},{16,17},{20,21},{24,25},{28,29}} | collective-permute-start | bytes 3145736 | tf_op jit(solution)/shard_map/ppermute | solution.py:580
  469.6 57.9 %collective-permute-start.15 = (bf16[256,2048]{1,0:T(8,128)(2,1)S(1)}, bf16[256,2048]{1,0:T(8,128)(2,1)}, u32[]{:S(2)}, u32[]{:S(2)}) collective-permute-start(bf16[256,2048]{1,0:T(8,128)(2,1)S(1)} %get-tuple-element.122), channel_id=1, source_target_pairs={{3,2},{7,6},{11,10},{15,14},{19,18},{23,22},{27,26},{31,30}} | collective-permute-start | bytes 3145736 | tf_op jit(solution)/shard_map/ppermute | solution.py:581
  471.3 7.8 %collective-permute-start.25 = (f32[1,4352]{1,0:T(1,128)S(1)}, f32[1,4352]{1,0:T(1,128)S(1)}, u32[]{:S(2)}, u32[]{:S(2)}) collective-permute-start(f32[1,4352]{1,0:T(1,128)S(1)} %reshape_add_fusion), channel_id=1, source_target_pairs={{0,8},{4,12},{8,0},{12,4},{16,24},{20,28},{24,16},{28,20},{1,9},{5... | collective-permute-start | bytes 52232 | tf_op jit(solution)/shard_map/ppermute | solution.py:534
  479.2 6.3 collective-permute-start.26
  485.4 119.5 %collective-permute-start.34 = (bf16[2,2,4,512,256]{4,3,2,1,0:T(8,128)(2,1)}, bf16[2,2,4,512,256]{4,3,2,1,0:T(8,128)(2,1)}, u32[]{:S(2)}, u32[]{:S(2)}) collective-permute-start(bf16[2,2,4,512,256]{4,3,2,1,0:T(8,128)(2,1)} %dynamic-slice_bitcast_fusion), channel_id=1, source_target_pairs={{0,4},{4,0},{8,12},{12,8},{16,20},{20,16},{24,28},{28,24},{1,5},{5... | collective-permute-start | bytes 12582920 | tf_op jit(solution)/shard_map/ppermute | solution.py:534
  485.5 7.1 %collective-permute-start.27 = (f32[1,4352]{1,0:T(1,128)S(1)}, f32[1,4352]{1,0:T(1,128)S(1)}, u32[]{:S(2)}, u32[]{:S(2)}) collective-permute-start(f32[1,4352]{1,0:T(1,128)S(1)} %add.281), channel_id=1, source_target_pairs={{0,1},{1,0},{2,3},{3,2},{4,5},{5,4},{6,7},{7,6},{8,9},{9,8},{10,11... | collective-permute-start | bytes 52232 | tf_op jit(solution)/shard_map/ppermute | solution.py:534
  489.4 36.6 %collective-permute-start.21 = (bf16[256,2048]{1,0:T(8,128)(2,1)S(1)}, bf16[256,2048]{1,0:T(8,128)(2,1)S(1)}, u32[]{:S(2)}, u32[]{:S(2)}) collective-permute-start(bf16[256,2048]{1,0:T(8,128)(2,1)S(1)} %convolution_convert_fusion.3), channel_id=1, source_target_pairs={{0,1},{1,2},{2,3},{3,0},{4,5},{5,6},{6,7},{7,4},{8,9},{9,10},{10,1... | collective-permute-start | bytes 3145736 | tf_op jit(solution)/shard_map/ppermute | solution.py:611
  492.7 28.3 %collective-permute-start.28 = (f32[1,4352]{1,0:T(1,128)S(1)}, f32[1,4352]{1,0:T(1,128)S(1)}, u32[]{:S(2)}, u32[]{:S(2)}) collective-permute-start(f32[1,4352]{1,0:T(1,128)S(1)} %add.282), channel_id=1, source_target_pairs={{0,2},{1,3},{2,0},{3,1},{4,6},{5,7},{6,4},{7,5},{8,10},{9,11},{10,... | collective-permute-start | bytes 52232 | tf_op jit(solution)/shard_map/ppermute | solution.py:534
  521.0 36.8 %collective-permute-start.29 = (bf16[2,2,256,1024]{3,2,1,0:T(8,128)(2,1)S(1)}, bf16[2,2,256,1024]{3,2,1,0:T(8,128)(2,1)S(1)}, u32[]{:S(2)}, u32[]{:S(2)}) collective-permute-start(bf16[2,2,256,1024]{3,2,1,0:T(8,128)(2,1)S(1)} %dynamic-slice_bitcast_fusion.1), channel_id=1, source_target_pairs={{0,4},{4,0},{8,12},{12,8},{16,20},{20,16},{24,28},{28,24},{1,5},{5... | collective-permute-start | bytes 6291464 | tf_op jit(solution)/shard_map/ppermute | solution.py:534
  522.7 25.6 %collective-permute-start.13 = (bf16[256,2048]{1,0:T(8,128)(2,1)S(1)}, bf16[256,2048]{1,0:T(8,128)(2,1)S(1)}, u32[]{:S(2)}, u32[]{:S(2)}) collective-permute-start(bf16[256,2048]{1,0:T(8,128)(2,1)S(1)} %add_convert_fusion.6), channel_id=1, source_target_pairs={{0,1},{1,2},{4,5},{5,6},{8,9},{9,10},{12,13},{13,14},{16,17},{17,1... | collective-permute-start | bytes 3145736 | tf_op jit(solution)/shard_map/ppermute | solution.py:580
  527.4 43.4 %collective-permute-start.22 = (bf16[256,2048]{1,0:T(8,128)(2,1)S(1)}, bf16[256,2048]{1,0:T(8,128)(2,1)S(1)}, u32[]{:S(2)}, u32[]{:S(2)}) collective-permute-start(bf16[256,2048]{1,0:T(8,128)(2,1)S(1)} %add_convert_fusion.1), channel_id=1, source_target_pairs={{0,1},{1,2},{2,3},{3,0},{4,5},{5,6},{6,7},{7,4},{8,9},{9,10},{10,1... | collective-permute-start | bytes 3145736 | tf_op jit(solution)/shard_map/ppermute | solution.py:611
  551.9 65.5 %collective-permute-start.16 = (bf16[256,2048]{1,0:T(8,128)(2,1)}, bf16[256,2048]{1,0:T(8,128)(2,1)S(1)}, u32[]{:S(2)}, u32[]{:S(2)}) collective-permute-start(bf16[256,2048]{1,0:T(8,128)(2,1)} %get-tuple-element.120), channel_id=1, source_target_pairs={{2,1},{3,2},{6,5},{7,6},{10,9},{11,10},{14,13},{15,14},{18,17},{19... | collective-permute-start | bytes 3145736 | tf_op jit(solution)/shard_map/ppermute | solution.py:581
  552.6 109.4 %collective-permute-start.14 = (bf16[256,2048]{1,0:T(8,128)(2,1)}, bf16[256,2048]{1,0:T(8,128)(2,1)S(1)}, u32[]{:S(2)}, u32[]{:S(2)}) collective-permute-start(bf16[256,2048]{1,0:T(8,128)(2,1)} %get-tuple-element.119), channel_id=1, source_target_pairs={{0,1},{1,2},{2,3},{4,5},{5,6},{6,7},{8,9},{9,10},{10,11},{12,13},{... | collective-permute-start | bytes 3145736 | tf_op jit(solution)/shard_map/ppermute | solution.py:580
  559.4 19.5 %collective-permute-start.32 = (bf16[2,256,512]{2,1,0:T(8,128)(2,1)S(1)}, bf16[2,256,512]{2,1,0:T(8,128)(2,1)S(1)}, u32[]{:S(2)}, u32[]{:S(2)}) collective-permute-start(bf16[2,256,512]{2,1,0:T(8,128)(2,1)S(1)} %fusion.13), channel_id=1, source_target_pairs={{0,16},{4,20},{8,24},{12,28},{16,0},{20,4},{24,8},{28,12},{1,17},{... | collective-permute-start | bytes 1572872 | tf_op jit(solution)/shard_map/ppermute | solution.py:534
  570.8 13.2 %collective-permute-start.30 = (bf16[2,256,512]{2,1,0:T(8,128)(2,1)S(1)}, bf16[2,256,512]{2,1,0:T(8,128)(2,1)S(1)}, u32[]{:S(2)}, u32[]{:S(2)}) collective-permute-start(bf16[2,256,512]{2,1,0:T(8,128)(2,1)S(1)} %fusion.12), channel_id=1, source_target_pairs={{0,8},{4,12},{8,0},{12,4},{16,24},{20,28},{24,16},{28,20},{1,9},{5... | collective-permute-start | bytes 1572872 | tf_op jit(solution)/shard_map/ppermute | solution.py:534
  578.9 41.9 %collective-permute-start.23 = (bf16[256,2048]{1,0:T(8,128)(2,1)}, bf16[256,2048]{1,0:T(8,128)(2,1)S(1)}, u32[]{:S(2)}, u32[]{:S(2)}) collective-permute-start(bf16[256,2048]{1,0:T(8,128)(2,1)} %add_convert_fusion), channel_id=1, source_target_pairs={{0,1},{1,2},{2,3},{3,0},{4,5},{5,6},{6,7},{7,4},{8,9},{9,10},{10,1... | collective-permute-start | bytes 3145736 | tf_op jit(solution)/shard_map/ppermute | solution.py:611
  583.9 13.8 %collective-permute-start.33 = (bf16[256,512]{1,0:T(8,128)(2,1)S(1)}, bf16[256,512]{1,0:T(8,128)(2,1)S(1)}, u32[]{:S(2)}, u32[]{:S(2)}) collective-permute-start(bf16[256,512]{1,0:T(8,128)(2,1)S(1)} %fusion.30), channel_id=1, source_target_pairs={{0,8},{4,12},{8,0},{12,4},{16,24},{20,28},{24,16},{28,20},{1,9},{5... | collective-permute-start | bytes 786440 | tf_op jit(solution)/shard_map/ppermute | solution.py:534
  597.7 6.4 collective-permute-start.31
  615.8 21.5 %collective-permute-start.35 = (bf16[2,4,512,128]{3,2,1,0:T(8,128)(2,1)S(1)}, bf16[2,4,512,128]{3,2,1,0:T(8,128)(2,1)S(1)}, u32[]{:S(2)}, u32[]{:S(2)}) collective-permute-start(bf16[2,4,512,128]{3,2,1,0:T(8,128)(2,1)S(1)} %fusion.8), channel_id=1, source_target_pairs={{0,8},{4,12},{8,0},{12,4},{16,24},{20,28},{24,16},{28,20},{1,9},{5... | collective-permute-start | bytes 3145736 | tf_op jit(solution)/shard_map/ppermute | solution.py:534
  617.9 44.2 %collective-permute-start.17 = (bf16[256,2048]{1,0:T(8,128)(2,1)S(1)}, bf16[256,2048]{1,0:T(8,128)(2,1)S(1)}, u32[]{:S(2)}, u32[]{:S(2)}) collective-permute-start(bf16[256,2048]{1,0:T(8,128)(2,1)S(1)} %add_convert_fusion.3), channel_id=1, source_target_pairs={{1,0},{2,1},{3,2},{5,4},{6,5},{7,6},{9,8},{10,9},{11,10},{13,12},{... | collective-permute-start | bytes 3145736 | tf_op jit(solution)/shard_map/ppermute | solution.py:581
  619.3 26.2 %collective-permute-start.37 = (bf16[2,4,512,128]{3,2,1,0:T(8,128)(2,1)S(1)}, bf16[2,4,512,128]{3,2,1,0:T(8,128)(2,1)S(1)}, u32[]{:S(2)}, u32[]{:S(2)}) collective-permute-start(bf16[2,4,512,128]{3,2,1,0:T(8,128)(2,1)S(1)} %fusion.9), channel_id=1, source_target_pairs={{0,16},{4,20},{8,24},{12,28},{16,0},{20,4},{24,8},{28,12},{1,17},{... | collective-permute-start | bytes 3145736 | tf_op jit(solution)/shard_map/ppermute | solution.py:534
  637.6 14.4 %collective-permute-start.36 = (bf16[4,512,128]{2,1,0:T(8,128)(2,1)S(1)}, bf16[4,512,128]{2,1,0:T(8,128)(2,1)S(1)}, u32[]{:S(2)}, u32[]{:S(2)}) collective-permute-start(bf16[4,512,128]{2,1,0:T(8,128)(2,1)S(1)} %fusion.14), channel_id=1, source_target_pairs={{0,16},{4,20},{8,24},{12,28},{16,0},{20,4},{24,8},{28,12},{1,17},{... | collective-permute-start | bytes 1572872 | tf_op jit(solution)/shard_map/ppermute | solution.py:534
  645.8 9.2 %collective-permute-start.38 = (bf16[4,512,128]{2,1,0:T(8,128)(2,1)S(1)}, bf16[4,512,128]{2,1,0:T(8,128)(2,1)S(1)}, u32[]{:S(2)}, u32[]{:S(2)}) collective-permute-start(bf16[4,512,128]{2,1,0:T(8,128)(2,1)S(1)} %fusion.15), channel_id=1, source_target_pairs={{0,8},{4,12},{8,0},{12,4},{16,24},{20,28},{24,16},{28,20},{1,9},{5... | collective-permute-start | bytes 1572872 | tf_op jit(solution)/shard_map/ppermute | solution.py:534
  655.3 11.9 %collective-permute-start.41 = (bf16[512,256]{1,0:T(8,128)(2,1)S(1)}, bf16[512,256]{1,0:T(8,128)(2,1)S(1)}, u32[]{:S(2)}, u32[]{:S(2)}) collective-permute-start(bf16[512,256]{1,0:T(8,128)(2,1)S(1)} %get-tuple-element.125), channel_id=1, source_target_pairs={{0,3},{1,0},{2,1},{3,2},{4,7},{5,4},{6,5},{7,6},{8,11},{9,8},{10,9... | collective-permute-start | bytes 786440 | tf_op jit(solution)/shard_map/ppermute | solution.py:611
  660.2 16.1 %collective-permute-start.40 = (bf16[512,256]{1,0:T(8,128)(2,1)S(1)}, bf16[512,256]{1,0:T(8,128)(2,1)S(1)}, u32[]{:S(2)}, u32[]{:S(2)}) collective-permute-start(bf16[512,256]{1,0:T(8,128)(2,1)S(1)} %get-tuple-element.124), channel_id=1, source_target_pairs={{0,2},{1,3},{2,0},{3,1},{4,6},{5,7},{6,4},{7,5},{8,10},{9,11},{10,... | collective-permute-start | bytes 786440 | tf_op jit(solution)/shard_map/ppermute | solution.py:611
  660.3 16.1 %collective-permute-start.39 = (bf16[512,256]{1,0:T(8,128)(2,1)S(1)}, bf16[512,256]{1,0:T(8,128)(2,1)S(1)}, u32[]{:S(2)}, u32[]{:S(2)}) collective-permute-start(bf16[512,256]{1,0:T(8,128)(2,1)S(1)} %get-tuple-element.123), channel_id=1, source_target_pairs={{0,1},{1,2},{2,3},{3,0},{4,5},{5,6},{6,7},{7,4},{8,9},{9,10},{10,1... | collective-permute-start | bytes 786440 | tf_op jit(solution)/shard_map/ppermute | solution.py:611
  (30 other events, 431.6 us)
Sparse Core Ops, SparseCore 0:
  10.2 30.6 all-gather.7
  42.7 53.8 all-gather.9
  118.3 123.5 all-gather.5
  393.2 63.1 reduce-scatter.3
  460.0 61.7 reduce-scatter.5
  525.0 75.2 reduce-scatter.7

commit v2 on v1

v2 whole, which is shorter than its diff:
```python
import functools

import jax
import jax.numpy as jnp
from jax import lax
from jax.experimental import pallas as pl
from jax.experimental.pallas import tpu as pltpu
from jax.sharding import Mesh, PartitionSpec as P

NORM_EPSILON = 1e-06
ROPE_BASE = 1000000.0
MASK_FILL = -1e30
VMEM_BYTES = 52 * 1024 * 1024
F32 = jnp.float32
BF16 = jnp.bfloat16
DP = ("chip", "core")
COST = 1000

NT = (((1,), (1,)), ((), ()))
TN = (((0,), (0,)), ((), ()))


def mm(a, b):
    return jnp.dot(a, b, preferred_element_type=F32)


def mm_nt(a, b):
    return lax.dot_general(a, b, NT, preferred_element_type=F32)


def mm_tn(a, b):
    return lax.dot_general(a, b, TN, preferred_element_type=F32)


def inv_root_of(values):
    return lax.rsqrt(jnp.mean(values * values, axis=-1, keepdims=True) + NORM_EPSILON)


def norm_back(grad_normed, normal, inv_root):
    return inv_root * (
        grad_normed - normal * jnp.mean(grad_normed * normal, axis=-1, keepdims=True)
    )


def call(kernel, grid_spec, out_shape, flops, nbytes, aliases=None):
    return pl.pallas_call(
        kernel,
        grid_spec=grid_spec,
        out_shape=out_shape,
        input_output_aliases=aliases or {},
        compiler_params=pltpu.CompilerParams(vmem_limit_bytes=VMEM_BYTES),
        cost_estimate=pl.CostEstimate(flops=flops // COST, bytes_accessed=nbytes // COST, transcendentals=0),
    )


def shape(dims, dtype):
    return jax.ShapeDtypeStruct(dims, dtype)


def positions_of(lengths, count_of_rows):
    seq_ends = jnp.cumsum(lengths, dtype=jnp.int32)
    starts = seq_ends - lengths
    place_index = jnp.arange(count_of_rows, dtype=jnp.int32)
    segment = jnp.sum(
        (place_index[:, None] >= seq_ends[None, :]).astype(jnp.int32), axis=1, dtype=jnp.int32
    )
    belongs = segment[:, None] == jnp.arange(lengths.shape[0], dtype=jnp.int32)[None, :]
    offset = jnp.sum(jnp.where(belongs, starts[None, :], 0), axis=1, dtype=jnp.int32)
    return (offset, place_index - offset)


def rope_tables(position, head_width):
    half_width = head_width // 2
    frequency = ROPE_BASE ** (-2.0 * jnp.arange(half_width, dtype=F32) / head_width)
    angles = position.astype(F32)[:, None] * frequency[None, :]
    cosine, sine = jnp.cos(angles), jnp.sin(angles)
    return (
        jnp.concatenate([cosine, cosine], axis=1),
        jnp.concatenate([-sine, sine], axis=1),
    )


def qkv_kernel(heads, kv_heads, dim, sid_ref, x_ref, gain_ref, w_ref, cos_ref, sin_ref, qg_ref, kg_ref, *refs):
    entry_ref, side_ref, raw_ref = refs[-3:]
    x = x_ref[...].astype(F32)
    entry = (x * inv_root_of(x) * gain_ref[...]).astype(BF16)
    entry_ref[...] = entry
    both = mm(entry, w_ref[...])
    cosine, sine = cos_ref[...], sin_ref[...]
    for h in range(heads + kv_heads):
        cols = slice(h * dim, (h + 1) * dim)
        raw = both[:, cols]
        raw_ref[:, cols] = raw.astype(BF16)
        gain = qg_ref[...] if h < heads else kg_ref[...]
        u = raw * inv_root_of(raw) * gain
        turned = u * cosine + pltpu.roll(u, dim // 2, 1) * sine
        if h < heads:
            turned = turned * dim ** (-0.5)
        side_ref[:, cols] = turned.astype(BF16)
    rest = slice((heads + kv_heads) * dim, (heads + 2 * kv_heads) * dim)
    side_ref[:, rest] = both[:, rest].astype(BF16)


def qkv_shard(sid, x, gain, w_qkv, cosine, sine, q_gain, k_gain, heads, kv_heads, dim, block_rows, kept):
    rows, width = x.shape
    cols = w_qkv.shape[1]
    raw_cols = (heads + kv_heads) * dim
    whole = lambda i, sid: (0, 0)
    mine = lambda i, sid: (sid[0], 0)
    in_specs = [
        pl.BlockSpec((rows, width), whole),
        pl.BlockSpec((1, width), whole),
        pl.BlockSpec((width, cols), whole),
        pl.BlockSpec((rows, dim), mine),
        pl.BlockSpec((rows, dim), mine),
        pl.BlockSpec((1, dim), whole),
        pl.BlockSpec((1, dim), whole),
    ]
    args = [sid, x, gain, w_qkv, cosine, sine, q_gain, k_gain]
    aliases = {}
    if kept is not None:
        for j, array in enumerate(kept):
            aliases[len(args)] = j
            args.append(array)
            in_specs.append(pl.BlockSpec(memory_space=pl.ANY))
    return call(
        functools.partial(qkv_kernel, heads, kv_heads, dim),
        pltpu.PrefetchScalarGridSpec(
            num_scalar_prefetch=1,
            grid=(1,),
            in_specs=in_specs,
            out_specs=[
                pl.BlockSpec((rows, width), mine),
                pl.BlockSpec((rows, cols), mine),
                pl.BlockSpec((rows, raw_cols), mine),
            ],
        ),
        [
            shape((block_rows, width), BF16),
            shape((block_rows, cols), BF16),
            shape((block_rows, raw_cols), BF16),
        ],
        2 * rows * width * cols,
        2 * (2 * rows * width + width * cols + 2 * rows * cols),
        aliases,
    )(*args)


def visible_keys(start_ref, first_row, rows, keys):
    key = lax.broadcasted_iota(jnp.int32, (keys, rows), 0)
    query = first_row + lax.broadcasted_iota(jnp.int32, (keys, rows), 1)
    return (key <= query) & (key >= start_ref[:, first_row : first_row + rows])


def attention_kernel(n, heads, kv_heads, dim, z_ref, side_ref, start_ref, mixed_ref, lse_ref):
    rows = side_ref.shape[0] // n
    group = heads // kv_heads
    for i in range(n):
        slot = lax.rem(i - z_ref[0] + n, n)
        keys = (i + 1) * rows
        here = slice(i * rows, (i + 1) * rows)
        visible = visible_keys(start_ref, i * rows, rows, keys)
        for h in range(heads):
            kv = h // group
            key = side_ref[:keys, (heads + kv) * dim : (heads + kv + 1) * dim]
            value = side_ref[
                :keys, (heads + kv_heads + kv) * dim : (heads + kv_heads + kv + 1) * dim
            ]
            cols = slice(h * dim, (h + 1) * dim)
            scores = jnp.where(visible, mm_nt(key, side_ref[here, cols]), MASK_FILL)
            peak = jnp.max(scores, axis=0, keepdims=True)
            spread = jnp.exp(scores - peak)
            total = jnp.sum(spread, axis=0, keepdims=True)
            mixed = mm_tn(value, spread.astype(BF16)) / total
            mixed_ref[slot, :, cols] = mixed.T.astype(BF16)
            lse_ref[h : h + 1, here] = peak + jnp.log(total)


def attention_forward(z, side, start, n, heads, kv_heads, dim):
    block_rows = side.shape[0]
    rows = block_rows // n
    whole2 = lambda i, z: (0, 0)
    return call(
        functools.partial(attention_kernel, n, heads, kv_heads, dim),
        pltpu.PrefetchScalarGridSpec(
            num_scalar_prefetch=1,
            grid=(1,),
            in_specs=[
                pl.BlockSpec(side.shape, whole2),
                pl.BlockSpec((1, block_rows), whole2),
            ],
            out_specs=[
                pl.BlockSpec((n, rows, heads * dim), lambda i, z: (0, 0, 0)),
                pl.BlockSpec((heads, block_rows), whole2),
            ],
        ),
        [shape((n, rows, heads * dim), BF16), shape((heads, block_rows), F32)],
        2 * block_rows * block_rows * heads * dim * 2,
        2 * side.size + 6 * block_rows * heads * dim,
    )(z, side, start)


def attention_back_kernel(n, heads, kv_heads, dim, z_ref, *refs):
    gm_refs = refs[:n]
    side_ref, raw_ref, lse_ref, start_ref, cos_ref, sin_ref, qg_ref, kg_ref = refs[n : n + 8]
    out_ref, gain_ref, gm_ref, key_acc, value_acc = refs[n + 8 :]
    block_rows = side_ref.shape[0]
    rows = block_rows // n
    group = heads // kv_heads
    q_sum = jnp.zeros((1, dim), F32)
    k_sum = jnp.zeros((1, dim), F32)
    for slot, ref in enumerate(gm_refs):
        gm_ref[slot] = ref[...]
    for kv in range(kv_heads):
        key_cols = slice((heads + kv) * dim, (heads + kv + 1) * dim)
        value_cols = slice((heads + kv_heads + kv) * dim, (heads + kv_heads + kv + 1) * dim)
        key_acc[...] = jnp.zeros_like(key_acc)
        value_acc[...] = jnp.zeros_like(value_acc)
        for i in range(n):
            slot = lax.rem(z_ref[0] - i + n, n)
            keys = (i + 1) * rows
            here = slice(i * rows, (i + 1) * rows)
            key = side_ref[:keys, key_cols]
            value = side_ref[:keys, value_cols]
            visible = visible_keys(start_ref, i * rows, rows, keys)
            cosine, sine = cos_ref[here, :], sin_ref[here, :]
            for g in range(group):
                h = kv * group + g
                cols = slice(h * dim, (h + 1) * dim)
                query = side_ref[here, cols]
                grad = gm_ref[slot, :, cols]
                scores = jnp.where(visible, mm_nt(key, query), MASK_FILL)
                soft = jnp.exp(scores - lse_ref[h : h + 1, here])
                grad_weights = mm_nt(value, grad)
                inner = jnp.sum(soft * grad_weights, axis=0, keepdims=True)
                grad_scores = (soft * (grad_weights - inner)).astype(BF16)
                value_acc[:keys, :] += mm(soft.astype(BF16), grad)
                key_acc[:keys, :] += mm(grad_scores, query)
                turned = mm_tn(key, grad_scores).T * dim ** (-0.5)
                back = turned * cosine - pltpu.roll(turned, dim // 2, 1) * sine
                raw = raw_ref[here, cols].astype(F32)
                scale = inv_root_of(raw)
                normal = raw * scale
                q_sum = q_sum + jnp.sum(back * normal, axis=0, keepdims=True)
                out_ref[here, cols] = norm_back(back * qg_ref[...], normal, scale).astype(BF16)
        turned = key_acc[...]
        back = turned * cos_ref[...] - pltpu.roll(turned, dim // 2, 1) * sin_ref[...]
        raw = raw_ref[:, key_cols].astype(F32)
        scale = inv_root_of(raw)
        normal = raw * scale
        k_sum = k_sum + jnp.sum(back * normal, axis=0, keepdims=True)
        out_ref[:, key_cols] = norm_back(back * kg_ref[...], normal, scale).astype(BF16)
        out_ref[:, value_cols] = value_acc[...].astype(BF16)
    gain_ref[...] = jnp.concatenate([q_sum, k_sum, jnp.zeros((6, dim), F32)], axis=0)


def attention_backward(z, gm, side, raw, lse, start, cosine, sine, q_gain, k_gain, heads, kv_heads, dim):
    n = len(gm)
    block_rows = side.shape[0]
    whole2 = lambda i, z: (0, 0)
    ins = (*gm, side, raw, lse, start, cosine, sine, q_gain, k_gain)
    return call(
        functools.partial(attention_back_kernel, n, heads, kv_heads, dim),
        pltpu.PrefetchScalarGridSpec(
            num_scalar_prefetch=1,
            grid=(1,),
            in_specs=[pl.BlockSpec(a.shape, whole2) for a in ins],
            out_specs=[pl.BlockSpec(side.shape, whole2), pl.BlockSpec((8, dim), whole2)],
            scratch_shapes=[
                pltpu.VMEM((n,) + gm[0].shape, BF16),
                pltpu.VMEM((block_rows, dim), F32),
                pltpu.VMEM((block_rows, dim), F32),
            ],
        ),
        [shape(side.shape, BF16), shape((8, dim), F32)],
        2 * block_rows * block_rows * heads * dim * 5,
        12 * side.size,
    )(z, *ins)


def column_block(place_ref, k, other, cols):
    block = 2 * lax.bitwise_xor(place_ref[1], k) + (1 - place_ref[2] if other else place_ref[2])
    return pl.ds(pl.multiple_of(block * cols, cols), cols)


def out_kernel(n, chips, place_ref, *refs):
    mixed_refs = refs[:n]
    own_ref, other_ref, x_ref, gain_ref, hidden_ref, entry_ref, acc = refs[n:]
    k = pl.program_id(0)
    for other, w_ref in enumerate((own_ref, other_ref)):
        part = mm(mixed_refs[0][...], w_ref[0, place_ref[0]])
        for s in range(1, n):
            part = part + mm(mixed_refs[s][...], w_ref[0, lax.rem(place_ref[0] - s + n, n)])
        acc[:, column_block(place_ref, k, other, part.shape[1])] = part

    @pl.when(k == chips - 1)
    def _():
        hidden = acc[...] + x_ref[...].astype(F32)
        hidden_ref[...] = hidden
        entry_ref[...] = (hidden * inv_root_of(hidden) * gain_ref[...]).astype(BF16)


def out_projection(place, mixed, w_own, w_other, x, gain, n):
    rows, width = x.shape
    chips = w_own.shape[0]
    whole = lambda k, place: (0, 0)
    block = pl.BlockSpec((1,) + w_own.shape[1:], lambda k, place: (k, 0, 0, 0))
    return call(
        functools.partial(out_kernel, n, chips),
        pltpu.PrefetchScalarGridSpec(
            num_scalar_prefetch=1,
            grid=(chips,),
            in_specs=[pl.BlockSpec(mixed[0].shape, whole)] * n
            + [
                block,
                block,
                pl.BlockSpec((rows, width), whole),
                pl.BlockSpec((1, width), whole),
            ],
            out_specs=[pl.BlockSpec((rows, width), whole), pl.BlockSpec((rows, width), whole)],
            scratch_shapes=[pltpu.VMEM((rows, width), F32)],
        ),
        [shape((rows, width), F32), shape((rows, width), BF16)],
        4 * rows * w_own.size,
        4 * w_own.size + 10 * rows * width,
    )(place, *mixed, w_own, w_other, x, gain)


def mlp_kernel(tiles, sid_ref, x_ref, go_ref, wg_ref, wu_ref, wd_ref, *refs):
    active_ref, gate_grad_ref, up_grad_ref, copy_ref, down_ref, inner_ref, down_acc, inner_acc = refs[-8:]
    j = pl.program_id(0)
    x = x_ref[...]
    gate = mm(x, wg_ref[...])
    up = mm(x, wu_ref[...])
    sigmoid = jax.nn.sigmoid(gate)
    silu = gate * sigmoid
    active = (silu * up).astype(BF16)
    active_ref[...] = active
    grad_active = mm_nt(go_ref[...], wd_ref[...])
    gate_grad = (grad_active * up * sigmoid * (1.0 + gate * (1.0 - sigmoid))).astype(BF16)
    up_grad = (grad_active * silu).astype(BF16)
    gate_grad_ref[...] = gate_grad
    up_grad_ref[...] = up_grad
    inner = mm_nt(gate_grad, wg_ref[...]) + mm_nt(up_grad, wu_ref[...])
    down = mm(active, wd_ref[...])

    @pl.when(j == 0)
    def _():
        copy_ref[...] = x
        inner_acc[...] = inner
        down_acc[...] = down

    @pl.when(j > 0)
    def _():
        inner_acc[...] += inner
        down_acc[...] += down

    @pl.when(j == tiles - 1)
    def _():
        inner_ref[...] = inner_acc[...].astype(BF16)
        down_ref[...] = down_acc[...].astype(BF16)


def mlp_shard(sid, x, grads, weights, kept, block_rows):
    w_gate, w_up, w_down = weights
    rows, width = x.shape
    units = w_gate.shape[1]
    tile = next(t for t in (512, 384, 256, 128) if units % t == 0)
    tiles = units // tile
    whole = pl.BlockSpec((rows, width), lambda j, sid: (0, 0))
    mine = pl.BlockSpec((rows, width), lambda j, sid: (sid[0], 0))
    tiled = pl.BlockSpec((rows, tile), lambda j, sid: (sid[0], j))
    column = pl.BlockSpec((width, tile), lambda j, sid: (0, j))
    in_specs = [
        whole,
        whole if grads.shape[0] == rows else mine,
        column,
        column,
        pl.BlockSpec((tile, width), lambda j, sid: (j, 0)),
    ]
    args = [sid.reshape(1), x, grads, w_gate, w_up, w_down]
    aliases = {}
    if kept is not None:
        for j, array in enumerate(kept):
            aliases[len(args)] = j
            args.append(array)
            in_specs.append(pl.BlockSpec(memory_space=pl.ANY))
    *kept, down, inner = call(
        functools.partial(mlp_kernel, tiles),
        pltpu.PrefetchScalarGridSpec(
            num_scalar_prefetch=1,
            grid=(tiles,),
            in_specs=in_specs,
            out_specs=[tiled] * 3 + [mine] + [whole] * 2,
            scratch_shapes=[pltpu.VMEM((rows, width), F32), pltpu.VMEM((rows, width), F32)],
        ),
        [shape((block_rows, units), BF16)] * 3
        + [shape((block_rows, width), BF16)]
        + [shape((rows, width), BF16)] * 2,
        2 * rows * width * units * 6,
        2 * (3 * width * units + 3 * rows * units + 5 * rows * width),
        aliases,
    )(*args)
    return kept, down, inner


def mid_kernel(n, chips, place_ref, own_part_ref, go_ref, hidden_ref, gain_ref, own_ref, other_ref, *refs):
    got_refs = refs[:-5]
    gm_ref, gh_ref, mid_ref, part_ref, acc = refs[-5:]
    k = pl.program_id(0)

    @pl.when(k == 0)
    def _():
        hidden = hidden_ref[...]
        scale = inv_root_of(hidden)
        normal = hidden * scale
        inner = own_part_ref[...].astype(F32)
        for ref in got_refs:
            inner = inner + ref[...].astype(F32)
        part_ref[...] = jnp.sum(inner * normal, axis=0, keepdims=True)
        grad_hidden = go_ref[...].astype(F32) + norm_back(inner * gain_ref[...], normal, scale)
        gh_ref[...] = grad_hidden
        mid_ref[...] = grad_hidden.astype(BF16)
        acc[...] = jnp.zeros_like(acc)

    cols = own_ref.shape[3]
    own = mid_ref[:, column_block(place_ref, k, False, cols)]
    other = mid_ref[:, column_block(place_ref, k, True, cols)]
    for s in range(n):
        t = lax.rem(place_ref[0] + s, n)
        acc[s] += mm_nt(own, own_ref[0, t]) + mm_nt(other, other_ref[0, t])

    @pl.when(k == chips - 1)
    def _():
        gm_ref[...] = acc[...].astype(BF16)


def mid_stage(place, own, got, go, hidden, gain, w_own, w_other, n):
    rows, width = go.shape
    chips, _, heads_cols, _ = w_own.shape
    whole = pl.BlockSpec((rows, width), lambda k, place: (0, 0))
    line = pl.BlockSpec((1, width), lambda k, place: (0, 0))
    block = pl.BlockSpec((1,) + w_own.shape[1:], lambda k, place: (k, 0, 0, 0))
    return call(
        functools.partial(mid_kernel, n, chips),
        pltpu.PrefetchScalarGridSpec(
            num_scalar_prefetch=1,
            grid=(chips,),
            in_specs=[whole, whole, whole, line, block, block] + [whole] * len(got),
            out_specs=[
                pl.BlockSpec((n, rows, heads_cols), lambda k, place: (0, 0, 0)),
                whole,
                whole,
                line,
            ],
            scratch_shapes=[pltpu.VMEM((n, rows, heads_cols), F32)],
        ),
        [
            shape((n, rows, heads_cols), BF16),
            shape((rows, width), F32),
            shape((rows, width), BF16),
            shape((1, width), F32),
        ],
        4 * rows * w_own.size,
        4 * w_own.size + 20 * rows * width,
    )(place, own, go, hidden, gain, w_own, w_other, *got)


def out_weight_kernel(n, place_ref, *refs):
    mixed_refs, mid_ref, out_ref = refs[:n], refs[n], refs[-1]
    for s in range(n):
        t = lax.rem(place_ref[0] - s + n, n)
        grad = mm_tn(mixed_refs[s][...], mid_ref[...])
        if len(refs) > n + 2:
            grad = grad + refs[n + 1][0, t].astype(F32)
        out_ref[0, t] = grad.astype(BF16)


def out_weight_grad(place, side, mixed, mid, n, chips, got):
    rows, width = mid.shape
    cols = mixed[0].shape[1]
    own = width // (2 * chips)
    block = pl.BlockSpec((1, n, cols, own), lambda c, place: (c, 0, 0, 0))
    extra = [] if got is None else [got]
    return call(
        functools.partial(out_weight_kernel, n),
        pltpu.PrefetchScalarGridSpec(
            num_scalar_prefetch=1,
            grid=(chips,),
            in_specs=[pl.BlockSpec((rows, cols), lambda c, place: (0, 0))] * n
            + [pl.BlockSpec((rows, own), lambda c, place: (0, 2 * c + place[3]))]
            + [block] * len(extra),
            out_specs=block,
        ),
        shape((chips, n, cols, own), BF16),
        rows * width * cols * n,
        n * cols * width,
    )(jnp.concatenate([place, side]), *mixed, mid, *extra)


def entry_kernel(sid_ref, grad_ref, w_ref, out_ref):
    out_ref[...] = mm_nt(grad_ref[...], w_ref[...]).astype(BF16)


def entry_shard(sid, grads, w_qkv, rows):
    width, cols = w_qkv.shape
    tile = width // 4
    return call(
        entry_kernel,
        pltpu.PrefetchScalarGridSpec(
            num_scalar_prefetch=1,
            grid=(4,),
            in_specs=[
                pl.BlockSpec((rows, cols), lambda j, sid: (sid[0], 0)),
                pl.BlockSpec((tile, cols), lambda j, sid: (j, 0)),
            ],
            out_specs=pl.BlockSpec((rows, tile), lambda j, sid: (0, j)),
        ),
        shape((rows, width), BF16),
        2 * rows * width * cols,
        2 * (width * cols + rows * cols + rows * width),
    )(sid, grads, w_qkv)


def rows_grad_kernel(x_ref, gate_ref, up_ref, out_ref):
    units = gate_ref.shape[1]
    for j, ref in enumerate((gate_ref, up_ref)):
        out_ref[0, :, j * units : (j + 1) * units] = mm_tn(x_ref[...], ref[...]).astype(BF16)


def gate_up_grad(x, gate_grad, up_grad, batches):
    block_rows, width = x.shape
    units = gate_grad.shape[1]
    rows = width // batches
    whole = lambda j: (0, 0)
    return call(
        rows_grad_kernel,
        pltpu.PrefetchScalarGridSpec(
            num_scalar_prefetch=0,
            grid=(batches,),
            in_specs=[
                pl.BlockSpec((block_rows, rows), lambda j: (0, j)),
                pl.BlockSpec((block_rows, units), whole),
                pl.BlockSpec((block_rows, units), whole),
            ],
            out_specs=pl.BlockSpec((1, rows, 2 * units), lambda j: (j, 0, 0)),
        ),
        shape((batches, rows, 2 * units), BF16),
        4 * block_rows * width * units,
        2 * (block_rows * width + 2 * block_rows * units + 2 * width * units),
    )(x, gate_grad, up_grad)


def cols_grad_kernel(active_ref, grad_ref, out_ref):
    out_ref[0] = mm_tn(active_ref[...], grad_ref[...]).astype(BF16)


def down_grad(active, grad_all, batches):
    block_rows, units = active.shape
    width = grad_all.shape[1]
    cols = width // batches
    return call(
        cols_grad_kernel,
        pltpu.PrefetchScalarGridSpec(
            num_scalar_prefetch=0,
            grid=(batches,),
            in_specs=[
                pl.BlockSpec((block_rows, units), lambda j: (0, 0)),
                pl.BlockSpec((block_rows, cols), lambda j: (0, j)),
            ],
            out_specs=pl.BlockSpec((1, units, cols), lambda j: (j, 0, 0)),
        ),
        shape((batches, units, cols), BF16),
        2 * block_rows * width * units,
        2 * (block_rows * units + block_rows * width + width * units),
    )(active, grad_all)


def qkv_weight_kernel(side_ref, entry_ref, grad_ref, w_ref, out_ref, part_ref):
    grad = mm_tn(entry_ref[...], grad_ref[...])
    out_ref[0] = grad.astype(BF16)
    both = grad * w_ref[...].astype(F32)
    lanes = part_ref.shape[2]
    total = both[:, :lanes]
    for first in range(lanes, both.shape[1], lanes):
        total = total + both[:, first : first + lanes]
    part_ref[0] = total


def qkv_weight_grad(side, entry, grads, w_qkv, chips):
    block_rows, width = entry.shape
    cols = grads.shape[1]
    rows = width // (2 * chips)
    return call(
        qkv_weight_kernel,
        pltpu.PrefetchScalarGridSpec(
            num_scalar_prefetch=1,
            grid=(chips,),
            in_specs=[
                pl.BlockSpec((block_rows, rows), lambda j, side: (0, 2 * j + side[0])),
                pl.BlockSpec((block_rows, cols), lambda j, side: (0, 0)),
                pl.BlockSpec((rows, cols), lambda j, side: (2 * j + side[0], 0)),
            ],
            out_specs=[
                pl.BlockSpec((1, rows, cols), lambda j, side: (j, 0, 0)),
                pl.BlockSpec((1, rows, 128), lambda j, side: (j, 0, 0)),
            ],
        ),
        [shape((chips, rows, cols), BF16), shape((chips, rows, 128), F32)],
        block_rows * width * cols,
        2 * (block_rows * width + block_rows * cols + 2 * width * cols),
    )(side, entry, grads, w_qkv)


def exchange(value, axis, step):
    size = lax.axis_size(axis)
    return lax.ppermute(value, axis, [(i, i ^ step) for i in range(size)])


def total_over(value, axis):
    step = 1
    while step < lax.axis_size(axis):
        value = value + exchange(value, axis, step)
        step *= 2
    return value


@jax.tree_util.register_pytree_node_class
class Halves:
    def __init__(self, values, axes):
        self.values, self.axes = tuple(values), tuple(axes)

    def tree_flatten(self):
        return self.values, self.axes

    @classmethod
    def tree_unflatten(cls, axes, values):
        return cls(values, axes)

    def orders(self, batches):
        bits = tuple(range(1, batches.bit_length() - 1))
        return bits, bits[::-1]

    def send(self, step, batches):
        done = [send_half(v, a, o[step]) for v, a, o in zip(self.values, self.axes, self.orders(batches))]
        kept, got, axes = zip(*done)
        return Halves(kept, axes), got

    def add(self, got):
        values = [v.astype(F32) + g.astype(F32) for v, g in zip(self.values, got)]
        return Halves(values, self.axes)

    def double(self, step, batches):
        done = []
        for value, axes, order in zip(self.values, self.axes, self.orders(batches)):
            got = exchange(value, DP, 1 << order[step])
            done.append((jnp.stack([value, got]), (order[step],) + axes))
        return Halves(*zip(*done))

    def pieces(self, batches):
        bits = self.orders(batches)[1]
        done = []
        for value, axes in zip(self.values, self.axes):
            rest = list(range(len(axes), value.ndim))
            value = value.transpose([axes.index(bit) for bit in bits] + rest)
            done.append(value.reshape((batches // 2,) + value.shape[len(axes) :]))
        return jnp.concatenate(done, axis=2)


def send_half(value, axes, bit):
    own = lax.rem(lax.div(lax.axis_index(DP), 1 << bit), 2)
    at = axes.index(bit)
    sent = lax.dynamic_index_in_dim(value, 1 - own, at, False).astype(BF16)
    kept = lax.dynamic_index_in_dim(value, own, at, False)
    return kept, exchange(sent, DP, 1 << bit), axes[:at] + axes[at + 1 :]


def halves_of(value):
    bits = value.shape[0].bit_length() - 1
    value = value.reshape((2,) * bits + value.shape[1:])
    axes = tuple(range(1, bits + 1))[::-1]
    middle = value.shape[-1] // 2
    return Halves((value[..., :middle], value[..., middle:]), (axes, axes))


def join(*values):
    return lax.optimization_barrier(values)


def add_low(a, b):
    return (a.astype(F32) + b.astype(F32)).astype(BF16)


class RingSum:
    def __init__(self, shift):
        self.parts, self.shift, self.step, self.moving = [], shift, 0, None

    def add(self):
        self.step += 1
        if self.step < len(self.parts):
            part = self.parts[self.step]
            self.moving = part if self.step == 1 else add_low(self.moving, part)

    def send(self):
        if self.step < len(self.parts):
            self.moving = self.shift(self.moving)

    def hop(self):
        self.add()
        self.send()


def total_of(own, got):
    total = own.astype(F32)
    for value in got:
        total = total + value.astype(F32)
    return total


def local(
    tokens,
    seq_lengths,
    attn_gain,
    mlp_gain,
    q_gain,
    k_gain,
    w_query,
    key_weight,
    value_weight,
    w_out,
    w_gate,
    w_up,
    w_down,
    out_grad,
):
    n = lax.axis_size("tensor")
    batches = lax.axis_size(DP)
    rows, width = tokens.shape
    block_rows = rows * n
    dim = q_gain.shape[0]
    heads = w_query.shape[1] // dim
    kv_heads = key_weight.shape[1] // dim
    z = lax.axis_index("tensor").astype(jnp.int32)
    zs = z.reshape(1)
    ring = [(i, (i + 1) % n) for i in range(n)]
    shift = lambda v, d=1: lax.ppermute(v, "tensor", [(i, (i + d) % n) for i in range(n)])
    shard_of = lambda s: lax.rem(z - s + n, n).reshape(1)

    chips = batches // 2
    core = lax.axis_index("core").astype(jnp.int32).reshape(1)
    place = jnp.stack([z, lax.axis_index("chip").astype(jnp.int32), core[0]])
    steps = batches.bit_length() - 2

    own_cols = width // batches
    piece = lax.dynamic_slice_in_dim(w_out, lax.axis_index(DP) * own_cols, own_cols, 1)
    piece = lax.all_gather(piece, "tensor", axis=0, tiled=False)

    offset, position = positions_of(seq_lengths[0], block_rows)
    start = offset[None, :]
    cosine, sine = rope_tables(position, dim)
    w_qkv = jnp.concatenate([w_query, key_weight, value_weight], axis=1)
    gain_one, gain_two = attn_gain[None, :], mlp_gain[None, :]
    qg, kg = q_gain[None, :], k_gain[None, :]

    came = shift(tokens)
    came, piece, w_qkv, cosine, sine, start = join(came, piece, w_qkv, cosine, sine, start)
    blocks = [tokens, came]
    middle = piece.shape[1] // 2
    halves = Halves((piece[:, :middle], piece[:, middle:]), ((), ()))
    kept, ready = None, 0
    for s in range(1, n):
        came = shift(blocks[s]) if s < n - 1 else None
        while ready <= s:
            kept = qkv_shard(
                shard_of(ready), blocks[ready], gain_one, w_qkv, cosine, sine, qg, kg, heads, kv_heads,
                dim, block_rows, kept,
            )
            ready += 1
        if s <= steps:
            halves = halves.double(s - 1, batches)
        if came is not None:
            came, kept, halves = join(came, kept, halves)
            blocks.append(came)
    entry_all, side, raw = kept
    w_own = halves.pieces(batches)
    w_other = exchange(w_own, "core", 1)

    later_grad, _ = join(out_grad, blocks[-1])
    grad_all = lax.all_gather(later_grad, "tensor", axis=0, tiled=True)

    mixed, lse = attention_forward(zs, side, start, n, heads, kv_heads, dim)
    mixed, w_own = join(mixed, w_own)
    mixed = [mixed[0]] + [shift(mixed[d], d) for d in range(1, n)]
    mixed, w_other = join(mixed, w_other)
    hidden, mlp_entry = out_projection(place, mixed, w_own, w_other, tokens, gain_two, n)

    weights = (w_gate, w_up, w_down)
    down_sum, inner_sum = RingSum(shift), RingSum(shift)
    over_dp = lambda g: lax.psum_scatter(g, DP, scatter_dimension=0, tiled=False)
    blocks, kept = [mlp_entry], None
    for t in range(2 * n - 2):
        if t < n - 1:
            blocks.append(shift(blocks[t]))
        else:
            inner_sum.hop()
        for s in {0: (0,), 1: (), 2: (1, 2)}.get(t, (t,)):
            if s < n:
                kept, down, inner = mlp_shard(
                    shard_of(s), blocks[s], grad_all if s else out_grad, weights, kept, block_rows
                )
                down_sum.parts.append(down)
                inner_sum.parts.append(inner)
        if t == 1:
            blocks, kept, grad_all = join(blocks, kept, grad_all)
        elif t == 2 * n - 4:
            w_down_grad = down_grad(active, grad_all, batches)
            inner_sum.moving, w_down_grad = join(inner_sum.moving, w_down_grad)
            w_down_grad = over_dp(w_down_grad)
        elif t == 2 * n - 3:
            down_sum.hop()
            w_gate_up_grad = gate_up_grad(mlp_all, gate_grad, up_grad, batches)
            inner_sum.moving, down_sum.moving, w_gate_up_grad = join(
                inner_sum.moving, down_sum.moving, w_gate_up_grad
            )
            w_gate_up_grad = over_dp(w_gate_up_grad)
        else:
            blocks, kept, inner_sum.parts, inner_sum.moving = join(
                blocks, kept, inner_sum.parts, inner_sum.moving
            )
            active, gate_grad, up_grad, mlp_all = kept

    gm, grad_hidden, grad_mid, mlp_part = mid_stage(
        place, inner_sum.parts[0], (inner_sum.moving,), out_grad, hidden, gain_two, w_own, w_other, n
    )

    gm = [gm[0]] + [shift(gm[d], d) for d in range(1, n)]
    got = out_weight_grad(place, 1 - core, mixed, grad_mid, n, chips, None)
    down_sum.add()
    gm, got, down_sum.moving = join(gm, got, down_sum.moving)

    down_sum.send()
    got = exchange(got, "core", 1)
    grads, gain_parts = attention_backward(
        zs, gm, side, raw, lse, start, cosine, sine, qg, kg, heads, kv_heads, dim
    )

    entry_part = lambda s: entry_shard(shard_of(s), grads, w_qkv, rows)
    entry_sum = RingSum(shift)
    entry_sum.parts = [None, entry_part(1)] + [None] * (n - 2)
    w_out_grad = out_weight_grad(place, core, mixed, grad_mid, n, chips, got)
    entry_sum.parts[1], grads, w_out_grad, down_sum.moving = join(
        entry_sum.parts[1], grads, w_out_grad, down_sum.moving
    )

    down_sum.add()
    out_halves = halves_of(w_out_grad)
    entry_sum.add()

    entry_sum.send()
    down_sum.send()
    out_halves, out_got = out_halves.send(0, batches)
    qkv_sent, lanes_sent = qkv_weight_grad(1 - core, entry_all, grads, w_qkv, chips)
    w_qkv_grad, lanes = qkv_weight_grad(core, entry_all, grads, w_qkv, chips)
    entry_sum.parts[2 % n] = entry_part(2 % n)
    entry_sum.add()
    state = (entry_sum.moving, down_sum.moving, out_halves, out_got, qkv_sent, w_qkv_grad)
    state, grads, lanes, lanes_sent = join(state, grads, lanes, lanes_sent)
    entry_sum.moving, down_sum.moving, out_halves, out_got, qkv_sent, w_qkv_grad = state
    lanes, lanes_sent = jnp.sum(lanes, axis=2), jnp.sum(lanes_sent, axis=2)
    lanes = jnp.where(core[0] == 0, jnp.stack([lanes, lanes_sent], 1), jnp.stack([lanes_sent, lanes], 1))
    attn_part = lanes.reshape(width) / attn_gain
    totals = jnp.concatenate([attn_part, mlp_part[0], gain_parts[0], gain_parts[1]])[None, :]

    entry_sum.send()
    down_sum.add()
    down_sum.send()
    out_halves = out_halves.add(out_got)
    if steps > 1:
        out_halves, out_got = out_halves.send(1, batches)
    qkv_got = exchange(qkv_sent, "core", 1)
    totals = total_over(totals, "tensor")
    entry_sum.parts[3 % n] = entry_part(3 % n)
    entry_sum.add()
    state = (entry_sum.moving, down_sum.moving, out_halves, out_got, qkv_got, w_qkv_grad)
    state, grads, totals = join(state, grads, totals)
    entry_sum.moving, down_sum.moving, out_halves, out_got, qkv_got, w_qkv_grad = state

    if steps > 1:
        out_halves = out_halves.add(out_got)
    for step in range(2, steps):
        out_halves, out_got = out_halves.send(step, batches)
        out_halves = out_halves.add(out_got)
    w_out_grad = jnp.concatenate(out_halves.values, axis=-1).astype(BF16)
    out_sum = RingSum(shift)
    out_sum.parts = [lax.dynamic_index_in_dim(w_out_grad, shard_of(d)[0], 0, False) for d in range(n)]
    for _ in range(n - 1):
        out_sum.hop()
    qkv_halves = halves_of(add_low(w_qkv_grad, qkv_got))
    for step in range(steps):
        qkv_halves, qkv_got = qkv_halves.send(step, batches)
        if step < steps - 1:
            qkv_halves = qkv_halves.add(qkv_got)
    totals = total_over(totals, DP)
    for s in range(3, n):
        entry_sum.send()
        down_sum.add()
        down_sum.send()
        entry_sum.parts[(s + 1) % n] = entry_part((s + 1) % n)
        if s < n - 1:
            entry_sum.add()
            entry_sum.moving, down_sum.moving, grads = join(entry_sum.moving, down_sum.moving, grads)
    grad_entry = total_of(entry_sum.parts[0], [entry_sum.moving]).astype(F32)
    state = (grad_entry, qkv_halves, qkv_got, out_sum.parts[0], out_sum.moving)
    (grad_entry, qkv_halves, qkv_got, own, moved), w_down_grad, w_gate_up_grad, totals = join(
        state, w_down_grad, w_gate_up_grad, totals
    )
    w_out_grad = total_of(own, [moved])
    w_qkv_grad = jnp.concatenate(qkv_halves.add(qkv_got).values, axis=-1)
    output = total_of(hidden, [down_sum.parts[0], down_sum.moving]).astype(BF16)

    x = tokens.astype(F32)
    scale = inv_root_of(x)
    token_grad = (grad_hidden + norm_back(grad_entry * attn_gain, x * scale, scale)).astype(BF16)

    totals = totals[0]
    attn_gain_grad = totals[:width]
    mlp_gain_grad = totals[width : 2 * width]
    q_gain_grad = totals[2 * width : 2 * width + dim]
    k_gain_grad = totals[2 * width + dim :]
    w_down_grad, w_gate_up_grad = w_down_grad.astype(F32), w_gate_up_grad.astype(F32)
    a, b = heads * dim, (heads + kv_heads) * dim
    return (
        output,
        token_grad,
        attn_gain_grad,
        mlp_gain_grad,
        q_gain_grad,
        k_gain_grad,
        w_qkv_grad[:, :a],
        w_qkv_grad[:, a:b],
        w_qkv_grad[:, b:],
        w_out_grad,
        w_gate_up_grad[:, : w_gate.shape[1]],
        w_gate_up_grad[:, w_gate.shape[1] :],
        w_down_grad,
    )


def solution(mesh):
    batches, shards = mesh.shape["dp"], mesh.shape["tensor"]
    return jax.shard_map(
        local,
        mesh=Mesh(mesh.devices.reshape(batches // 2, 2, shards), DP + ("tensor",)),
        in_specs=(
            P(("chip", "core", "tensor"), None),
            P(DP, None),
            P(),
            P(),
            P(),
            P(),
            P(None, "tensor"),
            P(None, "tensor"),
            P(None, "tensor"),
            P("tensor", None),
            P(None, "tensor"),
            P(None, "tensor"),
            P("tensor", None),
            P(("chip", "core", "tensor"), None),
        ),
        out_specs=(
            P(("chip", "core", "tensor"), None),
            P(("chip", "core", "tensor"), None),
            P(),
            P(),
            P(),
            P(),
            P(DP, "tensor"),
            P(DP, "tensor"),
            P(DP, "tensor"),
            P("tensor", DP),
            P(DP, "tensor"),
            P(DP, "tensor"),
            P("tensor", DP),
        ),
        check_vma=False,
    )
```

time: 702 us -> 632 us (0.900)
  waiting for transfers between devices: 345 us -> 261 us
  Pallas kernels: 156 us -> 212 us
  matrix products: 44.1 us -> 0 us
  local copies, waits for them, and re-layouts: 37 us -> 25.5 us
  starting transfers between devices: 57.2 us -> 65.9 us
    pallas_call x3 -> x10, Pallas kernels: 25.1 us -> 82 us  [the longest x1 19.5 us: gate_up_grad(): call(rows_grad_kernel, pltpu.PrefetchScalarGridSpec(num_scalar_prefetch=0...]
    dot_general x7 -> x0, matrix products: 44.1 us -> none  [the longest x3 33.9 us: mm_tn(): return lax.dot_general(a, b, TN, preferred_element_type=F32)]
    ppermute x21 -> x24, starting transfers between devices: 19.5 us -> 49.2 us  [local(): lax.ppermute(v, 'tensor', [(i, (i + d) % n) for i in range(n)])]
    all_gather x1, waiting for transfers between devices: 31.3 us -> 3.27 us  [local(): piece = lax.all_gather(piece, 'tensor', axis=0, tiled=False)]
    ppermute x15 -> x20, waiting for transfers between devices: 72.2 us -> 45.9 us  [exchange(): return lax.ppermute(value, axis, [(i, i ^ step) for i in range(size)])]
    ppermute x6 -> x0, waiting for transfers between devices: 20.9 us -> none  [the longest x3 20.8 us: line_sum(): right = lax.ppermute(to_right, 'tensor', [(i, i + 1) for i in range(s)])]
    all_gather x1, waiting for transfers between devices: 19.7 us -> 0.01 us  [local(): grad_all = lax.all_gather(later_grad, 'tensor', axis=0, tiled=True)]
    ppermute x6 -> x0, starting transfers between devices: 16.9 us -> none  [the longest x3 13.3 us: line_sum(): right = lax.ppermute(to_right, 'tensor', [(i, i + 1) for i in range(s)])]
  transfers between devices with their start and end apart: 48 -> 48, of which waited for: 27 -> 24; matrix products, arithmetic and copies ran while one was open for 15% -> 7% of each run, Pallas kernels for 23% -> 34%
where the time goes in v2:
time: 632 us; the launch traced here: 623 us
  waiting for transfers between devices  261 us (41%)
  Pallas kernels  212 us (34%)
  starting transfers between devices  65.9 us (10%)
  other arithmetic  44 us (7%)
  local copies, waits for them, and re-layouts  25.5 us (4%)
  between operations  15.1 us (2%)
    ppermute x24, waiting for transfers between devices, local(): lax.ppermute(v, 'tensor', [(i, (i + d) % n) for i in range(n)])  211 us
    pallas_call x4, Pallas kernels, mlp_shard(): call(functools.partial(mlp_kernel, tiles), pltpu.PrefetchScalarGridSpec(n...  72.2 us
    ppermute x24, starting transfers between devices, local(): lax.ppermute(v, 'tensor', [(i, (i + d) % n) for i in range(n)])  49.2 us
    ppermute x20, waiting for transfers between devices, exchange(): return lax.ppermute(value, axis, [(i, i ^ step) for i in range(size)])  45.9 us
    pallas_call x4, Pallas kernels, qkv_shard(): call(functools.partial(qkv_kernel, heads, kv_heads, dim), pltpu.PrefetchS...  20.5 us
    pallas_call x1, Pallas kernels, gate_up_grad(): call(rows_grad_kernel, pltpu.PrefetchScalarGridSpec(num_scalar_prefetch=0...  19.5 us
    pallas_call x4, Pallas kernels, entry_shard(): call(entry_kernel, pltpu.PrefetchScalarGridSpec(num_scalar_prefetch=1, gr...  17.9 us
    ppermute x20, starting transfers between devices, exchange(): return lax.ppermute(value, axis, [(i, i ^ step) for i in range(size)])  16.3 us
  transfers between devices with their start and end apart: 48, of which 24 were waited for; matrix products, arithmetic and copies ran while one was open for 7% of the time, Pallas kernels for 34%

profile of v2, /device:TPU:0, one launch (start us, length us, event | category | flops | bytes accessed | tf_op | source)
XLA Modules:
  0.0 623.4 jit_solution(1375439421830031217)
XLA Ops:
  9.6 3.1 collective-permute-start
  19.0 33.0 %collective-permute-done.x_ref = bf16[256,2048]{1,0:T(8,128)(2,1)} collective-permute-done((bf16[256,2048]{1,0:T(8,128)(2,1)}, bf16[256,2048]{1,0:T(8,128)(2,1)}, u32[]{:S(2)}, u32[]{:S(2)}) %collective-permute-start) | collective-permute-done | bytes 1048608 | tf_op jit(solution)/shard_map/ppermute | solution.py:746
  52.1 3.3 all-gather.6.cloned.1.call-done
  60.6 5.1 shard_map.237
  65.7 5.1 shard_map.238
  75.0 7.5 %collective-permute-done.1.x_ref = bf16[256,2048]{1,0:T(8,128)(2,1)} collective-permute-done((bf16[256,2048]{1,0:T(8,128)(2,1)}, bf16[256,2048]{1,0:T(8,128)(2,1)}, u32[]{:S(2)}, u32[]{:S(2)}) %collective-permute-start.1) | collective-permute-done | bytes 1048608 | tf_op jit(solution)/shard_map/ppermute | solution.py:746
  85.5 5.1 shard_map.239
  90.7 16.4 %collective-permute-done.6 = bf16[2,4,256,256]{3,2,1,0:T(8,128)(2,1)} collective-permute-done((bf16[2,4,256,256]{3,2,1,0:T(8,128)(2,1)}, bf16[2,4,256,256]{3,2,1,0:T(8,128)(2,1)}, u32[]{:S(2)}, u32[]{:S(2)}) %collective-permute-start.6) | collective-permute-done | bytes 1048608 | tf_op jit(solution)/shard_map/ppermute | solution.py:617
  114.1 5.1 shard_map.240
  119.2 9.5 %shard_map.241 = (bf16[4,256,512]{2,1,0:T(8,128)(2,1)S(1)}, f32[4,1024]{1,0:T(4,128)S(1)}) custom-call(s32[1]{0:T(128)} %bitcast.z_ref, bf16[1024,1024]{1,0:T(8,128)(2,1)} %get-tuple-element.188.side_ref.refs_4_, s32[1,1024]{1,0:T(1,128)S(1)} %bitcast.123), custom_call_target="tpu_custom_call" | custom-call | flops 2147483 | bytes 5242 | tf_op jit(solution)/shard_map/pallas_call | solution.py:183
  128.9 3.7 collective-permute-start.9
  132.7 12.6 %collective-permute-done.7.refs_1_ = bf16[256,512]{1,0:T(8,128)(2,1)S(1)} collective-permute-done((bf16[256,512]{1,0:T(8,128)(2,1)S(1)}, bf16[256,512]{1,0:T(8,128)(2,1)S(1)}, u32[]{:S(2)}, u32[]{:S(2)}) %collective-permute-start.7) | collective-permute-done | bytes 262176 | tf_op jit(solution)/shard_map/ppermute | solution.py:746
  145.4 18.1 %collective-permute-done.8.refs_2_ = bf16[256,512]{1,0:T(8,128)(2,1)S(1)} collective-permute-done((bf16[256,512]{1,0:T(8,128)(2,1)S(1)}, bf16[256,512]{1,0:T(8,128)(2,1)S(1)}, u32[]{:S(2)}, u32[]{:S(2)}) %collective-permute-start.8) | collective-permute-done | bytes 262176 | tf_op jit(solution)/shard_map/ppermute | solution.py:746
  163.5 8.6 %shard_map.242 = (f32[256,2048]{1,0:T(8,128)}, bf16[256,2048]{1,0:T(8,128)(2,1)}) custom-call(s32[3]{0:T(128)S(1)} %pad_add_fusion.place_ref, bf16[256,512]{1,0:T(8,128)(2,1)S(1)} %get-tuple-element.194.refs_0_, bf16[256,512]{1,0:T(8,128)(2,1)S(1)} %collective-permute-done.7.refs_1_, bf16[256,512]{1,0:T(8,128)(2,1)S(1)} %collective-permute-done.8.refs_2_, ...), custom_call_target="tpu_custom_call" | custom-call | flops 2147483 | bytes 13631 | tf_op jit(solution)/shard_map/pallas_call | solution.py:308
  172.2 21.2 %collective-permute-start.11 = (bf16[256,2048]{1,0:T(8,128)(2,1)}, bf16[256,2048]{1,0:T(8,128)(2,1)S(1)}, u32[]{:S(2)}, u32[]{:S(2)}) collective-permute-start(bf16[256,2048]{1,0:T(8,128)(2,1)} %get-tuple-element.201.x_ref), channel_id=1, source_target_pairs={{0,1},{1,2},{2,3},{3,0},{4,5},{5,6},{6,7},{7,4},{8,9},{9,10},{10,1... | collective-permute-start | bytes 3145736 | tf_op jit(solution)/shard_map/ppermute | solution.py:746
  193.4 18.0 %shard_map.243 = (bf16[1024,1536]{1,0:T(8,128)(2,1)}, bf16[1024,1536]{1,0:T(8,128)(2,1)}, bf16[1024,1536]{1,0:T(8,128)(2,1)}, bf16[1024,2048]{1,0:T(8,128)(2,1)}...) custom-call(s32[1]{0:T(128)} %bitcast.14.sid_ref, bf16[256,2048]{1,0:T(8,128)(2,1)} %get-tuple-element.201.x_ref, ...), custom_call_target="tpu_custom_call" | custom-call | flops 9663676 | bytes 26476 | tf_op jit(solution)/shard_map/pallas_call | solution.py:388
  211.4 19.6 %collective-permute-done.11.x_ref = bf16[256,2048]{1,0:T(8,128)(2,1)S(1)} collective-permute-done((bf16[256,2048]{1,0:T(8,128)(2,1)}, bf16[256,2048]{1,0:T(8,128)(2,1)S(1)}, u32[]{:S(2)}, u32[]{:S(2)}) %collective-permute-start.11) | collective-permute-done | bytes 1048608 | tf_op jit(solution)/shard_map/ppermute | solution.py:746
  232.0 3.2 collective-permute-start.12
  235.2 23.8 %collective-permute-done.12.x_ref = bf16[256,2048]{1,0:T(8,128)(2,1)} collective-permute-done((bf16[256,2048]{1,0:T(8,128)(2,1)S(1)}, bf16[256,2048]{1,0:T(8,128)(2,1)}, u32[]{:S(2)}, u32[]{:S(2)}) %collective-permute-start.12) | collective-permute-done | bytes 1048608 | tf_op jit(solution)/shard_map/ppermute | solution.py:746
  260.1 18.0 %shard_map.244 = (bf16[1024,1536]{1,0:T(8,128)(2,1)}, bf16[1024,1536]{1,0:T(8,128)(2,1)}, bf16[1024,1536]{1,0:T(8,128)(2,1)}, bf16[1024,2048]{1,0:T(8,128)(2,1)}...) custom-call(s32[1]{0:T(128)} %bitcast.10.sid_ref, ...), custom_call_target="tpu_custom_call", output_to_operand_aliasing={{0}: (6, {}), {1}: (7, {}), {2}: (8, {}), {3}: (9, {})} | custom-call | flops 9663676 | bytes 26476 | tf_op jit(solution)/shard_map/pallas_call | solution.py:388
  279.1 18.1 %shard_map.245 = (bf16[1024,1536]{1,0:T(8,128)(2,1)}, bf16[1024,1536]{1,0:T(8,128)(2,1)}, bf16[1024,1536]{1,0:T(8,128)(2,1)}, bf16[1024,2048]{1,0:T(8,128)(2,1)}...) custom-call(s32[1]{0:T(128)} %bitcast.19.sid_ref, ...), custom_call_target="tpu_custom_call", output_to_operand_aliasing={{0}: (6, {}), {1}: (7, {}), {2}: (8, {}), {3}: (9, {})} | custom-call | flops 9663676 | bytes 26476 | tf_op jit(solution)/shard_map/pallas_call | solution.py:388
  300.8 18.0 %shard_map.246 = (bf16[1024,1536]{1,0:T(8,128)(2,1)}, bf16[1024,1536]{1,0:T(8,128)(2,1)}, bf16[1024,1536]{1,0:T(8,128)(2,1)}, bf16[1024,2048]{1,0:T(8,128)(2,1)}...) custom-call(s32[1]{0:T(128)} %bitcast.3.sid_ref, ...), custom_call_target="tpu_custom_call", output_to_operand_aliasing={{0}: (6, {}), {1}: (7, {}), {2}: (8, {}), {3}: (9, {})} | custom-call | flops 9663676 | bytes 26476 | tf_op jit(solution)/shard_map/pallas_call | solution.py:388
  319.8 4.1 collective-permute-done.14
  325.8 12.3 %shard_map.247 = bf16[8,1536,256]{2,1,0:T(8,128)(2,1)} custom-call(bf16[1024,1536]{1,0:T(8,128)(2,1)} %get-tuple-element.248.active_ref, bf16[1024,2048]{1,0:T(8,128)(2,1)} %all-gather.4.cloned.1.call-done.go_ref.grad_ref), custom_call_target="tpu_custom_call" | custom-call | flops 6442450 | bytes 13631 | tf_op jit(solution)/shard_map/pallas_call | solution.py:562
  338.1 12.0 %collective-permute-done.15 = bf16[256,2048]{1,0:T(8,128)(2,1)} collective-permute-done((bf16[256,2048]{1,0:T(8,128)(2,1)}, bf16[256,2048]{1,0:T(8,128)(2,1)}, u32[]{:S(2)}, u32[]{:S(2)}) %collective-permute-start.15) | collective-permute-done | bytes 1048608 | tf_op jit(solution)/shard_map/ppermute | solution.py:746
  353.2 19.5 %shard_map.248 = bf16[8,256,3072]{2,1,0:T(8,128)(2,1)} custom-call(bf16[1024,2048]{1,0:T(8,128)(2,1)} %get-tuple-element.252.x_ref, bf16[1024,1536]{1,0:T(8,128)(2,1)} %get-tuple-element.253.gate_ref, bf16[1024,1536]{1,0:T(8,128)(2,1)} %get-tuple-element.254.up_ref), custom_call_target="tpu_custom_call" | custom-call | flops 12884901 | bytes 23068 | tf_op jit(solution)/shard_map/pallas_call | solution.py:536
  372.6 5.8 collective-permute-done.17
  378.4 18.2 %collective-permute-done.16.refs_0_ = bf16[256,2048]{1,0:T(8,128)(2,1)} collective-permute-done((bf16[256,2048]{1,0:T(8,128)(2,1)}, bf16[256,2048]{1,0:T(8,128)(2,1)}, u32[]{:S(2)}, u32[]{:S(2)}) %collective-permute-start.16) | collective-permute-done | bytes 1048608 | tf_op jit(solution)/shard_map/ppermute | solution.py:746
  396.8 11.9 %shard_map.249 = (bf16[4,256,512]{2,1,0:T(8,128)(2,1)S(1)}, f32[256,2048]{1,0:T(8,128)}, bf16[256,2048]{1,0:T(8,128)(2,1)}, f32[1,2048]{1,0:T(1,128)S(1)}) custom-call(s32[3]{0:T(128)S(1)} %pad_add_fusion.place_ref, bf16[256,2048]{1,0:T(8,128)(2,1)} %get-tuple-element.245.own_part_ref, bf16[256,2048]{1,0:T(8,128)(2,1)} %go_ref.3, ...), custom_call_target="tpu_custom_call" | custom-call | flops 2147483 | bytes 18874 | tf_op jit(solution)/shard_map/pallas_call | solution.py:444
  408.9 3.7 collective-permute-start.20
  415.2 5.4 shard_map.250
  420.6 5.4 collective-permute-done.19.refs_2_
  426.7 5.4 collective-permute-start.22
  433.0 15.3 %shard_map.251 = (bf16[1024,1024]{1,0:T(8,128)(2,1)}, f32[8,128]{1,0:T(8,128)S(1)}) custom-call(s32[1]{0:T(128)} %bitcast.z_ref, bf16[256,512]{1,0:T(8,128)(2,1)S(1)} %get-tuple-element.260.refs_0_, bf16[256,512]{1,0:T(8,128)(2,1)S(1)} %collective-permute-done.18.refs_1_, bf16[256,512]{1,0:T(8,128)(2,1)S(1)} %collective-permute-done.19.refs_2_, ...), custom_call_target="tpu_custom_call" | custom-call | flops 5368709 | bytes 12582 | tf_op jit(solution)/shard_map/pallas_call | solution.py:262
  448.3 5.5 shard_map.252
  453.8 6.5 %shard_map.253 = bf16[4,4,512,256]{3,2,1,0:T(8,128)(2,1)} custom-call(s32[4]{0:T(128)S(1)} %get-tuple-element.315.place_ref, bf16[256,512]{1,0:T(8,128)(2,1)S(1)} %get-tuple-element.194.refs_0_, bf16[256,512]{1,0:T(8,128)(2,1)S(1)} %collective-permute-done.7.refs_1_, bf16[256,512]{1,0:T(8,128)(2,1)S(1)} %collective-permute-done.8.refs_2_, ...), custom_call_target="tpu_custom_call" | custom-call | flops 1073741 | bytes 4194 | tf_op jit(solution)/shard_map/pallas_call | solution.py:485
  474.3 4.1 shard_map.254
  478.4 6.5 %shard_map.256 = (bf16[4,256,1024]{2,1,0:T(8,128)(2,1)}, f32[4,256,128]{2,1,0:T(8,128)S(1)}) custom-call(s32[1]{0:T(128)} %bitcast.2.side_ref, bf16[1024,2048]{1,0:T(8,128)(2,1)} %get-tuple-element.274.entry_ref, bf16[1024,1024]{1,0:T(8,128)(2,1)} %get-tuple-element.294.grad_ref, bf16[2048,1024]{1,0:T(8,128)(2,1)} %pad_maximum_fusion.w_ref), custom_call_target="tpu_custom_call" | custom-call | flops 2147483 | bytes 14680 | tf_op jit(solution)/shard_map/pallas_call | solution.py:594
  485.0 6.5 %shard_map.255 = (bf16[4,256,1024]{2,1,0:T(8,128)(2,1)}, f32[4,256,128]{2,1,0:T(8,128)S(1)}) custom-call(s32[1]{0:T(128)S(6)} %sub.19.side_ref, bf16[1024,2048]{1,0:T(8,128)(2,1)} %get-tuple-element.274.entry_ref, bf16[1024,1024]{1,0:T(8,128)(2,1)} %get-tuple-element.294.grad_ref, bf16[2048,1024]{1,0:T(8,128)(2,1)} %pad_maximum_fusion.w_ref), custom_call_target="tpu_custom_call" | custom-call | flops 2147483 | bytes 14680 | tf_op jit(solution)/shard_map/pallas_call | solution.py:594
  491.5 6.8 %collective-permute-done.23 = bf16[256,2048]{1,0:T(8,128)(2,1)} collective-permute-done((bf16[256,2048]{1,0:T(8,128)(2,1)}, bf16[256,2048]{1,0:T(8,128)(2,1)}, u32[]{:S(2)}, u32[]{:S(2)}) %collective-permute-start.23) | collective-permute-done | bytes 1048608 | tf_op jit(solution)/shard_map/ppermute | solution.py:746
  500.8 6.0 collective-permute-done.25
  506.8 12.7 %collective-permute-done.24 = bf16[256,2048]{1,0:T(8,128)(2,1)} collective-permute-done((bf16[256,2048]{1,0:T(8,128)(2,1)}, bf16[256,2048]{1,0:T(8,128)(2,1)}, u32[]{:S(2)}, u32[]{:S(2)}) %collective-permute-start.24) | collective-permute-done | bytes 1048608 | tf_op jit(solution)/shard_map/ppermute | solution.py:746
  527.8 4.1 shard_map.257
  532.0 21.0 %collective-permute-done.32 = f32[1,4352]{1,0:T(1,128)S(1)} collective-permute-done((f32[1,4352]{1,0:T(1,128)S(1)}, f32[1,4352]{1,0:T(1,128)S(1)}, u32[]{:S(2)}, u32[]{:S(2)}) %collective-permute-start.32) | collective-permute-done | bytes 17440 | tf_op jit(solution)/shard_map/ppermute | solution.py:617
  567.7 4.1 shard_map.258
  571.9 20.6 %collective-permute-done.39 = bf16[512,256]{1,0:T(8,128)(2,1)S(1)} collective-permute-done((bf16[512,256]{1,0:T(8,128)(2,1)S(1)}, bf16[512,256]{1,0:T(8,128)(2,1)S(1)}, u32[]{:S(2)}, u32[]{:S(2)}) %collective-permute-start.39) | collective-permute-done | bytes 262176 | tf_op jit(solution)/shard_map/ppermute | solution.py:746
  594.9 7.7 %collective-permute-done.40 = bf16[512,256]{1,0:T(8,128)(2,1)S(1)} collective-permute-done((bf16[512,256]{1,0:T(8,128)(2,1)S(1)}, bf16[512,256]{1,0:T(8,128)(2,1)S(1)}, u32[]{:S(2)}, u32[]{:S(2)}) %collective-permute-start.40) | collective-permute-done | bytes 262176 | tf_op jit(solution)/shard_map/ppermute | solution.py:746
  604.4 3.4 fusion.29
  (221 shorter events, 97.5 us)
Async XLA Ops:
  7.2 48.1 %all-gather.6.cloned.1.call-start = ((), (), s32[]{:S(2)}) async-start(), calls=%async_computation.5 | async-start | bytes 1310720 | tf_op jit(solution)/shard_map/all_gather | solution.py:756
  9.5 249.4 %all-gather.4.cloned.1.call-start = ((), (), s32[]{:S(2)}) async-start(), calls=%async_computation.2 | async-start | bytes 5242880 | tf_op jit(solution)/shard_map/all_gather | solution.py:789
  9.6 42.5 %collective-permute-start = (bf16[256,2048]{1,0:T(8,128)(2,1)}, bf16[256,2048]{1,0:T(8,128)(2,1)}, u32[]{:S(2)}, u32[]{:S(2)}) collective-permute-start(bf16[256,2048]{1,0:T(8,128)(2,1)} %refs_6_.1), channel_id=1, source_target_pairs={{0,1},{1,2},{2,3},{3,0},{4,5},{5,6},{6,7},{7,4},{8,9},{9,10},{10,1... | collective-permute-start | bytes 3145736 | tf_op jit(solution)/shard_map/ppermute | solution.py:746
  55.3 27.2 %collective-permute-start.1 = (bf16[256,2048]{1,0:T(8,128)(2,1)}, bf16[256,2048]{1,0:T(8,128)(2,1)}, u32[]{:S(2)}, u32[]{:S(2)}) collective-permute-start(bf16[256,2048]{1,0:T(8,128)(2,1)} %collective-permute-done.x_ref), channel_id=1, source_target_pairs={{0,1},{1,2},{2,3},{3,0},{4,5},{5,6},{6,7},{7,4},{8,9},{9,10},{10,1... | collective-permute-start | bytes 3145736 | tf_op jit(solution)/shard_map/ppermute | solution.py:746
  57.5 13.9 %collective-permute-start.2 = (bf16[4,256,256]{2,1,0:T(8,128)(2,1)S(1)}, bf16[4,256,256]{2,1,0:T(8,128)(2,1)}, u32[]{:S(2)}, u32[]{:S(2)}) collective-permute-start(bf16[4,256,256]{2,1,0:T(8,128)(2,1)S(1)} %get-tuple-element.340), channel_id=1, source_target_pairs={{0,8},{4,12},{8,0},{12,4},{16,24},{20,28},{24,16},{28,20},{1,9},{5... | collective-permute-start | bytes 1572872 | tf_op jit(solution)/shard_map/ppermute | solution.py:617
  59.0 13.9 %collective-permute-start.3 = (bf16[4,256,256]{2,1,0:T(8,128)(2,1)}, bf16[4,256,256]{2,1,0:T(8,128)(2,1)}, u32[]{:S(2)}, u32[]{:S(2)}) collective-permute-start(bf16[4,256,256]{2,1,0:T(8,128)(2,1)} %get-tuple-element.339), channel_id=1, source_target_pairs={{0,16},{4,20},{8,24},{12,28},{16,0},{20,4},{24,8},{28,12},{1,17},{... | collective-permute-start | bytes 1572872 | tf_op jit(solution)/shard_map/ppermute | solution.py:617
  82.5 24.5 %collective-permute-start.6 = (bf16[2,4,256,256]{3,2,1,0:T(8,128)(2,1)}, bf16[2,4,256,256]{3,2,1,0:T(8,128)(2,1)}, u32[]{:S(2)}, u32[]{:S(2)}) collective-permute-start(bf16[2,4,256,256]{3,2,1,0:T(8,128)(2,1)} %pad_maximum_fusion.5), channel_id=1, source_target_pairs={{0,8},{4,12},{8,0},{12,4},{16,24},{20,28},{24,16},{28,20},{1,9},{5... | collective-permute-start | bytes 3145736 | tf_op jit(solution)/shard_map/ppermute | solution.py:617
  84.0 24.8 %collective-permute-start.5 = (bf16[2,4,256,256]{3,2,1,0:T(8,128)(2,1)S(1)}, bf16[2,4,256,256]{3,2,1,0:T(8,128)(2,1)}, u32[]{:S(2)}, u32[]{:S(2)}) collective-permute-start(bf16[2,4,256,256]{3,2,1,0:T(8,128)(2,1)S(1)} %pad_maximum_fusion.4), channel_id=1, source_target_pairs={{0,16},{4,20},{8,24},{12,28},{16,0},{20,4},{24,8},{28,12},{1,17},{... | collective-permute-start | bytes 3145736 | tf_op jit(solution)/shard_map/ppermute | solution.py:617
  85.5 25.8 %collective-permute-start.4 = (bf16[256,2048]{1,0:T(8,128)(2,1)}, bf16[256,2048]{1,0:T(8,128)(2,1)}, u32[]{:S(2)}, u32[]{:S(2)}) collective-permute-start(bf16[256,2048]{1,0:T(8,128)(2,1)} %collective-permute-done.1.x_ref), channel_id=1, source_target_pairs={{0,1},{1,2},{2,3},{3,0},{4,5},{5,6},{6,7},{7,4},{8,9},{9,10},{10,1... | collective-permute-start | bytes 3145736 | tf_op jit(solution)/shard_map/ppermute | solution.py:746
  113.8 49.8 %collective-permute-start.10 = (bf16[4,4,512,256]{3,2,1,0:T(8,128)(2,1)}, bf16[4,4,512,256]{3,2,1,0:T(8,128)(2,1)}, u32[]{:S(2)}, u32[]{:S(2)}) collective-permute-start(bf16[4,4,512,256]{3,2,1,0:T(8,128)(2,1)} %pad_maximum_fusion.1.refs_4_.own_ref), channel_id=1, source_target_pairs={{0,4},{4,0},{1,5},{5,1},{2,6},{6,2},{3,7},{7,3},{8,12},{12,8},{9,1... | collective-permute-start | bytes 12582920 | tf_op jit(solution)/shard_map/ppermute | solution.py:617
  113.8 489.5 %reduce-scatter.3.cloned.1.call-start = ((), (), s32[]{:S(2)}) async-start(), calls=%async_computation.3 | async-start | bytes 7077888 | tf_op jit(solution)/shard_map/reduce_scatter | solution.py:799
  128.8 16.6 %collective-permute-start.7 = (bf16[256,512]{1,0:T(8,128)(2,1)S(1)}, bf16[256,512]{1,0:T(8,128)(2,1)S(1)}, u32[]{:S(2)}, u32[]{:S(2)}) collective-permute-start(bf16[256,512]{1,0:T(8,128)(2,1)S(1)} %get-tuple-element.335), channel_id=1, source_target_pairs={{0,1},{1,2},{2,3},{3,0},{4,5},{5,6},{6,7},{7,4},{8,9},{9,10},{10,1... | collective-permute-start | bytes 786440 | tf_op jit(solution)/shard_map/ppermute | solution.py:746
  128.8 34.7 %collective-permute-start.8 = (bf16[256,512]{1,0:T(8,128)(2,1)S(1)}, bf16[256,512]{1,0:T(8,128)(2,1)S(1)}, u32[]{:S(2)}, u32[]{:S(2)}) collective-permute-start(bf16[256,512]{1,0:T(8,128)(2,1)S(1)} %get-tuple-element.334), channel_id=1, source_target_pairs={{0,2},{1,3},{2,0},{3,1},{4,6},{5,7},{6,4},{7,5},{8,10},{9,11},{10,... | collective-permute-start | bytes 786440 | tf_op jit(solution)/shard_map/ppermute | solution.py:746
  128.9 34.6 %collective-permute-start.9 = (bf16[256,512]{1,0:T(8,128)(2,1)S(1)}, bf16[256,512]{1,0:T(8,128)(2,1)S(1)}, u32[]{:S(2)}, u32[]{:S(2)}) collective-permute-start(bf16[256,512]{1,0:T(8,128)(2,1)S(1)} %get-tuple-element.333), channel_id=1, source_target_pairs={{0,3},{1,0},{2,1},{3,2},{4,7},{5,4},{6,5},{7,6},{8,11},{9,8},{10,9... | collective-permute-start | bytes 786440 | tf_op jit(solution)/shard_map/ppermute | solution.py:746
  172.2 58.9 %collective-permute-start.11 = (bf16[256,2048]{1,0:T(8,128)(2,1)}, bf16[256,2048]{1,0:T(8,128)(2,1)S(1)}, u32[]{:S(2)}, u32[]{:S(2)}) collective-permute-start(bf16[256,2048]{1,0:T(8,128)(2,1)} %get-tuple-element.201.x_ref), channel_id=1, source_target_pairs={{0,1},{1,2},{2,3},{3,0},{4,5},{5,6},{6,7},{7,4},{8,9},{9,10},{10,1... | collective-permute-start | bytes 3145736 | tf_op jit(solution)/shard_map/ppermute | solution.py:746
  232.0 26.9 %collective-permute-start.12 = (bf16[256,2048]{1,0:T(8,128)(2,1)S(1)}, bf16[256,2048]{1,0:T(8,128)(2,1)}, u32[]{:S(2)}, u32[]{:S(2)}) collective-permute-start(bf16[256,2048]{1,0:T(8,128)(2,1)S(1)} %collective-permute-done.11.x_ref), channel_id=1, source_target_pairs={{0,1},{1,2},{2,3},{3,0},{4,5},{5,6},{6,7},{7,4},{8,9},{9,10},{10,1... | collective-permute-start | bytes 3145736 | tf_op jit(solution)/shard_map/ppermute | solution.py:746
  259.0 39.3 %collective-permute-start.13 = (bf16[256,2048]{1,0:T(8,128)(2,1)}, bf16[256,2048]{1,0:T(8,128)(2,1)S(1)}, u32[]{:S(2)}, u32[]{:S(2)}) collective-permute-start(bf16[256,2048]{1,0:T(8,128)(2,1)} %collective-permute-done.12.x_ref), channel_id=1, source_target_pairs={{0,1},{1,2},{2,3},{3,0},{4,5},{5,6},{6,7},{7,4},{8,9},{9,10},{10,1... | collective-permute-start | bytes 3145736 | tf_op jit(solution)/shard_map/ppermute | solution.py:746
  298.2 25.7 %collective-permute-start.14 = (bf16[256,2048]{1,0:T(8,128)(2,1)S(1)}, bf16[256,2048]{1,0:T(8,128)(2,1)S(1)}, u32[]{:S(2)}, u32[]{:S(2)}) collective-permute-start(bf16[256,2048]{1,0:T(8,128)(2,1)S(1)} %copy-done.32), channel_id=1, source_target_pairs={{0,1},{1,2},{2,3},{3,0},{4,5},{5,6},{6,7},{7,4},{8,9},{9,10},{10,1... | collective-permute-start | bytes 3145736 | tf_op jit(solution)/shard_map/ppermute | solution.py:746
  325.3 24.8 %collective-permute-start.15 = (bf16[256,2048]{1,0:T(8,128)(2,1)}, bf16[256,2048]{1,0:T(8,128)(2,1)}, u32[]{:S(2)}, u32[]{:S(2)}) collective-permute-start(bf16[256,2048]{1,0:T(8,128)(2,1)} %add_convert_fusion.7), channel_id=1, source_target_pairs={{0,1},{1,2},{2,3},{3,0},{4,5},{5,6},{6,7},{7,4},{8,9},{9,10},{10,1... | collective-permute-start | bytes 3145736 | tf_op jit(solution)/shard_map/ppermute | solution.py:746
  350.1 253.2 %reduce-scatter.5.cloned.1.call-start = ((), (), s32[]{:S(2)}) async-start(), calls=%async_computation.4 | async-start | bytes 14155776 | tf_op jit(solution)/shard_map/reduce_scatter | solution.py:799
  350.2 28.3 %collective-permute-start.17 = (bf16[256,2048]{1,0:T(8,128)(2,1)}, bf16[256,2048]{1,0:T(8,128)(2,1)}, u32[]{:S(2)}, u32[]{:S(2)}) collective-permute-start(bf16[256,2048]{1,0:T(8,128)(2,1)} %copy-done.13), channel_id=1, source_target_pairs={{0,1},{1,2},{2,3},{3,0},{4,5},{5,6},{6,7},{7,4},{8,9},{9,10},{10,1... | collective-permute-start | bytes 3145736 | tf_op jit(solution)/shard_map/ppermute | solution.py:746
  353.2 43.5 %collective-permute-start.16 = (bf16[256,2048]{1,0:T(8,128)(2,1)}, bf16[256,2048]{1,0:T(8,128)(2,1)}, u32[]{:S(2)}, u32[]{:S(2)}) collective-permute-start(bf16[256,2048]{1,0:T(8,128)(2,1)} %add_convert_fusion.6), channel_id=1, source_target_pairs={{0,1},{1,2},{2,3},{3,0},{4,5},{5,6},{6,7},{7,4},{8,9},{9,10},{10,1... | collective-permute-start | bytes 3145736 | tf_op jit(solution)/shard_map/ppermute | solution.py:746
  408.7 11.8 %collective-permute-start.18 = (bf16[256,512]{1,0:T(8,128)(2,1)S(1)}, bf16[256,512]{1,0:T(8,128)(2,1)S(1)}, u32[]{:S(2)}, u32[]{:S(2)}) collective-permute-start(bf16[256,512]{1,0:T(8,128)(2,1)S(1)} %get-tuple-element.331), channel_id=1, source_target_pairs={{0,1},{1,2},{2,3},{3,0},{4,5},{5,6},{6,7},{7,4},{8,9},{9,10},{10,1... | collective-permute-start | bytes 786440 | tf_op jit(solution)/shard_map/ppermute | solution.py:746
  408.8 17.2 %collective-permute-start.19 = (bf16[256,512]{1,0:T(8,128)(2,1)S(1)}, bf16[256,512]{1,0:T(8,128)(2,1)S(1)}, u32[]{:S(2)}, u32[]{:S(2)}) collective-permute-start(bf16[256,512]{1,0:T(8,128)(2,1)S(1)} %get-tuple-element.330), channel_id=1, source_target_pairs={{0,2},{1,3},{2,0},{3,1},{4,6},{5,7},{6,4},{7,5},{8,10},{9,11},{10,... | collective-permute-start | bytes 786440 | tf_op jit(solution)/shard_map/ppermute | solution.py:746
  408.9 17.1 %collective-permute-start.20 = (bf16[256,512]{1,0:T(8,128)(2,1)S(1)}, bf16[256,512]{1,0:T(8,128)(2,1)S(1)}, u32[]{:S(2)}, u32[]{:S(2)}) collective-permute-start(bf16[256,512]{1,0:T(8,128)(2,1)S(1)} %get-tuple-element.329), channel_id=1, source_target_pairs={{0,3},{1,0},{2,1},{3,2},{4,7},{5,4},{6,5},{7,6},{8,11},{9,8},{10,9... | collective-permute-start | bytes 786440 | tf_op jit(solution)/shard_map/ppermute | solution.py:746
  426.7 27.1 %collective-permute-start.21 = (bf16[4,4,512,256]{3,2,1,0:T(8,128)(2,1)}, bf16[4,4,512,256]{3,2,1,0:T(8,128)(2,1)}, u32[]{:S(2)}, u32[]{:S(2)}) collective-permute-start(bf16[4,4,512,256]{3,2,1,0:T(8,128)(2,1)} %shard_map.250), channel_id=1, source_target_pairs={{0,4},{4,0},{1,5},{5,1},{2,6},{6,2},{3,7},{7,3},{8,12},{12,8},{9,1... | collective-permute-start | bytes 12582920 | tf_op jit(solution)/shard_map/ppermute | solution.py:617
  426.7 33.6 %collective-permute-start.22 = (bf16[256,2048]{1,0:T(8,128)(2,1)}, bf16[256,2048]{1,0:T(8,128)(2,1)}, u32[]{:S(2)}, u32[]{:S(2)}) collective-permute-start(bf16[256,2048]{1,0:T(8,128)(2,1)} %add_convert_fusion.5), channel_id=1, source_target_pairs={{0,1},{1,2},{2,3},{3,0},{4,5},{5,6},{6,7},{7,4},{8,9},{9,10},{10,1... | collective-permute-start | bytes 3145736 | tf_op jit(solution)/shard_map/ppermute | solution.py:746
  464.8 42.0 %collective-permute-start.25 = (bf16[2,4,512,128]{3,2,1,0:T(8,128)(2,1)}, bf16[2,4,512,128]{3,2,1,0:T(8,128)(2,1)}, u32[]{:S(2)}, u32[]{:S(2)}) collective-permute-start(bf16[2,4,512,128]{3,2,1,0:T(8,128)(2,1)} %get-tuple-element.323), channel_id=1, source_target_pairs={{0,8},{4,12},{8,0},{12,4},{16,24},{20,28},{24,16},{28,20},{1,9},{5... | collective-permute-start | bytes 3145736 | tf_op jit(solution)/shard_map/ppermute | solution.py:617
  468.5 38.3 %collective-permute-start.26 = (bf16[2,4,512,128]{3,2,1,0:T(8,128)(2,1)}, bf16[2,4,512,128]{3,2,1,0:T(8,128)(2,1)}, u32[]{:S(2)}, u32[]{:S(2)}) collective-permute-start(bf16[2,4,512,128]{3,2,1,0:T(8,128)(2,1)} %get-tuple-element.321), channel_id=1, source_target_pairs={{0,16},{4,20},{8,24},{12,28},{16,0},{20,4},{24,8},{28,12},{1,17},{... | collective-permute-start | bytes 3145736 | tf_op jit(solution)/shard_map/ppermute | solution.py:617
  470.1 28.2 %collective-permute-start.23 = (bf16[256,2048]{1,0:T(8,128)(2,1)}, bf16[256,2048]{1,0:T(8,128)(2,1)}, u32[]{:S(2)}, u32[]{:S(2)}) collective-permute-start(bf16[256,2048]{1,0:T(8,128)(2,1)} %shard_map.252), channel_id=1, source_target_pairs={{0,1},{1,2},{2,3},{3,0},{4,5},{5,6},{6,7},{7,4},{8,9},{9,10},{10,1... | collective-permute-start | bytes 3145736 | tf_op jit(solution)/shard_map/ppermute | solution.py:746
  473.2 46.4 %collective-permute-start.24 = (bf16[256,2048]{1,0:T(8,128)(2,1)}, bf16[256,2048]{1,0:T(8,128)(2,1)}, u32[]{:S(2)}, u32[]{:S(2)}) collective-permute-start(bf16[256,2048]{1,0:T(8,128)(2,1)} %add_convert_fusion.3), channel_id=1, source_target_pairs={{0,1},{1,2},{2,3},{3,0},{4,5},{5,6},{6,7},{7,4},{8,9},{9,10},{10,1... | collective-permute-start | bytes 3145736 | tf_op jit(solution)/shard_map/ppermute | solution.py:746
  520.1 6.7 %collective-permute-start.31 = (f32[1,4352]{1,0:T(1,128)S(1)}, f32[1,4352]{1,0:T(1,128)S(1)}, u32[]{:S(2)}, u32[]{:S(2)}) collective-permute-start(f32[1,4352]{1,0:T(1,128)S(1)} %broadcast_in_dim.50), channel_id=1, source_target_pairs={{0,1},{1,0},{2,3},{3,2},{4,5},{5,4},{6,7},{7,6},{8,9},{9,8},{10,11... | collective-permute-start | bytes 52232 | tf_op jit(solution)/shard_map/ppermute | solution.py:617
  520.2 33.2 %collective-permute-start.30 = (bf16[4,256,1024]{2,1,0:T(8,128)(2,1)}, bf16[4,256,1024]{2,1,0:T(8,128)(2,1)S(1)}, u32[]{:S(2)}, u32[]{:S(2)}) collective-permute-start(bf16[4,256,1024]{2,1,0:T(8,128)(2,1)} %get-tuple-element.286), channel_id=1, source_target_pairs={{0,4},{4,0},{1,5},{5,1},{2,6},{6,2},{3,7},{7,3},{8,12},{12,8},{9,1... | collective-permute-start | bytes 6291464 | tf_op jit(solution)/shard_map/ppermute | solution.py:617
  524.9 28.1 %collective-permute-start.27 = (bf16[256,2048]{1,0:T(8,128)(2,1)S(1)}, bf16[256,2048]{1,0:T(8,128)(2,1)S(1)}, u32[]{:S(2)}, u32[]{:S(2)}) collective-permute-start(bf16[256,2048]{1,0:T(8,128)(2,1)S(1)} %copy-done.23), channel_id=1, source_target_pairs={{0,1},{1,2},{2,3},{3,0},{4,5},{5,6},{6,7},{7,4},{8,9},{9,10},{10,1... | collective-permute-start | bytes 3145736 | tf_op jit(solution)/shard_map/ppermute | solution.py:746
  526.8 26.2 %collective-permute-start.32 = (f32[1,4352]{1,0:T(1,128)S(1)}, f32[1,4352]{1,0:T(1,128)S(1)}, u32[]{:S(2)}, u32[]{:S(2)}) collective-permute-start(f32[1,4352]{1,0:T(1,128)S(1)} %reshape_add_fusion), channel_id=1, source_target_pairs={{0,2},{1,3},{2,0},{3,1},{4,6},{5,7},{6,4},{7,5},{8,10},{9,11},{10,... | collective-permute-start | bytes 52232 | tf_op jit(solution)/shard_map/ppermute | solution.py:617
  527.0 26.4 %collective-permute-start.29 = (bf16[4,512,128]{2,1,0:T(8,128)(2,1)S(1)}, bf16[4,512,128]{2,1,0:T(8,128)(2,1)S(1)}, u32[]{:S(2)}, u32[]{:S(2)}) collective-permute-start(bf16[4,512,128]{2,1,0:T(8,128)(2,1)S(1)} %fusion.9), channel_id=1, source_target_pairs={{0,8},{4,12},{8,0},{12,4},{16,24},{20,28},{24,16},{28,20},{1,9},{5... | collective-permute-start | bytes 1572872 | tf_op jit(solution)/shard_map/ppermute | solution.py:617
  527.5 25.9 %collective-permute-start.28 = (bf16[4,512,128]{2,1,0:T(8,128)(2,1)S(1)}, bf16[4,512,128]{2,1,0:T(8,128)(2,1)S(1)}, u32[]{:S(2)}, u32[]{:S(2)}) collective-permute-start(bf16[4,512,128]{2,1,0:T(8,128)(2,1)S(1)} %fusion.8), channel_id=1, source_target_pairs={{0,16},{4,20},{8,24},{12,28},{16,0},{20,4},{24,8},{28,12},{1,17},{... | collective-permute-start | bytes 1572872 | tf_op jit(solution)/shard_map/ppermute | solution.py:617
  553.4 3.6 collective-permute-start.41
  553.8 11.0 %collective-permute-start.38 = (bf16[512,256]{1,0:T(8,128)(2,1)S(1)}, bf16[512,256]{1,0:T(8,128)(2,1)S(1)}, u32[]{:S(2)}, u32[]{:S(2)}) collective-permute-start(bf16[512,256]{1,0:T(8,128)(2,1)S(1)} %get-tuple-element.327), channel_id=1, source_target_pairs={{0,1},{1,2},{2,3},{3,0},{4,5},{5,6},{6,7},{7,4},{8,9},{9,10},{10,1... | collective-permute-start | bytes 786440 | tf_op jit(solution)/shard_map/ppermute | solution.py:746
  556.5 36.4 %collective-permute-start.35 = (bf16[2,256,512]{2,1,0:T(8,128)(2,1)S(1)}, bf16[2,256,512]{2,1,0:T(8,128)(2,1)S(1)}, u32[]{:S(2)}, u32[]{:S(2)}) collective-permute-start(bf16[2,256,512]{2,1,0:T(8,128)(2,1)S(1)} %dynamic-slice_bitcast_fusion.7), channel_id=1, source_target_pairs={{0,16},{4,20},{8,24},{12,28},{16,0},{20,4},{24,8},{28,12},{1,17},{... | collective-permute-start | bytes 1572872 | tf_op jit(solution)/shard_map/ppermute | solution.py:617
  557.0 4.0 collective-permute-start.42
  557.4 36.2 %collective-permute-start.34 = (bf16[2,256,512]{2,1,0:T(8,128)(2,1)S(1)}, bf16[2,256,512]{2,1,0:T(8,128)(2,1)S(1)}, u32[]{:S(2)}, u32[]{:S(2)}) collective-permute-start(bf16[2,256,512]{2,1,0:T(8,128)(2,1)S(1)} %dynamic-slice_bitcast_fusion.9), channel_id=1, source_target_pairs={{0,8},{4,12},{8,0},{12,4},{16,24},{20,28},{24,16},{28,20},{1,9},{5... | collective-permute-start | bytes 1572872 | tf_op jit(solution)/shard_map/ppermute | solution.py:617
  559.2 35.2 %collective-permute-start.33 = (bf16[256,2048]{1,0:T(8,128)(2,1)S(1)}, bf16[256,2048]{1,0:T(8,128)(2,1)S(1)}, u32[]{:S(2)}, u32[]{:S(2)}) collective-permute-start(bf16[256,2048]{1,0:T(8,128)(2,1)S(1)} %add_convert_fusion.2), channel_id=1, source_target_pairs={{0,1},{1,2},{2,3},{3,0},{4,5},{5,6},{6,7},{7,4},{8,9},{9,10},{10,1... | collective-permute-start | bytes 3145736 | tf_op jit(solution)/shard_map/ppermute | solution.py:746
  561.0 10.8 %collective-permute-start.43 = (f32[1,4352]{1,0:T(1,128)S(1)}, f32[1,4352]{1,0:T(1,128)S(1)}, u32[]{:S(2)}, u32[]{:S(2)}) collective-permute-start(f32[1,4352]{1,0:T(1,128)S(1)} %add.225), channel_id=1, source_target_pairs={{0,16},{4,20},{8,24},{12,28},{16,0},{20,4},{24,8},{28,12},{1,17},{... | collective-permute-start | bytes 52232 | tf_op jit(solution)/shard_map/ppermute | solution.py:617
  564.9 27.6 %collective-permute-start.39 = (bf16[512,256]{1,0:T(8,128)(2,1)S(1)}, bf16[512,256]{1,0:T(8,128)(2,1)S(1)}, u32[]{:S(2)}, u32[]{:S(2)}) collective-permute-start(bf16[512,256]{1,0:T(8,128)(2,1)S(1)} %fusion.11), channel_id=1, source_target_pairs={{0,1},{1,2},{2,3},{3,0},{4,5},{5,6},{6,7},{7,4},{8,9},{9,10},{10,1... | collective-permute-start | bytes 786440 | tf_op jit(solution)/shard_map/ppermute | solution.py:746
  592.5 10.0 %collective-permute-start.40 = (bf16[512,256]{1,0:T(8,128)(2,1)S(1)}, bf16[512,256]{1,0:T(8,128)(2,1)S(1)}, u32[]{:S(2)}, u32[]{:S(2)}) collective-permute-start(bf16[512,256]{1,0:T(8,128)(2,1)S(1)} %fusion.10), channel_id=1, source_target_pairs={{0,1},{1,2},{2,3},{3,0},{4,5},{5,6},{6,7},{7,4},{8,9},{9,10},{10,1... | collective-permute-start | bytes 786440 | tf_op jit(solution)/shard_map/ppermute | solution.py:746
  593.1 9.5 %collective-permute-start.37 = (bf16[256,512]{1,0:T(8,128)(2,1)S(1)}, bf16[256,512]{1,0:T(8,128)(2,1)}, u32[]{:S(2)}, u32[]{:S(2)}) collective-permute-start(bf16[256,512]{1,0:T(8,128)(2,1)S(1)} %fusion.13), channel_id=1, source_target_pairs={{0,8},{4,12},{8,0},{12,4},{16,24},{20,28},{24,16},{28,20},{1,9},{5... | collective-permute-start | bytes 786440 | tf_op jit(solution)/shard_map/ppermute | solution.py:617
  593.9 9.4 %collective-permute-start.36 = (bf16[256,512]{1,0:T(8,128)(2,1)S(1)}, bf16[256,512]{1,0:T(8,128)(2,1)}, u32[]{:S(2)}, u32[]{:S(2)}) collective-permute-start(bf16[256,512]{1,0:T(8,128)(2,1)S(1)} %fusion.12), channel_id=1, source_target_pairs={{0,16},{4,20},{8,24},{12,28},{16,0},{20,4},{24,8},{28,12},{1,17},{... | collective-permute-start | bytes 786440 | tf_op jit(solution)/shard_map/ppermute | solution.py:617
  (33 other events, 385.7 us)
Sparse Core Ops, SparseCore 0:
  10.2 45.1 all-gather.5
  113.9 122.6 all-gather.3
  350.2 61.3 reduce-scatter.2
  415.4 114.7 reduce-scatter.4

commit v3 on v2

--- a/solution.py
+++ b/solution.py
@@ -466,33 +466,47 @@
     )(place, own, go, hidden, gain, w_own, w_other, *got)
 
 
-def out_weight_kernel(n, place_ref, *refs):
-    mixed_refs, mid_ref, out_ref = refs[:n], refs[n], refs[-1]
+def out_weight_kernel(n, count, place_ref, *refs):
+    mixed_refs, mid_ref, out_refs = refs[:n], refs[n], refs[len(refs) - count * count :]
+    cols = mid_ref.shape[1] // count
     for s in range(n):
+        grad = mm_tn(mixed_refs[s][...], mid_ref[...])
         t = lax.rem(place_ref[0] - s + n, n)
-        grad = mm_tn(mixed_refs[s][...], mid_ref[...])
-        if len(refs) > n + 2:
-            grad = grad + refs[n + 1][0, t].astype(F32)
-        out_ref[0, t] = grad.astype(BF16)
+        if count == 1:
+            out_refs[0][0, t] = grad.astype(BF16)
+            continue
+        grad = (grad + refs[n + 1][0, t].astype(F32)).astype(BF16)
+        for piece in range(count):
+            rows = n // count
+
+            @pl.when((t >= piece * rows) & (t < (piece + 1) * rows))
+            def _(piece=piece, rows=rows, grad=grad, t=t):
+                for half in range(count):
+                    out_refs[count * piece + half][0, t - piece * rows] = grad[
+                        :, half * cols : (half + 1) * cols
+                    ]
 
 
 def out_weight_grad(place, side, mixed, mid, n, chips, got):
     rows, width = mid.shape
     cols = mixed[0].shape[1]
     own = width // (2 * chips)
-    block = pl.BlockSpec((1, n, cols, own), lambda c, place: (c, 0, 0, 0))
+    count = 1 if got is None else 2
+    block = lambda count: pl.BlockSpec(
+        (1, n // count, cols, own // count), lambda c, place: (c, 0, 0, 0)
+    )
     extra = [] if got is None else [got]
     return call(
-        functools.partial(out_weight_kernel, n),
+        functools.partial(out_weight_kernel, n, count),
         pltpu.PrefetchScalarGridSpec(
             num_scalar_prefetch=1,
             grid=(chips,),
             in_specs=[pl.BlockSpec((rows, cols), lambda c, place: (0, 0))] * n
             + [pl.BlockSpec((rows, own), lambda c, place: (0, 2 * c + place[3]))]
-            + [block] * len(extra),
-            out_specs=block,
-        ),
-        shape((chips, n, cols, own), BF16),
+            + [block(1)] * len(extra),
+            out_specs=[block(count)] * count**2,
+        ),
+        [shape((chips, n // count, cols, own // count), BF16)] * count**2,
         rows * width * cols * n,
         n * cols * width,
     )(jnp.concatenate([place, side]), *mixed, mid, *extra)
@@ -522,58 +536,34 @@
     )(sid, grads, w_qkv)
 
 
-def rows_grad_kernel(x_ref, gate_ref, up_ref, out_ref):
-    units = gate_ref.shape[1]
-    for j, ref in enumerate((gate_ref, up_ref)):
+def rows_grad_kernel(count, x_ref, *refs):
+    out_ref = refs[-1]
+    units = refs[0].shape[1]
+    for j, ref in enumerate(refs[:count]):
         out_ref[0, :, j * units : (j + 1) * units] = mm_tn(x_ref[...], ref[...]).astype(BF16)
 
 
-def gate_up_grad(x, gate_grad, up_grad, batches):
+def rows_grad(x, factors, place, batches, kept):
     block_rows, width = x.shape
-    units = gate_grad.shape[1]
+    units = factors[0].shape[1]
     rows = width // batches
-    whole = lambda j: (0, 0)
+    count = len(factors)
+    extra = [] if kept is None else [kept]
     return call(
-        rows_grad_kernel,
+        functools.partial(rows_grad_kernel, count),
         pltpu.PrefetchScalarGridSpec(
             num_scalar_prefetch=0,
             grid=(batches,),
-            in_specs=[
-                pl.BlockSpec((block_rows, rows), lambda j: (0, j)),
-                pl.BlockSpec((block_rows, units), whole),
-                pl.BlockSpec((block_rows, units), whole),
-            ],
-            out_specs=pl.BlockSpec((1, rows, 2 * units), lambda j: (j, 0, 0)),
-        ),
-        shape((batches, rows, 2 * units), BF16),
-        4 * block_rows * width * units,
-        2 * (block_rows * width + 2 * block_rows * units + 2 * width * units),
-    )(x, gate_grad, up_grad)
-
-
-def cols_grad_kernel(active_ref, grad_ref, out_ref):
-    out_ref[0] = mm_tn(active_ref[...], grad_ref[...]).astype(BF16)
-
-
-def down_grad(active, grad_all, batches):
-    block_rows, units = active.shape
-    width = grad_all.shape[1]
-    cols = width // batches
-    return call(
-        cols_grad_kernel,
-        pltpu.PrefetchScalarGridSpec(
-            num_scalar_prefetch=0,
-            grid=(batches,),
-            in_specs=[
-                pl.BlockSpec((block_rows, units), lambda j: (0, 0)),
-                pl.BlockSpec((block_rows, cols), lambda j: (0, j)),
-            ],
-            out_specs=pl.BlockSpec((1, units, cols), lambda j: (j, 0, 0)),
-        ),
-        shape((batches, units, cols), BF16),
-        2 * block_rows * width * units,
-        2 * (block_rows * units + block_rows * width + width * units),
-    )(active, grad_all)
+            in_specs=[pl.BlockSpec((block_rows, rows), lambda j: (0, j))]
+            + [pl.BlockSpec((block_rows, units), lambda j: (0, 0))] * count
+            + [pl.BlockSpec(memory_space=pl.ANY)] * len(extra),
+            out_specs=pl.BlockSpec((1, rows, count * units), lambda j: (j, 0, place)),
+        ),
+        shape((batches, rows, 3 * units), BF16),
+        2 * block_rows * width * units * count,
+        2 * (block_rows * width + count * (block_rows + width) * units),
+        {1 + count: 0} if extra else None,
+    )(x, *factors, *extra)
 
 
 def qkv_weight_kernel(side_ref, entry_ref, grad_ref, w_ref, out_ref, part_ref):
@@ -675,12 +665,10 @@
     return kept, exchange(sent, DP, 1 << bit), axes[:at] + axes[at + 1 :]
 
 
-def halves_of(value):
-    bits = value.shape[0].bit_length() - 1
-    value = value.reshape((2,) * bits + value.shape[1:])
+def halves_of(first, second):
+    bits = first.shape[0].bit_length() - 1
     axes = tuple(range(1, bits + 1))[::-1]
-    middle = value.shape[-1] // 2
-    return Halves((value[..., :middle], value[..., middle:]), (axes, axes))
+    return Halves([v.reshape((2,) * bits + v.shape[1:]) for v in (first, second)], (axes, axes))
 
 
 def join(*values):
@@ -795,128 +783,136 @@
     hidden, mlp_entry = out_projection(place, mixed, w_own, w_other, tokens, gain_two, n)
 
     weights = (w_gate, w_up, w_down)
-    down_sum, inner_sum = RingSum(shift), RingSum(shift)
+    inner_sum = RingSum(shift)
+    down_one, down_two, down_parts = RingSum(shift), RingSum(shift), []
     over_dp = lambda g: lax.psum_scatter(g, DP, scatter_dimension=0, tiled=False)
     blocks, kept = [mlp_entry], None
     for t in range(2 * n - 2):
         if t < n - 1:
             blocks.append(shift(blocks[t]))
+        if t >= n - 1:
+            inner_sum.hop()
+        s = (0, -1)[t] if t < 2 else t - 1
+        if 0 <= s < n:
+            kept, down, inner = mlp_shard(
+                shard_of(s), blocks[s], grad_all if s else out_grad, weights, kept, block_rows
+            )
+            down_parts.append(down)
+            inner_sum.parts.append(inner)
+        if s >= n:
+            down_one.parts = [part[:, : width // 2] for part in down_parts]
+            down_two.parts = [part[:, width // 2 :] for part in down_parts]
+            down_one.hop()
+            mlp_grads = rows_grad(grad_all, [active], 2, batches, None)
+            mlp_grads = rows_grad(mlp_all, [gate_grad, up_grad], 0, batches, mlp_grads)
+            inner_sum.moving, down_one.moving, mlp_grads = join(
+                inner_sum.moving, down_one.moving, mlp_grads
+            )
+            mlp_grads = over_dp(mlp_grads)
         else:
-            inner_sum.hop()
-        for s in {0: (0,), 1: (), 2: (1, 2)}.get(t, (t,)):
-            if s < n:
-                kept, down, inner = mlp_shard(
-                    shard_of(s), blocks[s], grad_all if s else out_grad, weights, kept, block_rows
-                )
-                down_sum.parts.append(down)
-                inner_sum.parts.append(inner)
-        if t == 1:
-            blocks, kept, grad_all = join(blocks, kept, grad_all)
-        elif t == 2 * n - 4:
-            w_down_grad = down_grad(active, grad_all, batches)
-            inner_sum.moving, w_down_grad = join(inner_sum.moving, w_down_grad)
-            w_down_grad = over_dp(w_down_grad)
-        elif t == 2 * n - 3:
-            down_sum.hop()
-            w_gate_up_grad = gate_up_grad(mlp_all, gate_grad, up_grad, batches)
-            inner_sum.moving, down_sum.moving, w_gate_up_grad = join(
-                inner_sum.moving, down_sum.moving, w_gate_up_grad
-            )
-            w_gate_up_grad = over_dp(w_gate_up_grad)
-        else:
-            blocks, kept, inner_sum.parts, inner_sum.moving = join(
-                blocks, kept, inner_sum.parts, inner_sum.moving
-            )
+            state = (blocks, kept, inner_sum.parts, inner_sum.moving)
+            state, grad_all = join(state, grad_all) if t else (join(*state), grad_all)
+            blocks, kept, inner_sum.parts, inner_sum.moving = state
             active, gate_grad, up_grad, mlp_all = kept
 
+    down_two.hop()
     gm, grad_hidden, grad_mid, mlp_part = mid_stage(
         place, inner_sum.parts[0], (inner_sum.moving,), out_grad, hidden, gain_two, w_own, w_other, n
     )
+    gm, grad_mid, down_two.moving = join(gm, grad_mid, down_two.moving)
 
     gm = [gm[0]] + [shift(gm[d], d) for d in range(1, n)]
-    got = out_weight_grad(place, 1 - core, mixed, grad_mid, n, chips, None)
-    down_sum.add()
-    gm, got, down_sum.moving = join(gm, got, down_sum.moving)
-
-    down_sum.send()
+    (got,) = out_weight_grad(place, 1 - core, mixed, grad_mid, n, chips, None)
+    down_one.add()
+    down_two.add()
+    gm, got, down_one.moving, down_two.moving = join(gm, got, down_one.moving, down_two.moving)
+
+    down_one.send()
     got = exchange(got, "core", 1)
     grads, gain_parts = attention_backward(
         zs, gm, side, raw, lse, start, cosine, sine, qg, kg, heads, kv_heads, dim
     )
-
+    grads, got, down_one.moving = join(grads, got, down_one.moving)
+    down_two.send()
+    down_one.hop()
     entry_part = lambda s: entry_shard(shard_of(s), grads, w_qkv, rows)
     entry_sum = RingSum(shift)
     entry_sum.parts = [None, entry_part(1)] + [None] * (n - 2)
     w_out_grad = out_weight_grad(place, core, mixed, grad_mid, n, chips, got)
-    entry_sum.parts[1], grads, w_out_grad, down_sum.moving = join(
-        entry_sum.parts[1], grads, w_out_grad, down_sum.moving
-    )
-
-    down_sum.add()
-    out_halves = halves_of(w_out_grad)
+    entry_sum.parts[1], grads, w_out_grad, down_one.moving, down_two.moving = join(
+        entry_sum.parts[1], grads, w_out_grad, down_one.moving, down_two.moving
+    )
+
+    out_one, out_two = halves_of(*w_out_grad[:2]), halves_of(*w_out_grad[2:])
     entry_sum.add()
 
     entry_sum.send()
-    down_sum.send()
-    out_halves, out_got = out_halves.send(0, batches)
+    down_two.hop()
+    out_one, one_got = out_one.send(0, batches)
     qkv_sent, lanes_sent = qkv_weight_grad(1 - core, entry_all, grads, w_qkv, chips)
     w_qkv_grad, lanes = qkv_weight_grad(core, entry_all, grads, w_qkv, chips)
     entry_sum.parts[2 % n] = entry_part(2 % n)
     entry_sum.add()
-    state = (entry_sum.moving, down_sum.moving, out_halves, out_got, qkv_sent, w_qkv_grad)
-    state, grads, lanes, lanes_sent = join(state, grads, lanes, lanes_sent)
-    entry_sum.moving, down_sum.moving, out_halves, out_got, qkv_sent, w_qkv_grad = state
+    state = (entry_sum.moving, down_two.moving, qkv_sent, w_qkv_grad)
+    state, grads, lanes, lanes_sent, out_one, one_got, out_two = join(
+        state, grads, lanes, lanes_sent, out_one, one_got, out_two
+    )
+    entry_sum.moving, down_two.moving, qkv_sent, w_qkv_grad = state
     lanes, lanes_sent = jnp.sum(lanes, axis=2), jnp.sum(lanes_sent, axis=2)
     lanes = jnp.where(core[0] == 0, jnp.stack([lanes, lanes_sent], 1), jnp.stack([lanes_sent, lanes], 1))
     attn_part = lanes.reshape(width) / attn_gain
     totals = jnp.concatenate([attn_part, mlp_part[0], gain_parts[0], gain_parts[1]])[None, :]
 
     entry_sum.send()
-    down_sum.add()
-    down_sum.send()
-    out_halves = out_halves.add(out_got)
-    if steps > 1:
-        out_halves, out_got = out_halves.send(1, batches)
+    out_two, two_got = out_two.send(0, batches)
     qkv_got = exchange(qkv_sent, "core", 1)
-    totals = total_over(totals, "tensor")
+    totals = total_over(totals, DP)
     entry_sum.parts[3 % n] = entry_part(3 % n)
     entry_sum.add()
-    state = (entry_sum.moving, down_sum.moving, out_halves, out_got, qkv_got, w_qkv_grad)
-    state, grads, totals = join(state, grads, totals)
-    entry_sum.moving, down_sum.moving, out_halves, out_got, qkv_got, w_qkv_grad = state
-
-    if steps > 1:
-        out_halves = out_halves.add(out_got)
-    for step in range(2, steps):
+    while down_one.step < n - 1:
+        down_one.hop()
+        down_two.hop()
+    moved = jnp.concatenate([down_one.moving, down_two.moving], axis=1)
+    output = total_of(hidden, [down_parts[0], moved]).astype(BF16)
+    state = (entry_sum.moving, out_one, one_got, out_two, two_got, qkv_got, w_qkv_grad)
+    state, grads, totals, output = join(state, grads, totals, output)
+    entry_sum.moving, out_one, one_got, out_two, two_got, qkv_got, w_qkv_grad = state
+
+    out_one, out_two = out_one.add(one_got), out_two.add(two_got)
+    values = [jnp.concatenate(pair, axis=-3) for pair in zip(out_one.values, out_two.values)]
+    out_halves = Halves(values, out_one.axes)
+    for step in range(1, steps):
         out_halves, out_got = out_halves.send(step, batches)
+        out_got, w_qkv_grad, qkv_got = join(out_got, w_qkv_grad, qkv_got)
         out_halves = out_halves.add(out_got)
     w_out_grad = jnp.concatenate(out_halves.values, axis=-1).astype(BF16)
     out_sum = RingSum(shift)
     out_sum.parts = [lax.dynamic_index_in_dim(w_out_grad, shard_of(d)[0], 0, False) for d in range(n)]
     for _ in range(n - 1):
         out_sum.hop()
-    qkv_halves = halves_of(add_low(w_qkv_grad, qkv_got))
+    middle = w_qkv_grad.shape[-1] // 2
+    qkv_halves = halves_of(
+        add_low(w_qkv_grad[..., :middle], qkv_got[..., :middle]),
+        add_low(w_qkv_grad[..., middle:], qkv_got[..., middle:]),
+    )
     for step in range(steps):
         qkv_halves, qkv_got = qkv_halves.send(step, batches)
         if step < steps - 1:
             qkv_halves = qkv_halves.add(qkv_got)
-    totals = total_over(totals, DP)
+    totals = total_over(totals, "tensor")
     for s in range(3, n):
         entry_sum.send()
-        down_sum.add()
-        down_sum.send()
         entry_sum.parts[(s + 1) % n] = entry_part((s + 1) % n)
         if s < n - 1:
             entry_sum.add()
-            entry_sum.moving, down_sum.moving, grads = join(entry_sum.moving, down_sum.moving, grads)
-    grad_entry = total_of(entry_sum.parts[0], [entry_sum.moving]).astype(F32)
-    state = (grad_entry, qkv_halves, qkv_got, out_sum.parts[0], out_sum.moving)
-    (grad_entry, qkv_halves, qkv_got, own, moved), w_down_grad, w_gate_up_grad, totals = join(
-        state, w_down_grad, w_gate_up_grad, totals
-    )
-    w_out_grad = total_of(own, [moved])
+            entry_sum.moving, grads = join(entry_sum.moving, grads)
+    grad_entry = total_of(entry_sum.parts[0], [entry_sum.moving])
+    units = w_gate.shape[1]
+    mlp_grads = mlp_grads.astype(F32)
+    mlp_grads = mlp_grads[:, :units], mlp_grads[:, units : 2 * units], mlp_grads[:, 2 * units :].T
+    out_sum.moving, mlp_grads = join(out_sum.moving, mlp_grads)
+    w_out_grad = total_of(out_sum.parts[0], [out_sum.moving])
     w_qkv_grad = jnp.concatenate(qkv_halves.add(qkv_got).values, axis=-1)
-    output = total_of(hidden, [down_sum.parts[0], down_sum.moving]).astype(BF16)
 
     x = tokens.astype(F32)
     scale = inv_root_of(x)
@@ -927,7 +923,6 @@
     mlp_gain_grad = totals[width : 2 * width]
     q_gain_grad = totals[2 * width : 2 * width + dim]
     k_gain_grad = totals[2 * width + dim :]
-    w_down_grad, w_gate_up_grad = w_down_grad.astype(F32), w_gate_up_grad.astype(F32)
     a, b = heads * dim, (heads + kv_heads) * dim
     return (
         output,
@@ -940,9 +935,7 @@
         w_qkv_grad[:, a:b],
         w_qkv_grad[:, b:],
         w_out_grad,
-        w_gate_up_grad[:, : w_gate.shape[1]],
-        w_gate_up_grad[:, w_gate.shape[1] :],
-        w_down_grad,
+        *mlp_grads,
     )
 
 

time: 632 us -> 596 us (0.943)
  waiting for transfers between devices: 261 us -> 221 us
  starting transfers between devices: 65.9 us -> 73.6 us
  local copies, waits for them, and re-layouts: 25.5 us -> 18 us
    ppermute x24 -> x27, waiting for transfers between devices: 211 us -> 183 us  [local(): lax.ppermute(v, 'tensor', [(i, (i + d) % n) for i in range(n)])]
    ppermute x20 -> x22, waiting for transfers between devices: 45.9 us -> 34.9 us  [exchange(): return lax.ppermute(value, axis, [(i, i ^ step) for i in range(size)])]
    ppermute x20 -> x22, starting transfers between devices: 16.3 us -> 25.4 us  [exchange(): return lax.ppermute(value, axis, [(i, i ^ step) for i in range(size)])]
    ppermute x24 -> x27, starting transfers between devices: 49.2 us -> 47.5 us  [local(): lax.ppermute(v, 'tensor', [(i, (i + d) % n) for i in range(n)])]
    convert_element_type x9 -> x10, other arithmetic: 13.6 us -> 13 us  [add_low(): return (a.astype(F32) + b.astype(F32)).astype(BF16)]
  transfers between devices with their start and end apart: 48 -> 52, of which waited for: 24 -> 23; matrix products, arithmetic and copies ran while one was open for 7% -> 8% of each run, Pallas kernels for 34% -> 37%
where the time goes in v3:
time: 596 us; the launch traced here: 588 us
  waiting for transfers between devices  221 us (37%)
  Pallas kernels  215 us (36%)
  starting transfers between devices  73.6 us (12%)
  other arithmetic  46 us (8%)
  local copies, waits for them, and re-layouts  18 us (3%)
  between operations  14.9 us (2%)
    ppermute x27, waiting for transfers between devices, local(): lax.ppermute(v, 'tensor', [(i, (i + d) % n) for i in range(n)])  183 us
    pallas_call x4, Pallas kernels, mlp_shard(): call(functools.partial(mlp_kernel, tiles), pltpu.PrefetchScalarGridSpec(n...  72.5 us
    ppermute x27, starting transfers between devices, local(): lax.ppermute(v, 'tensor', [(i, (i + d) % n) for i in range(n)])  47.5 us
    ppermute x22, waiting for transfers between devices, exchange(): return lax.ppermute(value, axis, [(i, i ^ step) for i in range(size)])  34.9 us
    pallas_call x2, Pallas kernels, rows_grad(): call(functools.partial(rows_grad_kernel, count), pltpu.PrefetchScalarGrid...  31.1 us
    ppermute x22, starting transfers between devices, exchange(): return lax.ppermute(value, axis, [(i, i ^ step) for i in range(size)])  25.4 us
    pallas_call x4, Pallas kernels, qkv_shard(): call(functools.partial(qkv_kernel, heads, kv_heads, dim), pltpu.PrefetchS...  20.6 us
    pallas_call x4, Pallas kernels, entry_shard(): call(entry_kernel, pltpu.PrefetchScalarGridSpec(num_scalar_prefetch=1, gr...  17.7 us
  transfers between devices with their start and end apart: 52, of which 23 were waited for; matrix products, arithmetic and copies ran while one was open for 8% of the time, Pallas kernels for 37%

profile of v3, /device:TPU:0, one launch (start us, length us, event | category | flops | bytes accessed | tf_op | source)
XLA Modules:
  0.0 588.0 jit_solution(6450344898484762803)
XLA Ops:
  9.6 3.1 collective-permute-start
  19.0 33.1 %collective-permute-done.x_ref = bf16[256,2048]{1,0:T(8,128)(2,1)} collective-permute-done((bf16[256,2048]{1,0:T(8,128)(2,1)}, bf16[256,2048]{1,0:T(8,128)(2,1)}, u32[]{:S(2)}, u32[]{:S(2)}) %collective-permute-start) | collective-permute-done | bytes 1048608 | tf_op jit(solution)/shard_map/ppermute | solution.py:734
  52.1 3.3 all-gather.6.cloned.1.call-done
  60.7 5.1 shard_map.237
  65.9 5.2 shard_map.238
  75.6 6.9 %collective-permute-done.1.x_ref = bf16[256,2048]{1,0:T(8,128)(2,1)} collective-permute-done((bf16[256,2048]{1,0:T(8,128)(2,1)}, bf16[256,2048]{1,0:T(8,128)(2,1)}, u32[]{:S(2)}, u32[]{:S(2)}) %collective-permute-start.1) | collective-permute-done | bytes 1048608 | tf_op jit(solution)/shard_map/ppermute | solution.py:734
  85.5 5.1 shard_map.239
  90.7 16.2 %collective-permute-done.5 = bf16[2,4,256,256]{3,2,1,0:T(8,128)(2,1)} collective-permute-done((bf16[2,4,256,256]{3,2,1,0:T(8,128)(2,1)S(1)}, bf16[2,4,256,256]{3,2,1,0:T(8,128)(2,1)}, u32[]{:S(2)}, u32[]{:S(2)}) %collective-permute-start.5) | collective-permute-done | bytes 1048608 | tf_op jit(solution)/shard_map/ppermute | solution.py:607
  114.3 5.1 shard_map.240
  119.5 9.6 %shard_map.241 = (bf16[4,256,512]{2,1,0:T(8,128)(2,1)S(1)}, f32[4,1024]{1,0:T(4,128)S(1)}) custom-call(s32[1]{0:T(128)} %bitcast.1.z_ref, bf16[1024,1024]{1,0:T(8,128)(2,1)} %get-tuple-element.216.side_ref.refs_4_, s32[1,1024]{1,0:T(1,128)S(1)} %bitcast.151), custom_call_target="tpu_custom_call" | custom-call | flops 2147483 | bytes 5242 | tf_op jit(solution)/shard_map/pallas_call | solution.py:183
  129.3 3.7 collective-permute-start.9
  133.1 12.6 %collective-permute-done.7.refs_1_ = bf16[256,512]{1,0:T(8,128)(2,1)S(1)} collective-permute-done((bf16[256,512]{1,0:T(8,128)(2,1)S(1)}, bf16[256,512]{1,0:T(8,128)(2,1)S(1)}, u32[]{:S(2)}, u32[]{:S(2)}) %collective-permute-start.7) | collective-permute-done | bytes 262176 | tf_op jit(solution)/shard_map/ppermute | solution.py:734
  145.7 18.8 %collective-permute-done.8.refs_2_ = bf16[256,512]{1,0:T(8,128)(2,1)S(1)} collective-permute-done((bf16[256,512]{1,0:T(8,128)(2,1)S(1)}, bf16[256,512]{1,0:T(8,128)(2,1)S(1)}, u32[]{:S(2)}, u32[]{:S(2)}) %collective-permute-start.8) | collective-permute-done | bytes 262176 | tf_op jit(solution)/shard_map/ppermute | solution.py:734
  164.6 8.7 %shard_map.242 = (f32[256,2048]{1,0:T(8,128)}, bf16[256,2048]{1,0:T(8,128)(2,1)}) custom-call(s32[3]{0:T(128)S(1)} %pad_add_fusion.place_ref, bf16[256,512]{1,0:T(8,128)(2,1)S(1)} %get-tuple-element.222.refs_0_, bf16[256,512]{1,0:T(8,128)(2,1)S(1)} %collective-permute-done.7.refs_1_, bf16[256,512]{1,0:T(8,128)(2,1)S(1)} %collective-permute-done.8.refs_2_, ...), custom_call_target="tpu_custom_call" | custom-call | flops 2147483 | bytes 13631 | tf_op jit(solution)/shard_map/pallas_call | solution.py:308
  173.2 20.3 %collective-permute-start.11 = (bf16[256,2048]{1,0:T(8,128)(2,1)}, bf16[256,2048]{1,0:T(8,128)(2,1)S(1)}, u32[]{:S(2)}, u32[]{:S(2)}) collective-permute-start(bf16[256,2048]{1,0:T(8,128)(2,1)} %get-tuple-element.228.x_ref), channel_id=1, source_target_pairs={{0,1},{1,2},{2,3},{3,0},{4,5},{5,6},{6,7},{7,4},{8,9},{9,10},{10,1... | collective-permute-start | bytes 3145736 | tf_op jit(solution)/shard_map/ppermute | solution.py:734
  193.5 18.1 %shard_map.243 = (bf16[1024,1536]{1,0:T(8,128)(2,1)}, bf16[1024,1536]{1,0:T(8,128)(2,1)}, bf16[1024,1536]{1,0:T(8,128)(2,1)}, bf16[1024,2048]{1,0:T(8,128)(2,1)}...) custom-call(s32[1]{0:T(128)} %bitcast.14.sid_ref, bf16[256,2048]{1,0:T(8,128)(2,1)} %get-tuple-element.228.x_ref, ...), custom_call_target="tpu_custom_call" | custom-call | flops 9663676 | bytes 26476 | tf_op jit(solution)/shard_map/pallas_call | solution.py:388
  211.6 19.3 %collective-permute-done.11.x_ref = bf16[256,2048]{1,0:T(8,128)(2,1)S(1)} collective-permute-done((bf16[256,2048]{1,0:T(8,128)(2,1)}, bf16[256,2048]{1,0:T(8,128)(2,1)S(1)}, u32[]{:S(2)}, u32[]{:S(2)}) %collective-permute-start.11) | collective-permute-done | bytes 1048608 | tf_op jit(solution)/shard_map/ppermute | solution.py:734
  231.8 3.2 collective-permute-start.12
  235.0 23.8 %collective-permute-done.12.x_ref = bf16[256,2048]{1,0:T(8,128)(2,1)} collective-permute-done((bf16[256,2048]{1,0:T(8,128)(2,1)S(1)}, bf16[256,2048]{1,0:T(8,128)(2,1)}, u32[]{:S(2)}, u32[]{:S(2)}) %collective-permute-start.12) | collective-permute-done | bytes 1048608 | tf_op jit(solution)/shard_map/ppermute | solution.py:734
  260.0 18.1 %shard_map.244 = (bf16[1024,1536]{1,0:T(8,128)(2,1)}, bf16[1024,1536]{1,0:T(8,128)(2,1)}, bf16[1024,1536]{1,0:T(8,128)(2,1)}, bf16[1024,2048]{1,0:T(8,128)(2,1)}...) custom-call(s32[1]{0:T(128)} %bitcast.sid_ref, ...), custom_call_target="tpu_custom_call", output_to_operand_aliasing={{0}: (6, {}), {1}: (7, {}), {2}: (8, {}), {3}: (9, {})} | custom-call | flops 9663676 | bytes 26476 | tf_op jit(solution)/shard_map/pallas_call | solution.py:388
  278.1 6.8 %collective-permute-done.13.x_ref = bf16[256,2048]{1,0:T(8,128)(2,1)S(1)} collective-permute-done((bf16[256,2048]{1,0:T(8,128)(2,1)}, bf16[256,2048]{1,0:T(8,128)(2,1)S(1)}, u32[]{:S(2)}, u32[]{:S(2)}) %collective-permute-start.13) | collective-permute-done | bytes 1048608 | tf_op jit(solution)/shard_map/ppermute | solution.py:734
  285.1 18.2 %shard_map.245 = (bf16[1024,1536]{1,0:T(8,128)(2,1)}, bf16[1024,1536]{1,0:T(8,128)(2,1)}, bf16[1024,1536]{1,0:T(8,128)(2,1)}, bf16[1024,2048]{1,0:T(8,128)(2,1)}...) custom-call(s32[1]{0:T(128)} %bitcast.19.sid_ref, ...), custom_call_target="tpu_custom_call", output_to_operand_aliasing={{0}: (6, {}), {1}: (7, {}), {2}: (8, {}), {3}: (9, {})} | custom-call | flops 9663676 | bytes 26476 | tf_op jit(solution)/shard_map/pallas_call | solution.py:388
  303.3 7.0 %collective-permute-done.14 = bf16[256,2048]{1,0:T(8,128)(2,1)S(1)} collective-permute-done((bf16[256,2048]{1,0:T(8,128)(2,1)}, bf16[256,2048]{1,0:T(8,128)(2,1)S(1)}, u32[]{:S(2)}, u32[]{:S(2)}) %collective-permute-start.14) | collective-permute-done | bytes 1048608 | tf_op jit(solution)/shard_map/ppermute | solution.py:734
  312.0 18.2 %shard_map.246 = (bf16[1024,1536]{1,0:T(8,128)(2,1)}, bf16[1024,1536]{1,0:T(8,128)(2,1)}, bf16[1024,1536]{1,0:T(8,128)(2,1)}, bf16[1024,2048]{1,0:T(8,128)(2,1)}...) custom-call(s32[1]{0:T(128)} %bitcast.4.sid_ref, ...), custom_call_target="tpu_custom_call", output_to_operand_aliasing={{0}: (6, {}), {1}: (7, {}), {2}: (8, {}), {3}: (9, {})} | custom-call | flops 9663676 | bytes 26476 | tf_op jit(solution)/shard_map/pallas_call | solution.py:388
  330.3 5.9 %collective-permute-done.15 = bf16[256,2048]{1,0:T(8,128)(2,1)S(1)} collective-permute-done((bf16[256,2048]{1,0:T(8,128)(2,1)S(1)}, bf16[256,2048]{1,0:T(8,128)(2,1)S(1)}, u32[]{:S(2)}, u32[]{:S(2)}) %collective-permute-start.15) | collective-permute-done | bytes 1048608 | tf_op jit(solution)/shard_map/ppermute | solution.py:734
  336.1 2.6 add_convert_fusion.5
  339.8 12.1 %shard_map.247.refs_2_ = bf16[8,256,4608]{2,1,0:T(8,128)(2,1)} custom-call(bf16[1024,2048]{1,0:T(8,128)(2,1)} %all-gather.4.cloned.1.call-done.go_ref.x_ref, bf16[1024,1536]{1,0:T(8,128)(2,1)} %get-tuple-element.291.refs_0_), custom_call_target="tpu_custom_call" | custom-call | flops 6442450 | bytes 13631 | tf_op jit(solution)/shard_map/pallas_call | solution.py:552
  351.9 19.0 %shard_map.248 = bf16[8,256,4608]{2,1,0:T(8,128)(2,1)} custom-call(bf16[1024,2048]{1,0:T(8,128)(2,1)} %get-tuple-element.287.x_ref, bf16[1024,1536]{1,0:T(8,128)(2,1)} %get-tuple-element.288.refs_0_, bf16[1024,1536]{1,0:T(8,128)(2,1)} %get-tuple-element.289.refs_1_, bf16[8,256,4608]{2,1,0:T(8,128)(2,1)} %shard_map.247.refs_2_), custom_call_target="tpu_custom_call", output_to_operand_aliasing={{}: (3, {})} | custom-call | flops 12884901 | bytes 23068 | tf_op jit(solution)/shard_map/pallas_call | solution.py:552
  373.6 12.1 %shard_map.249 = (bf16[4,256,512]{2,1,0:T(8,128)(2,1)S(1)}, f32[256,2048]{1,0:T(8,128)}, bf16[256,2048]{1,0:T(8,128)(2,1)}, f32[1,2048]{1,0:T(1,128)S(1)}) custom-call(s32[3]{0:T(128)S(1)} %pad_add_fusion.place_ref, bf16[256,2048]{1,0:T(8,128)(2,1)} %get-tuple-element.282.own_part_ref, bf16[256,2048]{1,0:T(8,128)(2,1)} %go_ref.3, ...), custom_call_target="tpu_custom_call" | custom-call | flops 2147483 | bytes 18874 | tf_op jit(solution)/shard_map/pallas_call | solution.py:444
  390.7 5.5 shard_map.250
  396.7 6.8 %collective-permute-done.20.refs_2_ = bf16[256,512]{1,0:T(8,128)(2,1)S(1)} collective-permute-done((bf16[256,512]{1,0:T(8,128)(2,1)S(1)}, bf16[256,512]{1,0:T(8,128)(2,1)S(1)}, u32[]{:S(2)}, u32[]{:S(2)}) %collective-permute-start.20) | collective-permute-done | bytes 262176 | tf_op jit(solution)/shard_map/ppermute | solution.py:734
  403.5 4.5 collective-permute-start.23
  408.4 14.9 %shard_map.251 = (bf16[1024,1024]{1,0:T(8,128)(2,1)}, f32[8,128]{1,0:T(8,128)S(1)}) custom-call(s32[1]{0:T(128)} %bitcast.1.z_ref, bf16[256,512]{1,0:T(8,128)(2,1)S(1)} %get-tuple-element.300.refs_0_, bf16[256,512]{1,0:T(8,128)(2,1)S(1)} %collective-permute-done.19.refs_1_, bf16[256,512]{1,0:T(8,128)(2,1)S(1)} %collective-permute-done.20.refs_2_, ...), custom_call_target="tpu_custom_call" | custom-call | flops 5368709 | bytes 12582 | tf_op jit(solution)/shard_map/pallas_call | solution.py:262
  425.7 5.0 shard_map.252
  430.8 8.7 %shard_map.253 = (bf16[4,2,512,128]{3,2,1,0:T(8,128)(2,1)}, bf16[4,2,512,128]{3,2,1,0:T(8,128)(2,1)}, bf16[4,2,512,128]{3,2,1,0:T(8,128)(2,1)}, bf16[4,2,512,128]{3,2,1,0:T(8,128)(2,1)}) custom-call(s32[4]{0:T(128)S(1)} %get-tuple-element.397.place_ref, bf16[256,512]{1,0:T(8,128)(2,1)S(1)} %get-tuple-element.222.refs_0_, ...), custom_call_target="tpu_custom_call" | custom-call | flops 1073741 | bytes 4194 | tf_op jit(solution)/shard_map/pallas_call | solution.py:499
  439.5 4.3 collective-permute-done.24
  452.1 4.2 shard_map.254
  456.3 6.6 %shard_map.255 = (bf16[4,256,1024]{2,1,0:T(8,128)(2,1)}, f32[4,256,128]{2,1,0:T(8,128)S(1)}) custom-call(s32[1]{0:T(128)S(6)} %sub.19.side_ref, bf16[1024,2048]{1,0:T(8,128)(2,1)} %get-tuple-element.321.entry_ref, bf16[1024,1024]{1,0:T(8,128)(2,1)} %get-tuple-element.349.grad_ref, bf16[2048,1024]{1,0:T(8,128)(2,1)} %pad_maximum_fusion.w_ref), custom_call_target="tpu_custom_call" | custom-call | flops 2147483 | bytes 14680 | tf_op jit(solution)/shard_map/pallas_call | solution.py:584
  463.0 6.6 %shard_map.256 = (bf16[4,256,1024]{2,1,0:T(8,128)(2,1)}, f32[4,256,128]{2,1,0:T(8,128)S(1)}) custom-call(s32[1]{0:T(128)} %bitcast.3.side_ref, bf16[1024,2048]{1,0:T(8,128)(2,1)} %get-tuple-element.321.entry_ref, bf16[1024,1024]{1,0:T(8,128)(2,1)} %get-tuple-element.349.grad_ref, bf16[2048,1024]{1,0:T(8,128)(2,1)} %pad_maximum_fusion.w_ref), custom_call_target="tpu_custom_call" | custom-call | flops 2147483 | bytes 14680 | tf_op jit(solution)/shard_map/pallas_call | solution.py:584
  474.6 7.6 %collective-permute-done.27 = bf16[256,1024]{1,0:T(8,128)(2,1)} collective-permute-done((bf16[256,1024]{1,0:T(8,128)(2,1)S(1)}, bf16[256,1024]{1,0:T(8,128)(2,1)}, u32[]{:S(2)}, u32[]{:S(2)}) %collective-permute-start.27) | collective-permute-done | bytes 524320 | tf_op jit(solution)/shard_map/ppermute | solution.py:734
  492.9 4.1 shard_map.257
  497.1 16.1 %collective-permute-done.36 = f32[1,4352]{1,0:T(1,128)S(1)} collective-permute-done((f32[1,4352]{1,0:T(1,128)S(1)}, f32[1,4352]{1,0:T(1,128)S(1)}, u32[]{:S(2)}, u32[]{:S(2)}) %collective-permute-start.36) | collective-permute-done | bytes 17440 | tf_op jit(solution)/shard_map/ppermute | solution.py:607
  513.3 2.6 add_convert_fusion.3
  524.2 4.5 collective-permute-start.39
  528.8 4.3 shard_map.258
  542.1 17.0 %collective-permute-done.46 = bf16[512,256]{1,0:T(8,128)(2,1)S(1)} collective-permute-done((bf16[512,256]{1,0:T(8,128)(2,1)S(1)}, bf16[512,256]{1,0:T(8,128)(2,1)S(1)}, u32[]{:S(2)}, u32[]{:S(2)}) %collective-permute-start.46) | collective-permute-done | bytes 262176 | tf_op jit(solution)/shard_map/ppermute | solution.py:734
  561.0 6.5 %collective-permute-done.47 = bf16[512,256]{1,0:T(8,128)(2,1)S(1)} collective-permute-done((bf16[512,256]{1,0:T(8,128)(2,1)S(1)}, bf16[512,256]{1,0:T(8,128)(2,1)S(1)}, u32[]{:S(2)}, u32[]{:S(2)}) %collective-permute-start.47) | collective-permute-done | bytes 262176 | tf_op jit(solution)/shard_map/ppermute | solution.py:734
  577.2 3.2 copy.54
  (248 shorter events, 98.9 us)
Async XLA Ops:
  7.2 48.1 %all-gather.6.cloned.1.call-start = ((), (), s32[]{:S(2)}) async-start(), calls=%async_computation.3 | async-start | bytes 1310720 | tf_op jit(solution)/shard_map/all_gather | solution.py:744
  9.5 249.2 %all-gather.4.cloned.1.call-start = ((), (), s32[]{:S(2)}) async-start(), calls=%async_computation.1 | async-start | bytes 5242880 | tf_op jit(solution)/shard_map/all_gather | solution.py:777
  9.6 42.5 %collective-permute-start = (bf16[256,2048]{1,0:T(8,128)(2,1)}, bf16[256,2048]{1,0:T(8,128)(2,1)}, u32[]{:S(2)}, u32[]{:S(2)}) collective-permute-start(bf16[256,2048]{1,0:T(8,128)(2,1)} %refs_6_.1), channel_id=1, source_target_pairs={{0,1},{1,2},{2,3},{3,0},{4,5},{5,6},{6,7},{7,4},{8,9},{9,10},{10,1... | collective-permute-start | bytes 3145736 | tf_op jit(solution)/shard_map/ppermute | solution.py:734
  55.3 27.2 %collective-permute-start.1 = (bf16[256,2048]{1,0:T(8,128)(2,1)}, bf16[256,2048]{1,0:T(8,128)(2,1)}, u32[]{:S(2)}, u32[]{:S(2)}) collective-permute-start(bf16[256,2048]{1,0:T(8,128)(2,1)} %collective-permute-done.x_ref), channel_id=1, source_target_pairs={{0,1},{1,2},{2,3},{3,0},{4,5},{5,6},{6,7},{7,4},{8,9},{9,10},{10,1... | collective-permute-start | bytes 3145736 | tf_op jit(solution)/shard_map/ppermute | solution.py:734
  57.7 13.8 %collective-permute-start.2 = (bf16[4,256,256]{2,1,0:T(8,128)(2,1)S(1)}, bf16[4,256,256]{2,1,0:T(8,128)(2,1)S(1)}, u32[]{:S(2)}, u32[]{:S(2)}) collective-permute-start(bf16[4,256,256]{2,1,0:T(8,128)(2,1)S(1)} %get-tuple-element.427), channel_id=1, source_target_pairs={{0,8},{4,12},{8,0},{12,4},{16,24},{20,28},{24,16},{28,20},{1,9},{5... | collective-permute-start | bytes 1572872 | tf_op jit(solution)/shard_map/ppermute | solution.py:607
  59.2 14.3 %collective-permute-start.3 = (bf16[4,256,256]{2,1,0:T(8,128)(2,1)}, bf16[4,256,256]{2,1,0:T(8,128)(2,1)}, u32[]{:S(2)}, u32[]{:S(2)}) collective-permute-start(bf16[4,256,256]{2,1,0:T(8,128)(2,1)} %get-tuple-element.426), channel_id=1, source_target_pairs={{0,16},{4,20},{8,24},{12,28},{16,0},{20,4},{24,8},{28,12},{1,17},{... | collective-permute-start | bytes 1572872 | tf_op jit(solution)/shard_map/ppermute | solution.py:607
  82.5 24.3 %collective-permute-start.5 = (bf16[2,4,256,256]{3,2,1,0:T(8,128)(2,1)S(1)}, bf16[2,4,256,256]{3,2,1,0:T(8,128)(2,1)}, u32[]{:S(2)}, u32[]{:S(2)}) collective-permute-start(bf16[2,4,256,256]{3,2,1,0:T(8,128)(2,1)S(1)} %pad_maximum_fusion.4), channel_id=1, source_target_pairs={{0,16},{4,20},{8,24},{12,28},{16,0},{20,4},{24,8},{28,12},{1,17},{... | collective-permute-start | bytes 3145736 | tf_op jit(solution)/shard_map/ppermute | solution.py:607
  84.1 24.3 %collective-permute-start.6 = (bf16[2,4,256,256]{3,2,1,0:T(8,128)(2,1)}, bf16[2,4,256,256]{3,2,1,0:T(8,128)(2,1)}, u32[]{:S(2)}, u32[]{:S(2)}) collective-permute-start(bf16[2,4,256,256]{3,2,1,0:T(8,128)(2,1)} %pad_maximum_fusion.5), channel_id=1, source_target_pairs={{0,8},{4,12},{8,0},{12,4},{16,24},{20,28},{24,16},{28,20},{1,9},{5... | collective-permute-start | bytes 3145736 | tf_op jit(solution)/shard_map/ppermute | solution.py:607
  85.5 25.8 %collective-permute-start.4 = (bf16[256,2048]{1,0:T(8,128)(2,1)}, bf16[256,2048]{1,0:T(8,128)(2,1)}, u32[]{:S(2)}, u32[]{:S(2)}) collective-permute-start(bf16[256,2048]{1,0:T(8,128)(2,1)} %collective-permute-done.1.x_ref), channel_id=1, source_target_pairs={{0,1},{1,2},{2,3},{3,0},{4,5},{5,6},{6,7},{7,4},{8,9},{9,10},{10,1... | collective-permute-start | bytes 3145736 | tf_op jit(solution)/shard_map/ppermute | solution.py:734
  113.7 50.8 %collective-permute-start.10 = (bf16[4,4,512,256]{3,2,1,0:T(8,128)(2,1)}, bf16[4,4,512,256]{3,2,1,0:T(8,128)(2,1)}, u32[]{:S(2)}, u32[]{:S(2)}) collective-permute-start(bf16[4,4,512,256]{3,2,1,0:T(8,128)(2,1)} %pad_maximum_fusion.1.refs_4_.own_ref), channel_id=1, source_target_pairs={{0,4},{4,0},{1,5},{5,1},{2,6},{6,2},{3,7},{7,3},{8,12},{12,8},{9,1... | collective-permute-start | bytes 12582920 | tf_op jit(solution)/shard_map/ppermute | solution.py:607
  113.7 459.0 %reduce-scatter.2.cloned.1.call-start = ((), (), s32[]{:S(2)}) async-start(), calls=%async_computation.2 | async-start | bytes 21233664 | tf_op jit(solution)/shard_map/reduce_scatter | solution.py:788
  129.1 16.6 %collective-permute-start.7 = (bf16[256,512]{1,0:T(8,128)(2,1)S(1)}, bf16[256,512]{1,0:T(8,128)(2,1)S(1)}, u32[]{:S(2)}, u32[]{:S(2)}) collective-permute-start(bf16[256,512]{1,0:T(8,128)(2,1)S(1)} %get-tuple-element.422), channel_id=1, source_target_pairs={{0,1},{1,2},{2,3},{3,0},{4,5},{5,6},{6,7},{7,4},{8,9},{9,10},{10,1... | collective-permute-start | bytes 786440 | tf_op jit(solution)/shard_map/ppermute | solution.py:734
  129.2 35.4 %collective-permute-start.8 = (bf16[256,512]{1,0:T(8,128)(2,1)S(1)}, bf16[256,512]{1,0:T(8,128)(2,1)S(1)}, u32[]{:S(2)}, u32[]{:S(2)}) collective-permute-start(bf16[256,512]{1,0:T(8,128)(2,1)S(1)} %get-tuple-element.421), channel_id=1, source_target_pairs={{0,2},{1,3},{2,0},{3,1},{4,6},{5,7},{6,4},{7,5},{8,10},{9,11},{10,... | collective-permute-start | bytes 786440 | tf_op jit(solution)/shard_map/ppermute | solution.py:734
  129.3 35.3 %collective-permute-start.9 = (bf16[256,512]{1,0:T(8,128)(2,1)S(1)}, bf16[256,512]{1,0:T(8,128)(2,1)S(1)}, u32[]{:S(2)}, u32[]{:S(2)}) collective-permute-start(bf16[256,512]{1,0:T(8,128)(2,1)S(1)} %get-tuple-element.420), channel_id=1, source_target_pairs={{0,3},{1,0},{2,1},{3,2},{4,7},{5,4},{6,5},{7,6},{8,11},{9,8},{10,9... | collective-permute-start | bytes 786440 | tf_op jit(solution)/shard_map/ppermute | solution.py:734
  173.2 57.6 %collective-permute-start.11 = (bf16[256,2048]{1,0:T(8,128)(2,1)}, bf16[256,2048]{1,0:T(8,128)(2,1)S(1)}, u32[]{:S(2)}, u32[]{:S(2)}) collective-permute-start(bf16[256,2048]{1,0:T(8,128)(2,1)} %get-tuple-element.228.x_ref), channel_id=1, source_target_pairs={{0,1},{1,2},{2,3},{3,0},{4,5},{5,6},{6,7},{7,4},{8,9},{9,10},{10,1... | collective-permute-start | bytes 3145736 | tf_op jit(solution)/shard_map/ppermute | solution.py:734
  231.8 26.9 %collective-permute-start.12 = (bf16[256,2048]{1,0:T(8,128)(2,1)S(1)}, bf16[256,2048]{1,0:T(8,128)(2,1)}, u32[]{:S(2)}, u32[]{:S(2)}) collective-permute-start(bf16[256,2048]{1,0:T(8,128)(2,1)S(1)} %collective-permute-done.11.x_ref), channel_id=1, source_target_pairs={{0,1},{1,2},{2,3},{3,0},{4,5},{5,6},{6,7},{7,4},{8,9},{9,10},{10,1... | collective-permute-start | bytes 3145736 | tf_op jit(solution)/shard_map/ppermute | solution.py:734
  258.7 26.2 %collective-permute-start.13 = (bf16[256,2048]{1,0:T(8,128)(2,1)}, bf16[256,2048]{1,0:T(8,128)(2,1)S(1)}, u32[]{:S(2)}, u32[]{:S(2)}) collective-permute-start(bf16[256,2048]{1,0:T(8,128)(2,1)} %collective-permute-done.12.x_ref), channel_id=1, source_target_pairs={{0,1},{1,2},{2,3},{3,0},{4,5},{5,6},{6,7},{7,4},{8,9},{9,10},{10,1... | collective-permute-start | bytes 3145736 | tf_op jit(solution)/shard_map/ppermute | solution.py:734
  284.9 25.4 %collective-permute-start.14 = (bf16[256,2048]{1,0:T(8,128)(2,1)}, bf16[256,2048]{1,0:T(8,128)(2,1)S(1)}, u32[]{:S(2)}, u32[]{:S(2)}) collective-permute-start(bf16[256,2048]{1,0:T(8,128)(2,1)} %get-tuple-element.266), channel_id=1, source_target_pairs={{0,1},{1,2},{2,3},{3,0},{4,5},{5,6},{6,7},{7,4},{8,9},{9,10},{10,1... | collective-permute-start | bytes 3145736 | tf_op jit(solution)/shard_map/ppermute | solution.py:734
  312.0 24.2 %collective-permute-start.15 = (bf16[256,2048]{1,0:T(8,128)(2,1)S(1)}, bf16[256,2048]{1,0:T(8,128)(2,1)S(1)}, u32[]{:S(2)}, u32[]{:S(2)}) collective-permute-start(bf16[256,2048]{1,0:T(8,128)(2,1)S(1)} %add_convert_fusion.6), channel_id=1, source_target_pairs={{0,1},{1,2},{2,3},{3,0},{4,5},{5,6},{6,7},{7,4},{8,9},{9,10},{10,1... | collective-permute-start | bytes 3145736 | tf_op jit(solution)/shard_map/ppermute | solution.py:734
  338.7 34.6 %collective-permute-start.16 = (bf16[256,2048]{1,0:T(8,128)(2,1)}, bf16[256,2048]{1,0:T(8,128)(2,1)}, u32[]{:S(2)}, u32[]{:S(2)}) collective-permute-start(bf16[256,2048]{1,0:T(8,128)(2,1)} %add_convert_fusion.5), channel_id=1, source_target_pairs={{0,1},{1,2},{2,3},{3,0},{4,5},{5,6},{6,7},{7,4},{8,9},{9,10},{10,1... | collective-permute-start | bytes 3145736 | tf_op jit(solution)/shard_map/ppermute | solution.py:734
  339.8 33.6 %collective-permute-start.17 = (bf16[256,1024]{1,0:T(8,128)(2,1)}, bf16[256,1024]{1,0:T(8,128)(2,1)S(1)}, u32[]{:S(2)}, u32[]{:S(2)}) collective-permute-start(bf16[256,1024]{1,0:T(8,128)(2,1)} %get-tuple-element.419), channel_id=1, source_target_pairs={{0,1},{1,2},{2,3},{3,0},{4,5},{5,6},{6,7},{7,4},{8,9},{9,10},{10,1... | collective-permute-start | bytes 1572872 | tf_op jit(solution)/shard_map/ppermute | solution.py:734
  373.4 12.3 %collective-permute-start.18 = (bf16[256,1024]{1,0:T(8,128)(2,1)}, bf16[256,1024]{1,0:T(8,128)(2,1)S(1)}, u32[]{:S(2)}, u32[]{:S(2)}) collective-permute-start(bf16[256,1024]{1,0:T(8,128)(2,1)} %get-tuple-element.418), channel_id=1, source_target_pairs={{0,1},{1,2},{2,3},{3,0},{4,5},{5,6},{6,7},{7,4},{8,9},{9,10},{10,1... | collective-permute-start | bytes 1572872 | tf_op jit(solution)/shard_map/ppermute | solution.py:734
  385.8 10.9 %collective-permute-start.19 = (bf16[256,512]{1,0:T(8,128)(2,1)S(1)}, bf16[256,512]{1,0:T(8,128)(2,1)S(1)}, u32[]{:S(2)}, u32[]{:S(2)}) collective-permute-start(bf16[256,512]{1,0:T(8,128)(2,1)S(1)} %get-tuple-element.416), channel_id=1, source_target_pairs={{0,1},{1,2},{2,3},{3,0},{4,5},{5,6},{6,7},{7,4},{8,9},{9,10},{10,1... | collective-permute-start | bytes 786440 | tf_op jit(solution)/shard_map/ppermute | solution.py:734
  388.3 15.2 %collective-permute-start.20 = (bf16[256,512]{1,0:T(8,128)(2,1)S(1)}, bf16[256,512]{1,0:T(8,128)(2,1)S(1)}, u32[]{:S(2)}, u32[]{:S(2)}) collective-permute-start(bf16[256,512]{1,0:T(8,128)(2,1)S(1)} %get-tuple-element.415), channel_id=1, source_target_pairs={{0,2},{1,3},{2,0},{3,1},{4,6},{5,7},{6,4},{7,5},{8,10},{9,11},{10,... | collective-permute-start | bytes 786440 | tf_op jit(solution)/shard_map/ppermute | solution.py:734
  390.4 13.0 %collective-permute-start.21 = (bf16[256,512]{1,0:T(8,128)(2,1)S(1)}, bf16[256,512]{1,0:T(8,128)(2,1)S(1)}, u32[]{:S(2)}, u32[]{:S(2)}) collective-permute-start(bf16[256,512]{1,0:T(8,128)(2,1)S(1)} %get-tuple-element.414), channel_id=1, source_target_pairs={{0,3},{1,0},{2,1},{3,2},{4,7},{5,4},{6,5},{7,6},{8,11},{9,8},{10,9... | collective-permute-start | bytes 786440 | tf_op jit(solution)/shard_map/ppermute | solution.py:734
  403.5 19.9 %collective-permute-start.22 = (bf16[4,4,512,256]{3,2,1,0:T(8,128)(2,1)}, bf16[4,4,512,256]{3,2,1,0:T(8,128)(2,1)S(1)}, u32[]{:S(2)}, u32[]{:S(2)}) collective-permute-start(bf16[4,4,512,256]{3,2,1,0:T(8,128)(2,1)} %shard_map.250), channel_id=1, source_target_pairs={{0,4},{4,0},{1,5},{5,1},{2,6},{6,2},{3,7},{7,3},{8,12},{12,8},{9,1... | collective-permute-start | bytes 12582920 | tf_op jit(solution)/shard_map/ppermute | solution.py:607
  403.5 19.9 %collective-permute-start.23 = (bf16[256,1024]{1,0:T(8,128)(2,1)S(1)}, bf16[256,1024]{1,0:T(8,128)(2,1)S(1)}, u32[]{:S(2)}, u32[]{:S(2)}) collective-permute-start(bf16[256,1024]{1,0:T(8,128)(2,1)S(1)} %get-tuple-element.308), channel_id=1, source_target_pairs={{0,1},{1,2},{2,3},{3,0},{4,5},{5,6},{6,7},{7,4},{8,9},{9,10},{10,1... | collective-permute-start | bytes 1572872 | tf_op jit(solution)/shard_map/ppermute | solution.py:734
  407.9 31.5 %collective-permute-start.25 = (bf16[256,1024]{1,0:T(8,128)(2,1)S(1)}, bf16[256,1024]{1,0:T(8,128)(2,1)S(1)}, u32[]{:S(2)}, u32[]{:S(2)}) collective-permute-start(bf16[256,1024]{1,0:T(8,128)(2,1)S(1)} %get-tuple-element.317), channel_id=1, source_target_pairs={{0,1},{1,2},{2,3},{3,0},{4,5},{5,6},{6,7},{7,4},{8,9},{9,10},{10,1... | collective-permute-start | bytes 1572872 | tf_op jit(solution)/shard_map/ppermute | solution.py:734
  423.6 20.3 %collective-permute-start.24 = (bf16[256,1024]{1,0:T(8,128)(2,1)S(1)}, bf16[256,1024]{1,0:T(8,128)(2,1)S(1)}, u32[]{:S(2)}, u32[]{:S(2)}) collective-permute-start(bf16[256,1024]{1,0:T(8,128)(2,1)S(1)} %add_convert_fusion.8), channel_id=1, source_target_pairs={{0,1},{1,2},{2,3},{3,0},{4,5},{5,6},{6,7},{7,4},{8,9},{9,10},{10,1... | collective-permute-start | bytes 1572872 | tf_op jit(solution)/shard_map/ppermute | solution.py:734
  443.8 28.1 %collective-permute-start.26 = (bf16[256,2048]{1,0:T(8,128)(2,1)}, bf16[256,2048]{1,0:T(8,128)(2,1)}, u32[]{:S(2)}, u32[]{:S(2)}) collective-permute-start(bf16[256,2048]{1,0:T(8,128)(2,1)} %shard_map.252), channel_id=1, source_target_pairs={{0,1},{1,2},{2,3},{3,0},{4,5},{5,6},{6,7},{7,4},{8,9},{9,10},{10,1... | collective-permute-start | bytes 3145736 | tf_op jit(solution)/shard_map/ppermute | solution.py:734
  447.8 34.4 %collective-permute-start.27 = (bf16[256,1024]{1,0:T(8,128)(2,1)S(1)}, bf16[256,1024]{1,0:T(8,128)(2,1)}, u32[]{:S(2)}, u32[]{:S(2)}) collective-permute-start(bf16[256,1024]{1,0:T(8,128)(2,1)S(1)} %add_convert_fusion.7), channel_id=1, source_target_pairs={{0,1},{1,2},{2,3},{3,0},{4,5},{5,6},{6,7},{7,4},{8,9},{9,10},{10,1... | collective-permute-start | bytes 1572872 | tf_op jit(solution)/shard_map/ppermute | solution.py:734
  449.1 33.1 %collective-permute-start.28 = (bf16[2,2,512,128]{3,2,1,0:T(8,128)(2,1)S(1)}, bf16[2,2,512,128]{3,2,1,0:T(8,128)(2,1)}, u32[]{:S(2)}, u32[]{:S(2)}) collective-permute-start(bf16[2,2,512,128]{3,2,1,0:T(8,128)(2,1)S(1)} %get-tuple-element.410), channel_id=1, source_target_pairs={{0,8},{4,12},{8,0},{12,4},{16,24},{20,28},{24,16},{28,20},{1,9},{5... | collective-permute-start | bytes 1572872 | tf_op jit(solution)/shard_map/ppermute | solution.py:607
  450.7 31.5 %collective-permute-start.29 = (bf16[2,2,512,128]{3,2,1,0:T(8,128)(2,1)S(1)}, bf16[2,2,512,128]{3,2,1,0:T(8,128)(2,1)}, u32[]{:S(2)}, u32[]{:S(2)}) collective-permute-start(bf16[2,2,512,128]{3,2,1,0:T(8,128)(2,1)S(1)} %get-tuple-element.408), channel_id=1, source_target_pairs={{0,16},{4,20},{8,24},{12,28},{16,0},{20,4},{24,8},{28,12},{1,17},{... | collective-permute-start | bytes 1572872 | tf_op jit(solution)/shard_map/ppermute | solution.py:607
  482.2 31.1 %collective-permute-start.30 = (bf16[256,2048]{1,0:T(8,128)(2,1)}, bf16[256,2048]{1,0:T(8,128)(2,1)}, u32[]{:S(2)}, u32[]{:S(2)}) collective-permute-start(bf16[256,2048]{1,0:T(8,128)(2,1)} %add_convert_fusion.4), channel_id=1, source_target_pairs={{0,1},{1,2},{2,3},{3,0},{4,5},{5,6},{6,7},{7,4},{8,9},{9,10},{10,1... | collective-permute-start | bytes 3145736 | tf_op jit(solution)/shard_map/ppermute | solution.py:734
  484.3 31.6 %collective-permute-start.33 = (bf16[4,256,1024]{2,1,0:T(8,128)(2,1)}, bf16[4,256,1024]{2,1,0:T(8,128)(2,1)S(1)}, u32[]{:S(2)}, u32[]{:S(2)}) collective-permute-start(bf16[4,256,1024]{2,1,0:T(8,128)(2,1)} %get-tuple-element.338), channel_id=1, source_target_pairs={{0,4},{4,0},{1,5},{5,1},{2,6},{6,2},{3,7},{7,3},{8,12},{12,8},{9,1... | collective-permute-start | bytes 6291464 | tf_op jit(solution)/shard_map/ppermute | solution.py:607
  486.3 29.6 %collective-permute-start.31 = (bf16[2,2,512,128]{3,2,1,0:T(8,128)(2,1)S(1)}, bf16[2,2,512,128]{3,2,1,0:T(8,128)(2,1)S(1)}, u32[]{:S(2)}, u32[]{:S(2)}) collective-permute-start(bf16[2,2,512,128]{3,2,1,0:T(8,128)(2,1)S(1)} %get-tuple-element.406), channel_id=1, source_target_pairs={{0,8},{4,12},{8,0},{12,4},{16,24},{20,28},{24,16},{28,20},{1,9},{5... | collective-permute-start | bytes 1572872 | tf_op jit(solution)/shard_map/ppermute | solution.py:607
  486.9 29.0 %collective-permute-start.32 = (bf16[2,2,512,128]{3,2,1,0:T(8,128)(2,1)S(1)}, bf16[2,2,512,128]{3,2,1,0:T(8,128)(2,1)S(1)}, u32[]{:S(2)}, u32[]{:S(2)}) collective-permute-start(bf16[2,2,512,128]{3,2,1,0:T(8,128)(2,1)S(1)} %get-tuple-element.404), channel_id=1, source_target_pairs={{0,16},{4,20},{8,24},{12,28},{16,0},{20,4},{24,8},{28,12},{1,17},{... | collective-permute-start | bytes 1572872 | tf_op jit(solution)/shard_map/ppermute | solution.py:607
  488.9 24.3 %collective-permute-start.36 = (f32[1,4352]{1,0:T(1,128)S(1)}, f32[1,4352]{1,0:T(1,128)S(1)}, u32[]{:S(2)}, u32[]{:S(2)}) collective-permute-start(f32[1,4352]{1,0:T(1,128)S(1)} %add.226), channel_id=1, source_target_pairs={{0,16},{4,20},{8,24},{12,28},{16,0},{20,4},{24,8},{28,12},{1,17},{... | collective-permute-start | bytes 52232 | tf_op jit(solution)/shard_map/ppermute | solution.py:607
  518.7 15.1 %collective-permute-start.40 = (bf16[4,512,128]{2,1,0:T(8,128)(2,1)}, bf16[4,512,128]{2,1,0:T(8,128)(2,1)S(1)}, u32[]{:S(2)}, u32[]{:S(2)}) collective-permute-start(bf16[4,512,128]{2,1,0:T(8,128)(2,1)} %fusion.20), channel_id=1, source_target_pairs={{0,16},{4,20},{8,24},{12,28},{16,0},{20,4},{24,8},{28,12},{1,17},{... | collective-permute-start | bytes 1572872 | tf_op jit(solution)/shard_map/ppermute | solution.py:607
  522.7 12.6 %collective-permute-start.41 = (bf16[4,512,128]{2,1,0:T(8,128)(2,1)}, bf16[4,512,128]{2,1,0:T(8,128)(2,1)S(1)}, u32[]{:S(2)}, u32[]{:S(2)}) collective-permute-start(bf16[4,512,128]{2,1,0:T(8,128)(2,1)} %fusion.21), channel_id=1, source_target_pairs={{0,8},{4,12},{8,0},{12,4},{16,24},{20,28},{24,16},{28,20},{1,9},{5... | collective-permute-start | bytes 1572872 | tf_op jit(solution)/shard_map/ppermute | solution.py:607
  524.2 8.9 %collective-permute-start.39 = (f32[1,4352]{1,0:T(1,128)S(1)}, f32[1,4352]{1,0:T(1,128)S(1)}, u32[]{:S(2)}, u32[]{:S(2)}) collective-permute-start(f32[1,4352]{1,0:T(1,128)S(1)} %add.234), channel_id=1, source_target_pairs={{0,2},{1,3},{2,0},{3,1},{4,6},{5,7},{6,4},{7,5},{8,10},{9,11},{10,... | collective-permute-start | bytes 52232 | tf_op jit(solution)/shard_map/ppermute | solution.py:607
  528.7 39.8 %collective-permute-start.37 = (bf16[256,2048]{1,0:T(8,128)(2,1)}, bf16[256,2048]{1,0:T(8,128)(2,1)S(1)}, u32[]{:S(2)}, u32[]{:S(2)}) collective-permute-start(bf16[256,2048]{1,0:T(8,128)(2,1)} %add_convert_fusion.3), channel_id=1, source_target_pairs={{0,1},{1,2},{2,3},{3,0},{4,5},{5,6},{6,7},{7,4},{8,9},{9,10},{10,1... | collective-permute-start | bytes 3145736 | tf_op jit(solution)/shard_map/ppermute | solution.py:734
  536.3 23.0 %collective-permute-start.42 = (bf16[2,256,512]{2,1,0:T(8,128)(2,1)S(1)}, bf16[2,256,512]{2,1,0:T(8,128)(2,1)S(1)}, u32[]{:S(2)}, u32[]{:S(2)}) collective-permute-start(bf16[2,256,512]{2,1,0:T(8,128)(2,1)S(1)} %dynamic-slice_bitcast_fusion.1), channel_id=1, source_target_pairs={{0,8},{4,12},{8,0},{12,4},{16,24},{20,28},{24,16},{28,20},{1,9},{5... | collective-permute-start | bytes 1572872 | tf_op jit(solution)/shard_map/ppermute | solution.py:607
  539.2 20.0 %collective-permute-start.46 = (bf16[512,256]{1,0:T(8,128)(2,1)S(1)}, bf16[512,256]{1,0:T(8,128)(2,1)S(1)}, u32[]{:S(2)}, u32[]{:S(2)}) collective-permute-start(bf16[512,256]{1,0:T(8,128)(2,1)S(1)} %fusion.31), channel_id=1, source_target_pairs={{0,1},{1,2},{2,3},{3,0},{4,5},{5,6},{6,7},{7,4},{8,9},{9,10},{10,1... | collective-permute-start | bytes 786440 | tf_op jit(solution)/shard_map/ppermute | solution.py:734
  541.5 18.7 %collective-permute-start.44 = (bf16[2,256,512]{2,1,0:T(8,128)(2,1)S(1)}, bf16[2,256,512]{2,1,0:T(8,128)(2,1)S(1)}, u32[]{:S(2)}, u32[]{:S(2)}) collective-permute-start(bf16[2,256,512]{2,1,0:T(8,128)(2,1)S(1)} %dynamic-slice_bitcast_fusion), channel_id=1, source_target_pairs={{0,16},{4,20},{8,24},{12,28},{16,0},{20,4},{24,8},{28,12},{1,17},{... | collective-permute-start | bytes 1572872 | tf_op jit(solution)/shard_map/ppermute | solution.py:607
  559.6 12.3 %collective-permute-start.43 = (bf16[256,512]{1,0:T(8,128)(2,1)S(1)}, bf16[256,512]{1,0:T(8,128)(2,1)S(1)}, u32[]{:S(2)}, u32[]{:S(2)}) collective-permute-start(bf16[256,512]{1,0:T(8,128)(2,1)S(1)} %fusion.24), channel_id=1, source_target_pairs={{0,16},{4,20},{8,24},{12,28},{16,0},{20,4},{24,8},{28,12},{1,17},{... | collective-permute-start | bytes 786440 | tf_op jit(solution)/shard_map/ppermute | solution.py:607
  560.4 10.5 %collective-permute-start.45 = (bf16[256,512]{1,0:T(8,128)(2,1)S(1)}, bf16[256,512]{1,0:T(8,128)(2,1)S(1)}, u32[]{:S(2)}, u32[]{:S(2)}) collective-permute-start(bf16[256,512]{1,0:T(8,128)(2,1)S(1)} %fusion.25), channel_id=1, source_target_pairs={{0,8},{4,12},{8,0},{12,4},{16,24},{20,28},{24,16},{28,20},{1,9},{5... | collective-permute-start | bytes 786440 | tf_op jit(solution)/shard_map/ppermute | solution.py:607
  568.3 8.9 %collective-permute-start.48 = (bf16[512,256]{1,0:T(8,128)(2,1)}, bf16[512,256]{1,0:T(8,128)(2,1)S(1)}, u32[]{:S(2)}, u32[]{:S(2)}) collective-permute-start(bf16[512,256]{1,0:T(8,128)(2,1)} %fusion.22), channel_id=1, source_target_pairs={{0,1},{1,2},{2,3},{3,0},{4,5},{5,6},{6,7},{7,4},{8,9},{9,10},{10,1... | collective-permute-start | bytes 786440 | tf_op jit(solution)/shard_map/ppermute | solution.py:734
  (47 other events, 483.1 us)
Sparse Core Ops, SparseCore 0:
  10.2 45.1 all-gather.5
  113.9 122.4 all-gather.3
  373.5 148.2 reduce-scatter.1

commit v4 on v3

--- a/solution.py
+++ b/solution.py
@@ -607,8 +607,7 @@
     return lax.ppermute(value, axis, [(i, i ^ step) for i in range(size)])
 
 
-def total_over(value, axis):
-    step = 1
+def total_over(value, axis, step=1):
     while step < lax.axis_size(axis):
         value = value + exchange(value, axis, step)
         step *= 2
@@ -878,6 +877,7 @@
     state, grads, totals, output = join(state, grads, totals, output)
     entry_sum.moving, out_one, one_got, out_two, two_got, qkv_got, w_qkv_grad = state
 
+    totals = totals + exchange(totals, "tensor", 1)
     out_one, out_two = out_one.add(one_got), out_two.add(two_got)
     values = [jnp.concatenate(pair, axis=-3) for pair in zip(out_one.values, out_two.values)]
     out_halves = Halves(values, out_one.axes)
@@ -888,7 +888,12 @@
     w_out_grad = jnp.concatenate(out_halves.values, axis=-1).astype(BF16)
     out_sum = RingSum(shift)
     out_sum.parts = [lax.dynamic_index_in_dim(w_out_grad, shard_of(d)[0], 0, False) for d in range(n)]
-    for _ in range(n - 1):
+    out_sum.hop()
+    units = w_gate.shape[1]
+    mlp_grads = mlp_grads.astype(F32)
+    mlp_grads = mlp_grads[:, :units], mlp_grads[:, units : 2 * units], mlp_grads[:, 2 * units :].T
+    out_sum.moving, mlp_grads, totals = join(out_sum.moving, mlp_grads, totals)
+    for _ in range(n - 2):
         out_sum.hop()
     middle = w_qkv_grad.shape[-1] // 2
     qkv_halves = halves_of(
@@ -899,7 +904,7 @@
         qkv_halves, qkv_got = qkv_halves.send(step, batches)
         if step < steps - 1:
             qkv_halves = qkv_halves.add(qkv_got)
-    totals = total_over(totals, "tensor")
+    totals = total_over(totals, "tensor", 2)
     for s in range(3, n):
         entry_sum.send()
         entry_sum.parts[(s + 1) % n] = entry_part((s + 1) % n)
@@ -907,10 +912,6 @@
             entry_sum.add()
             entry_sum.moving, grads = join(entry_sum.moving, grads)
     grad_entry = total_of(entry_sum.parts[0], [entry_sum.moving])
-    units = w_gate.shape[1]
-    mlp_grads = mlp_grads.astype(F32)
-    mlp_grads = mlp_grads[:, :units], mlp_grads[:, units : 2 * units], mlp_grads[:, 2 * units :].T
-    out_sum.moving, mlp_grads = join(out_sum.moving, mlp_grads)
     w_out_grad = total_of(out_sum.parts[0], [out_sum.moving])
     w_qkv_grad = jnp.concatenate(qkv_halves.add(qkv_got).values, axis=-1)
 

time: 596 us -> 596 us (level)
    ppermute x27, waiting for transfers between devices: 183 us -> 167 us  [local(): lax.ppermute(v, 'tensor', [(i, (i + d) % n) for i in range(n)])]
    ppermute x22, waiting for transfers between devices: 34.9 us -> 45.5 us  [exchange(): return lax.ppermute(value, axis, [(i, i ^ step) for i in range(size)])]
  transfers between devices with their start and end apart: 52 -> 52, of which waited for: 23 -> 26; matrix products, arithmetic and copies ran while one was open for 8% -> 9% of each run, Pallas kernels for 37% -> 36%
where the time goes in v4:
time: 596 us; the launch traced here: 588 us
  waiting for transfers between devices  216 us (36%)
  Pallas kernels  214 us (36%)
  starting transfers between devices  77.4 us (13%)
  other arithmetic  44.1 us (7%)
  local copies, waits for them, and re-layouts  21.1 us (4%)
  between operations  14.8 us (2%)
    ppermute x27, waiting for transfers between devices, local(): lax.ppermute(v, 'tensor', [(i, (i + d) % n) for i in range(n)])  167 us
    pallas_call x4, Pallas kernels, mlp_shard(): call(functools.partial(mlp_kernel, tiles), pltpu.PrefetchScalarGridSpec(n...  72.6 us
    ppermute x27, starting transfers between devices, local(): lax.ppermute(v, 'tensor', [(i, (i + d) % n) for i in range(n)])  49.9 us
    ppermute x22, waiting for transfers between devices, exchange(): return lax.ppermute(value, axis, [(i, i ^ step) for i in range(size)])  45.5 us
    pallas_call x2, Pallas kernels, rows_grad(): call(functools.partial(rows_grad_kernel, count), pltpu.PrefetchScalarGrid...  31.1 us
    ppermute x22, starting transfers between devices, exchange(): return lax.ppermute(value, axis, [(i, i ^ step) for i in range(size)])  27.1 us
    pallas_call x4, Pallas kernels, qkv_shard(): call(functools.partial(qkv_kernel, heads, kv_heads, dim), pltpu.PrefetchS...  20.6 us
    pallas_call x4, Pallas kernels, entry_shard(): call(entry_kernel, pltpu.PrefetchScalarGridSpec(num_scalar_prefetch=1, gr...  17.9 us
  transfers between devices with their start and end apart: 52, of which 26 were waited for; matrix products, arithmetic and copies ran while one was open for 9% of the time, Pallas kernels for 36%

profile of v4, /device:TPU:0, one launch (start us, length us, event | category | flops | bytes accessed | tf_op | source)
XLA Modules:
  0.0 587.8 jit_solution(10598987440609145521)
XLA Ops:
  9.6 3.1 collective-permute-start
  19.0 33.1 %collective-permute-done.x_ref = bf16[256,2048]{1,0:T(8,128)(2,1)} collective-permute-done((bf16[256,2048]{1,0:T(8,128)(2,1)}, bf16[256,2048]{1,0:T(8,128)(2,1)}, u32[]{:S(2)}, u32[]{:S(2)}) %collective-permute-start) | collective-permute-done | bytes 1048608 | tf_op jit(solution)/shard_map/ppermute | solution.py:733
  52.1 3.3 all-gather.6.cloned.1.call-done
  60.8 5.1 shard_map.237
  65.9 5.2 shard_map.238
  75.6 6.9 %collective-permute-done.1.x_ref = bf16[256,2048]{1,0:T(8,128)(2,1)} collective-permute-done((bf16[256,2048]{1,0:T(8,128)(2,1)}, bf16[256,2048]{1,0:T(8,128)(2,1)}, u32[]{:S(2)}, u32[]{:S(2)}) %collective-permute-start.1) | collective-permute-done | bytes 1048608 | tf_op jit(solution)/shard_map/ppermute | solution.py:733
  85.5 5.1 shard_map.239
  90.7 16.2 %collective-permute-done.5 = bf16[2,4,256,256]{3,2,1,0:T(8,128)(2,1)} collective-permute-done((bf16[2,4,256,256]{3,2,1,0:T(8,128)(2,1)S(1)}, bf16[2,4,256,256]{3,2,1,0:T(8,128)(2,1)}, u32[]{:S(2)}, u32[]{:S(2)}) %collective-permute-start.5) | collective-permute-done | bytes 1048608 | tf_op jit(solution)/shard_map/ppermute | solution.py:607
  114.1 5.1 shard_map.240
  119.2 9.5 %shard_map.241 = (bf16[4,256,512]{2,1,0:T(8,128)(2,1)S(1)}, f32[4,1024]{1,0:T(4,128)S(1)}) custom-call(s32[1]{0:T(128)} %bitcast.1.z_ref, bf16[1024,1024]{1,0:T(8,128)(2,1)} %get-tuple-element.217.side_ref.refs_4_, s32[1,1024]{1,0:T(1,128)S(1)} %bitcast.151), custom_call_target="tpu_custom_call" | custom-call | flops 2147483 | bytes 5242 | tf_op jit(solution)/shard_map/pallas_call | solution.py:183
  129.0 3.7 collective-permute-start.9
  132.8 12.7 %collective-permute-done.7.refs_1_ = bf16[256,512]{1,0:T(8,128)(2,1)S(1)} collective-permute-done((bf16[256,512]{1,0:T(8,128)(2,1)S(1)}, bf16[256,512]{1,0:T(8,128)(2,1)S(1)}, u32[]{:S(2)}, u32[]{:S(2)}) %collective-permute-start.7) | collective-permute-done | bytes 262176 | tf_op jit(solution)/shard_map/ppermute | solution.py:733
  145.5 18.7 %collective-permute-done.8.refs_2_ = bf16[256,512]{1,0:T(8,128)(2,1)S(1)} collective-permute-done((bf16[256,512]{1,0:T(8,128)(2,1)S(1)}, bf16[256,512]{1,0:T(8,128)(2,1)S(1)}, u32[]{:S(2)}, u32[]{:S(2)}) %collective-permute-start.8) | collective-permute-done | bytes 262176 | tf_op jit(solution)/shard_map/ppermute | solution.py:733
  164.2 8.7 %shard_map.242 = (f32[256,2048]{1,0:T(8,128)}, bf16[256,2048]{1,0:T(8,128)(2,1)}) custom-call(s32[3]{0:T(128)S(1)} %pad_add_fusion.place_ref, bf16[256,512]{1,0:T(8,128)(2,1)S(1)} %get-tuple-element.223.refs_0_, bf16[256,512]{1,0:T(8,128)(2,1)S(1)} %collective-permute-done.7.refs_1_, bf16[256,512]{1,0:T(8,128)(2,1)S(1)} %collective-permute-done.8.refs_2_, ...), custom_call_target="tpu_custom_call" | custom-call | flops 2147483 | bytes 13631 | tf_op jit(solution)/shard_map/pallas_call | solution.py:308
  172.8 20.8 %collective-permute-start.11 = (bf16[256,2048]{1,0:T(8,128)(2,1)}, bf16[256,2048]{1,0:T(8,128)(2,1)S(1)}, u32[]{:S(2)}, u32[]{:S(2)}) collective-permute-start(bf16[256,2048]{1,0:T(8,128)(2,1)} %get-tuple-element.229.x_ref), channel_id=1, source_target_pairs={{0,1},{1,2},{2,3},{3,0},{4,5},{5,6},{6,7},{7,4},{8,9},{9,10},{10,1... | collective-permute-start | bytes 3145736 | tf_op jit(solution)/shard_map/ppermute | solution.py:733
  193.6 18.1 %shard_map.243 = (bf16[1024,1536]{1,0:T(8,128)(2,1)}, bf16[1024,1536]{1,0:T(8,128)(2,1)}, bf16[1024,1536]{1,0:T(8,128)(2,1)}, bf16[1024,2048]{1,0:T(8,128)(2,1)}...) custom-call(s32[1]{0:T(128)} %bitcast.14.sid_ref, bf16[256,2048]{1,0:T(8,128)(2,1)} %get-tuple-element.229.x_ref, ...), custom_call_target="tpu_custom_call" | custom-call | flops 9663676 | bytes 26476 | tf_op jit(solution)/shard_map/pallas_call | solution.py:388
  211.7 19.1 %collective-permute-done.11.x_ref = bf16[256,2048]{1,0:T(8,128)(2,1)S(1)} collective-permute-done((bf16[256,2048]{1,0:T(8,128)(2,1)}, bf16[256,2048]{1,0:T(8,128)(2,1)S(1)}, u32[]{:S(2)}, u32[]{:S(2)}) %collective-permute-start.11) | collective-permute-done | bytes 1048608 | tf_op jit(solution)/shard_map/ppermute | solution.py:733
  231.8 3.2 collective-permute-start.12
  234.9 23.8 %collective-permute-done.12.x_ref = bf16[256,2048]{1,0:T(8,128)(2,1)} collective-permute-done((bf16[256,2048]{1,0:T(8,128)(2,1)S(1)}, bf16[256,2048]{1,0:T(8,128)(2,1)}, u32[]{:S(2)}, u32[]{:S(2)}) %collective-permute-start.12) | collective-permute-done | bytes 1048608 | tf_op jit(solution)/shard_map/ppermute | solution.py:733
  260.0 18.1 %shard_map.244 = (bf16[1024,1536]{1,0:T(8,128)(2,1)}, bf16[1024,1536]{1,0:T(8,128)(2,1)}, bf16[1024,1536]{1,0:T(8,128)(2,1)}, bf16[1024,2048]{1,0:T(8,128)(2,1)}...) custom-call(s32[1]{0:T(128)} %bitcast.sid_ref, ...), custom_call_target="tpu_custom_call", output_to_operand_aliasing={{0}: (6, {}), {1}: (7, {}), {2}: (8, {}), {3}: (9, {})} | custom-call | flops 9663676 | bytes 26476 | tf_op jit(solution)/shard_map/pallas_call | solution.py:388
  278.1 6.8 %collective-permute-done.13.x_ref = bf16[256,2048]{1,0:T(8,128)(2,1)S(1)} collective-permute-done((bf16[256,2048]{1,0:T(8,128)(2,1)}, bf16[256,2048]{1,0:T(8,128)(2,1)S(1)}, u32[]{:S(2)}, u32[]{:S(2)}) %collective-permute-start.13) | collective-permute-done | bytes 1048608 | tf_op jit(solution)/shard_map/ppermute | solution.py:733
  285.1 18.2 %shard_map.245 = (bf16[1024,1536]{1,0:T(8,128)(2,1)}, bf16[1024,1536]{1,0:T(8,128)(2,1)}, bf16[1024,1536]{1,0:T(8,128)(2,1)}, bf16[1024,2048]{1,0:T(8,128)(2,1)}...) custom-call(s32[1]{0:T(128)} %bitcast.19.sid_ref, ...), custom_call_target="tpu_custom_call", output_to_operand_aliasing={{0}: (6, {}), {1}: (7, {}), {2}: (8, {}), {3}: (9, {})} | custom-call | flops 9663676 | bytes 26476 | tf_op jit(solution)/shard_map/pallas_call | solution.py:388
  303.3 7.0 %collective-permute-done.14 = bf16[256,2048]{1,0:T(8,128)(2,1)S(1)} collective-permute-done((bf16[256,2048]{1,0:T(8,128)(2,1)}, bf16[256,2048]{1,0:T(8,128)(2,1)S(1)}, u32[]{:S(2)}, u32[]{:S(2)}) %collective-permute-start.14) | collective-permute-done | bytes 1048608 | tf_op jit(solution)/shard_map/ppermute | solution.py:733
  312.0 18.2 %shard_map.246 = (bf16[1024,1536]{1,0:T(8,128)(2,1)}, bf16[1024,1536]{1,0:T(8,128)(2,1)}, bf16[1024,1536]{1,0:T(8,128)(2,1)}, bf16[1024,2048]{1,0:T(8,128)(2,1)}...) custom-call(s32[1]{0:T(128)} %bitcast.4.sid_ref, ...), custom_call_target="tpu_custom_call", output_to_operand_aliasing={{0}: (6, {}), {1}: (7, {}), {2}: (8, {}), {3}: (9, {})} | custom-call | flops 9663676 | bytes 26476 | tf_op jit(solution)/shard_map/pallas_call | solution.py:388
  330.2 5.9 collective-permute-done.15
  339.7 12.2 %shard_map.247.refs_2_ = bf16[8,256,4608]{2,1,0:T(8,128)(2,1)} custom-call(bf16[1024,2048]{1,0:T(8,128)(2,1)} %all-gather.4.cloned.1.call-done.go_ref.x_ref, bf16[1024,1536]{1,0:T(8,128)(2,1)} %get-tuple-element.292.refs_0_), custom_call_target="tpu_custom_call" | custom-call | flops 6442450 | bytes 13631 | tf_op jit(solution)/shard_map/pallas_call | solution.py:552
  351.9 18.9 %shard_map.248 = bf16[8,256,4608]{2,1,0:T(8,128)(2,1)} custom-call(bf16[1024,2048]{1,0:T(8,128)(2,1)} %get-tuple-element.288.x_ref, bf16[1024,1536]{1,0:T(8,128)(2,1)} %get-tuple-element.289.refs_0_, bf16[1024,1536]{1,0:T(8,128)(2,1)} %get-tuple-element.290.refs_1_, bf16[8,256,4608]{2,1,0:T(8,128)(2,1)} %shard_map.247.refs_2_), custom_call_target="tpu_custom_call", output_to_operand_aliasing={{}: (3, {})} | custom-call | flops 12884901 | bytes 23068 | tf_op jit(solution)/shard_map/pallas_call | solution.py:552
  373.6 11.9 %shard_map.249 = (bf16[4,256,512]{2,1,0:T(8,128)(2,1)S(1)}, f32[256,2048]{1,0:T(8,128)}, bf16[256,2048]{1,0:T(8,128)(2,1)}, f32[1,2048]{1,0:T(1,128)S(1)}) custom-call(s32[3]{0:T(128)S(1)} %pad_add_fusion.place_ref, bf16[256,2048]{1,0:T(8,128)(2,1)} %get-tuple-element.283.own_part_ref, bf16[256,2048]{1,0:T(8,128)(2,1)} %go_ref.3, ...), custom_call_target="tpu_custom_call" | custom-call | flops 2147483 | bytes 18874 | tf_op jit(solution)/shard_map/pallas_call | solution.py:444
  385.6 2.7 collective-permute-start.19
  390.7 5.5 shard_map.250
  396.7 6.6 %collective-permute-done.20.refs_2_ = bf16[256,512]{1,0:T(8,128)(2,1)S(1)} collective-permute-done((bf16[256,512]{1,0:T(8,128)(2,1)S(1)}, bf16[256,512]{1,0:T(8,128)(2,1)S(1)}, u32[]{:S(2)}, u32[]{:S(2)}) %collective-permute-start.20) | collective-permute-done | bytes 262176 | tf_op jit(solution)/shard_map/ppermute | solution.py:733
  403.2 4.7 collective-permute-start.23
  408.1 14.8 %shard_map.251 = (bf16[1024,1024]{1,0:T(8,128)(2,1)}, f32[8,128]{1,0:T(8,128)S(1)}) custom-call(s32[1]{0:T(128)} %bitcast.1.z_ref, bf16[256,512]{1,0:T(8,128)(2,1)S(1)} %get-tuple-element.301.refs_0_, bf16[256,512]{1,0:T(8,128)(2,1)S(1)} %collective-permute-done.19.refs_1_, bf16[256,512]{1,0:T(8,128)(2,1)S(1)} %collective-permute-done.20.refs_2_, ...), custom_call_target="tpu_custom_call" | custom-call | flops 5368709 | bytes 12582 | tf_op jit(solution)/shard_map/pallas_call | solution.py:262
  425.7 5.0 shard_map.252
  430.7 8.6 %shard_map.253 = (bf16[4,2,512,128]{3,2,1,0:T(8,128)(2,1)}, bf16[4,2,512,128]{3,2,1,0:T(8,128)(2,1)}, bf16[4,2,512,128]{3,2,1,0:T(8,128)(2,1)}, bf16[4,2,512,128]{3,2,1,0:T(8,128)(2,1)}) custom-call(s32[4]{0:T(128)S(1)} %get-tuple-element.399.place_ref, bf16[256,512]{1,0:T(8,128)(2,1)S(1)} %get-tuple-element.223.refs_0_, ...), custom_call_target="tpu_custom_call" | custom-call | flops 1073741 | bytes 4194 | tf_op jit(solution)/shard_map/pallas_call | solution.py:499
  439.3 4.6 collective-permute-done.24
  452.6 4.4 shard_map.254
  456.9 6.5 %shard_map.255 = (bf16[4,256,1024]{2,1,0:T(8,128)(2,1)}, f32[4,256,128]{2,1,0:T(8,128)S(1)}) custom-call(s32[1]{0:T(128)S(6)} %sub.19.side_ref, bf16[1024,2048]{1,0:T(8,128)(2,1)} %get-tuple-element.322.entry_ref, bf16[1024,1024]{1,0:T(8,128)(2,1)} %get-tuple-element.350.grad_ref, bf16[2048,1024]{1,0:T(8,128)(2,1)} %pad_maximum_fusion.w_ref), custom_call_target="tpu_custom_call" | custom-call | flops 2147483 | bytes 14680 | tf_op jit(solution)/shard_map/pallas_call | solution.py:584
  463.5 6.5 %shard_map.256 = (bf16[4,256,1024]{2,1,0:T(8,128)(2,1)}, f32[4,256,128]{2,1,0:T(8,128)S(1)}) custom-call(s32[1]{0:T(128)} %bitcast.3.side_ref, bf16[1024,2048]{1,0:T(8,128)(2,1)} %get-tuple-element.322.entry_ref, bf16[1024,1024]{1,0:T(8,128)(2,1)} %get-tuple-element.350.grad_ref, bf16[2048,1024]{1,0:T(8,128)(2,1)} %pad_maximum_fusion.w_ref), custom_call_target="tpu_custom_call" | custom-call | flops 2147483 | bytes 14680 | tf_op jit(solution)/shard_map/pallas_call | solution.py:584
  474.7 7.6 %collective-permute-done.27 = bf16[256,1024]{1,0:T(8,128)(2,1)} collective-permute-done((bf16[256,1024]{1,0:T(8,128)(2,1)S(1)}, bf16[256,1024]{1,0:T(8,128)(2,1)}, u32[]{:S(2)}, u32[]{:S(2)}) %collective-permute-start.27) | collective-permute-done | bytes 524320 | tf_op jit(solution)/shard_map/ppermute | solution.py:733
  493.1 4.4 shard_map.257
  497.5 15.9 %collective-permute-done.36 = f32[1,4352]{1,0:T(1,128)S(1)} collective-permute-done((f32[1,4352]{1,0:T(1,128)S(1)}, f32[1,4352]{1,0:T(1,128)S(1)}, u32[]{:S(2)}, u32[]{:S(2)}) %collective-permute-start.36) | collective-permute-done | bytes 17440 | tf_op jit(solution)/shard_map/ppermute | solution.py:607
  526.7 4.1 shard_map.258
  532.1 3.0 collective-permute-done.39
  540.1 7.8 %collective-permute-done.43 = bf16[2,256,512]{2,1,0:T(8,128)(2,1)S(1)} collective-permute-done((bf16[2,256,512]{2,1,0:T(8,128)(2,1)S(1)}, bf16[2,256,512]{2,1,0:T(8,128)(2,1)S(1)}, u32[]{:S(2)}, u32[]{:S(2)}) %collective-permute-start.43) | collective-permute-done | bytes 524320 | tf_op jit(solution)/shard_map/ppermute | solution.py:607
  563.5 3.4 collective-permute-start.42
  567.8 3.2 copy.54
  573.2 7.0 %collective-permute-done.48 = bf16[512,256]{1,0:T(8,128)(2,1)S(1)} collective-permute-done((bf16[512,256]{1,0:T(8,128)(2,1)S(1)}, bf16[512,256]{1,0:T(8,128)(2,1)S(1)}, u32[]{:S(2)}, u32[]{:S(2)}) %collective-permute-start.48) | collective-permute-done | bytes 262176 | tf_op jit(solution)/shard_map/ppermute | solution.py:733
  (250 shorter events, 108.3 us)
Async XLA Ops:
  7.2 48.1 %all-gather.6.cloned.1.call-start = ((), (), s32[]{:S(2)}) async-start(), calls=%async_computation.3 | async-start | bytes 1310720 | tf_op jit(solution)/shard_map/all_gather | solution.py:743
  9.5 249.2 %all-gather.4.cloned.1.call-start = ((), (), s32[]{:S(2)}) async-start(), calls=%async_computation.1 | async-start | bytes 5242880 | tf_op jit(solution)/shard_map/all_gather | solution.py:776
  9.6 42.5 %collective-permute-start = (bf16[256,2048]{1,0:T(8,128)(2,1)}, bf16[256,2048]{1,0:T(8,128)(2,1)}, u32[]{:S(2)}, u32[]{:S(2)}) collective-permute-start(bf16[256,2048]{1,0:T(8,128)(2,1)} %refs_6_.1), channel_id=1, source_target_pairs={{0,1},{1,2},{2,3},{3,0},{4,5},{5,6},{6,7},{7,4},{8,9},{9,10},{10,1... | collective-permute-start | bytes 3145736 | tf_op jit(solution)/shard_map/ppermute | solution.py:733
  55.3 27.2 %collective-permute-start.1 = (bf16[256,2048]{1,0:T(8,128)(2,1)}, bf16[256,2048]{1,0:T(8,128)(2,1)}, u32[]{:S(2)}, u32[]{:S(2)}) collective-permute-start(bf16[256,2048]{1,0:T(8,128)(2,1)} %collective-permute-done.x_ref), channel_id=1, source_target_pairs={{0,1},{1,2},{2,3},{3,0},{4,5},{5,6},{6,7},{7,4},{8,9},{9,10},{10,1... | collective-permute-start | bytes 3145736 | tf_op jit(solution)/shard_map/ppermute | solution.py:733
  57.7 13.8 %collective-permute-start.2 = (bf16[4,256,256]{2,1,0:T(8,128)(2,1)S(1)}, bf16[4,256,256]{2,1,0:T(8,128)(2,1)S(1)}, u32[]{:S(2)}, u32[]{:S(2)}) collective-permute-start(bf16[4,256,256]{2,1,0:T(8,128)(2,1)S(1)} %get-tuple-element.429), channel_id=1, source_target_pairs={{0,8},{4,12},{8,0},{12,4},{16,24},{20,28},{24,16},{28,20},{1,9},{5... | collective-permute-start | bytes 1572872 | tf_op jit(solution)/shard_map/ppermute | solution.py:607
  59.2 14.3 %collective-permute-start.3 = (bf16[4,256,256]{2,1,0:T(8,128)(2,1)}, bf16[4,256,256]{2,1,0:T(8,128)(2,1)}, u32[]{:S(2)}, u32[]{:S(2)}) collective-permute-start(bf16[4,256,256]{2,1,0:T(8,128)(2,1)} %get-tuple-element.428), channel_id=1, source_target_pairs={{0,16},{4,20},{8,24},{12,28},{16,0},{20,4},{24,8},{28,12},{1,17},{... | collective-permute-start | bytes 1572872 | tf_op jit(solution)/shard_map/ppermute | solution.py:607
  82.5 24.3 %collective-permute-start.5 = (bf16[2,4,256,256]{3,2,1,0:T(8,128)(2,1)S(1)}, bf16[2,4,256,256]{3,2,1,0:T(8,128)(2,1)}, u32[]{:S(2)}, u32[]{:S(2)}) collective-permute-start(bf16[2,4,256,256]{3,2,1,0:T(8,128)(2,1)S(1)} %pad_maximum_fusion.4), channel_id=1, source_target_pairs={{0,16},{4,20},{8,24},{12,28},{16,0},{20,4},{24,8},{28,12},{1,17},{... | collective-permute-start | bytes 3145736 | tf_op jit(solution)/shard_map/ppermute | solution.py:607
  84.1 24.3 %collective-permute-start.6 = (bf16[2,4,256,256]{3,2,1,0:T(8,128)(2,1)}, bf16[2,4,256,256]{3,2,1,0:T(8,128)(2,1)}, u32[]{:S(2)}, u32[]{:S(2)}) collective-permute-start(bf16[2,4,256,256]{3,2,1,0:T(8,128)(2,1)} %pad_maximum_fusion.5), channel_id=1, source_target_pairs={{0,8},{4,12},{8,0},{12,4},{16,24},{20,28},{24,16},{28,20},{1,9},{5... | collective-permute-start | bytes 3145736 | tf_op jit(solution)/shard_map/ppermute | solution.py:607
  85.5 25.8 %collective-permute-start.4 = (bf16[256,2048]{1,0:T(8,128)(2,1)}, bf16[256,2048]{1,0:T(8,128)(2,1)}, u32[]{:S(2)}, u32[]{:S(2)}) collective-permute-start(bf16[256,2048]{1,0:T(8,128)(2,1)} %collective-permute-done.1.x_ref), channel_id=1, source_target_pairs={{0,1},{1,2},{2,3},{3,0},{4,5},{5,6},{6,7},{7,4},{8,9},{9,10},{10,1... | collective-permute-start | bytes 3145736 | tf_op jit(solution)/shard_map/ppermute | solution.py:733
  113.7 50.4 %collective-permute-start.10 = (bf16[4,4,512,256]{3,2,1,0:T(8,128)(2,1)}, bf16[4,4,512,256]{3,2,1,0:T(8,128)(2,1)}, u32[]{:S(2)}, u32[]{:S(2)}) collective-permute-start(bf16[4,4,512,256]{3,2,1,0:T(8,128)(2,1)} %pad_maximum_fusion.1.refs_4_.own_ref), channel_id=1, source_target_pairs={{0,4},{4,0},{1,5},{5,1},{2,6},{6,2},{3,7},{7,3},{8,12},{12,8},{9,1... | collective-permute-start | bytes 12582920 | tf_op jit(solution)/shard_map/ppermute | solution.py:607
  113.7 442.3 %reduce-scatter.2.cloned.1.call-start = ((), (), s32[]{:S(2)}) async-start(), calls=%async_computation.2 | async-start | bytes 21233664 | tf_op jit(solution)/shard_map/reduce_scatter | solution.py:787
  128.8 16.6 %collective-permute-start.7 = (bf16[256,512]{1,0:T(8,128)(2,1)S(1)}, bf16[256,512]{1,0:T(8,128)(2,1)S(1)}, u32[]{:S(2)}, u32[]{:S(2)}) collective-permute-start(bf16[256,512]{1,0:T(8,128)(2,1)S(1)} %get-tuple-element.424), channel_id=1, source_target_pairs={{0,1},{1,2},{2,3},{3,0},{4,5},{5,6},{6,7},{7,4},{8,9},{9,10},{10,1... | collective-permute-start | bytes 786440 | tf_op jit(solution)/shard_map/ppermute | solution.py:733
  128.9 35.2 %collective-permute-start.8 = (bf16[256,512]{1,0:T(8,128)(2,1)S(1)}, bf16[256,512]{1,0:T(8,128)(2,1)S(1)}, u32[]{:S(2)}, u32[]{:S(2)}) collective-permute-start(bf16[256,512]{1,0:T(8,128)(2,1)S(1)} %get-tuple-element.423), channel_id=1, source_target_pairs={{0,2},{1,3},{2,0},{3,1},{4,6},{5,7},{6,4},{7,5},{8,10},{9,11},{10,... | collective-permute-start | bytes 786440 | tf_op jit(solution)/shard_map/ppermute | solution.py:733
  129.0 35.2 %collective-permute-start.9 = (bf16[256,512]{1,0:T(8,128)(2,1)S(1)}, bf16[256,512]{1,0:T(8,128)(2,1)S(1)}, u32[]{:S(2)}, u32[]{:S(2)}) collective-permute-start(bf16[256,512]{1,0:T(8,128)(2,1)S(1)} %get-tuple-element.422), channel_id=1, source_target_pairs={{0,3},{1,0},{2,1},{3,2},{4,7},{5,4},{6,5},{7,6},{8,11},{9,8},{10,9... | collective-permute-start | bytes 786440 | tf_op jit(solution)/shard_map/ppermute | solution.py:733
  172.8 58.0 %collective-permute-start.11 = (bf16[256,2048]{1,0:T(8,128)(2,1)}, bf16[256,2048]{1,0:T(8,128)(2,1)S(1)}, u32[]{:S(2)}, u32[]{:S(2)}) collective-permute-start(bf16[256,2048]{1,0:T(8,128)(2,1)} %get-tuple-element.229.x_ref), channel_id=1, source_target_pairs={{0,1},{1,2},{2,3},{3,0},{4,5},{5,6},{6,7},{7,4},{8,9},{9,10},{10,1... | collective-permute-start | bytes 3145736 | tf_op jit(solution)/shard_map/ppermute | solution.py:733
  231.8 26.9 %collective-permute-start.12 = (bf16[256,2048]{1,0:T(8,128)(2,1)S(1)}, bf16[256,2048]{1,0:T(8,128)(2,1)}, u32[]{:S(2)}, u32[]{:S(2)}) collective-permute-start(bf16[256,2048]{1,0:T(8,128)(2,1)S(1)} %collective-permute-done.11.x_ref), channel_id=1, source_target_pairs={{0,1},{1,2},{2,3},{3,0},{4,5},{5,6},{6,7},{7,4},{8,9},{9,10},{10,1... | collective-permute-start | bytes 3145736 | tf_op jit(solution)/shard_map/ppermute | solution.py:733
  258.7 26.2 %collective-permute-start.13 = (bf16[256,2048]{1,0:T(8,128)(2,1)}, bf16[256,2048]{1,0:T(8,128)(2,1)S(1)}, u32[]{:S(2)}, u32[]{:S(2)}) collective-permute-start(bf16[256,2048]{1,0:T(8,128)(2,1)} %collective-permute-done.12.x_ref), channel_id=1, source_target_pairs={{0,1},{1,2},{2,3},{3,0},{4,5},{5,6},{6,7},{7,4},{8,9},{9,10},{10,1... | collective-permute-start | bytes 3145736 | tf_op jit(solution)/shard_map/ppermute | solution.py:733
  284.9 25.4 %collective-permute-start.14 = (bf16[256,2048]{1,0:T(8,128)(2,1)}, bf16[256,2048]{1,0:T(8,128)(2,1)S(1)}, u32[]{:S(2)}, u32[]{:S(2)}) collective-permute-start(bf16[256,2048]{1,0:T(8,128)(2,1)} %get-tuple-element.267), channel_id=1, source_target_pairs={{0,1},{1,2},{2,3},{3,0},{4,5},{5,6},{6,7},{7,4},{8,9},{9,10},{10,1... | collective-permute-start | bytes 3145736 | tf_op jit(solution)/shard_map/ppermute | solution.py:733
  311.9 24.2 %collective-permute-start.15 = (bf16[256,2048]{1,0:T(8,128)(2,1)S(1)}, bf16[256,2048]{1,0:T(8,128)(2,1)S(1)}, u32[]{:S(2)}, u32[]{:S(2)}) collective-permute-start(bf16[256,2048]{1,0:T(8,128)(2,1)S(1)} %add_convert_fusion.6), channel_id=1, source_target_pairs={{0,1},{1,2},{2,3},{3,0},{4,5},{5,6},{6,7},{7,4},{8,9},{9,10},{10,1... | collective-permute-start | bytes 3145736 | tf_op jit(solution)/shard_map/ppermute | solution.py:733
  338.7 34.6 %collective-permute-start.16 = (bf16[256,2048]{1,0:T(8,128)(2,1)}, bf16[256,2048]{1,0:T(8,128)(2,1)}, u32[]{:S(2)}, u32[]{:S(2)}) collective-permute-start(bf16[256,2048]{1,0:T(8,128)(2,1)} %add_convert_fusion.5), channel_id=1, source_target_pairs={{0,1},{1,2},{2,3},{3,0},{4,5},{5,6},{6,7},{7,4},{8,9},{9,10},{10,1... | collective-permute-start | bytes 3145736 | tf_op jit(solution)/shard_map/ppermute | solution.py:733
  339.7 33.6 %collective-permute-start.17 = (bf16[256,1024]{1,0:T(8,128)(2,1)}, bf16[256,1024]{1,0:T(8,128)(2,1)S(1)}, u32[]{:S(2)}, u32[]{:S(2)}) collective-permute-start(bf16[256,1024]{1,0:T(8,128)(2,1)} %get-tuple-element.421), channel_id=1, source_target_pairs={{0,1},{1,2},{2,3},{3,0},{4,5},{5,6},{6,7},{7,4},{8,9},{9,10},{10,1... | collective-permute-start | bytes 1572872 | tf_op jit(solution)/shard_map/ppermute | solution.py:733
  373.4 12.1 %collective-permute-start.18 = (bf16[256,1024]{1,0:T(8,128)(2,1)}, bf16[256,1024]{1,0:T(8,128)(2,1)S(1)}, u32[]{:S(2)}, u32[]{:S(2)}) collective-permute-start(bf16[256,1024]{1,0:T(8,128)(2,1)} %get-tuple-element.420), channel_id=1, source_target_pairs={{0,1},{1,2},{2,3},{3,0},{4,5},{5,6},{6,7},{7,4},{8,9},{9,10},{10,1... | collective-permute-start | bytes 1572872 | tf_op jit(solution)/shard_map/ppermute | solution.py:733
  385.6 11.1 %collective-permute-start.19 = (bf16[256,512]{1,0:T(8,128)(2,1)S(1)}, bf16[256,512]{1,0:T(8,128)(2,1)S(1)}, u32[]{:S(2)}, u32[]{:S(2)}) collective-permute-start(bf16[256,512]{1,0:T(8,128)(2,1)S(1)} %get-tuple-element.418), channel_id=1, source_target_pairs={{0,1},{1,2},{2,3},{3,0},{4,5},{5,6},{6,7},{7,4},{8,9},{9,10},{10,1... | collective-permute-start | bytes 786440 | tf_op jit(solution)/shard_map/ppermute | solution.py:733
  388.3 14.9 %collective-permute-start.20 = (bf16[256,512]{1,0:T(8,128)(2,1)S(1)}, bf16[256,512]{1,0:T(8,128)(2,1)S(1)}, u32[]{:S(2)}, u32[]{:S(2)}) collective-permute-start(bf16[256,512]{1,0:T(8,128)(2,1)S(1)} %get-tuple-element.417), channel_id=1, source_target_pairs={{0,2},{1,3},{2,0},{3,1},{4,6},{5,7},{6,4},{7,5},{8,10},{9,11},{10,... | collective-permute-start | bytes 786440 | tf_op jit(solution)/shard_map/ppermute | solution.py:733
  390.0 13.2 %collective-permute-start.21 = (bf16[256,512]{1,0:T(8,128)(2,1)S(1)}, bf16[256,512]{1,0:T(8,128)(2,1)S(1)}, u32[]{:S(2)}, u32[]{:S(2)}) collective-permute-start(bf16[256,512]{1,0:T(8,128)(2,1)S(1)} %get-tuple-element.416), channel_id=1, source_target_pairs={{0,3},{1,0},{2,1},{3,2},{4,7},{5,4},{6,5},{7,6},{8,11},{9,8},{10,9... | collective-permute-start | bytes 786440 | tf_op jit(solution)/shard_map/ppermute | solution.py:733
  403.2 19.7 %collective-permute-start.22 = (bf16[4,4,512,256]{3,2,1,0:T(8,128)(2,1)}, bf16[4,4,512,256]{3,2,1,0:T(8,128)(2,1)S(1)}, u32[]{:S(2)}, u32[]{:S(2)}) collective-permute-start(bf16[4,4,512,256]{3,2,1,0:T(8,128)(2,1)} %shard_map.250), channel_id=1, source_target_pairs={{0,4},{4,0},{1,5},{5,1},{2,6},{6,2},{3,7},{7,3},{8,12},{12,8},{9,1... | collective-permute-start | bytes 12582920 | tf_op jit(solution)/shard_map/ppermute | solution.py:607
  403.2 19.7 %collective-permute-start.23 = (bf16[256,1024]{1,0:T(8,128)(2,1)S(1)}, bf16[256,1024]{1,0:T(8,128)(2,1)S(1)}, u32[]{:S(2)}, u32[]{:S(2)}) collective-permute-start(bf16[256,1024]{1,0:T(8,128)(2,1)S(1)} %get-tuple-element.309), channel_id=1, source_target_pairs={{0,1},{1,2},{2,3},{3,0},{4,5},{5,6},{6,7},{7,4},{8,9},{9,10},{10,1... | collective-permute-start | bytes 1572872 | tf_op jit(solution)/shard_map/ppermute | solution.py:733
  407.9 31.4 %collective-permute-start.25 = (bf16[256,1024]{1,0:T(8,128)(2,1)S(1)}, bf16[256,1024]{1,0:T(8,128)(2,1)S(1)}, u32[]{:S(2)}, u32[]{:S(2)}) collective-permute-start(bf16[256,1024]{1,0:T(8,128)(2,1)S(1)} %get-tuple-element.318), channel_id=1, source_target_pairs={{0,1},{1,2},{2,3},{3,0},{4,5},{5,6},{6,7},{7,4},{8,9},{9,10},{10,1... | collective-permute-start | bytes 1572872 | tf_op jit(solution)/shard_map/ppermute | solution.py:733
  423.2 20.8 %collective-permute-start.24 = (bf16[256,1024]{1,0:T(8,128)(2,1)S(1)}, bf16[256,1024]{1,0:T(8,128)(2,1)S(1)}, u32[]{:S(2)}, u32[]{:S(2)}) collective-permute-start(bf16[256,1024]{1,0:T(8,128)(2,1)S(1)} %add_convert_fusion.8), channel_id=1, source_target_pairs={{0,1},{1,2},{2,3},{3,0},{4,5},{5,6},{6,7},{7,4},{8,9},{9,10},{10,1... | collective-permute-start | bytes 1572872 | tf_op jit(solution)/shard_map/ppermute | solution.py:733
  443.9 28.1 %collective-permute-start.26 = (bf16[256,2048]{1,0:T(8,128)(2,1)}, bf16[256,2048]{1,0:T(8,128)(2,1)}, u32[]{:S(2)}, u32[]{:S(2)}) collective-permute-start(bf16[256,2048]{1,0:T(8,128)(2,1)} %shard_map.252), channel_id=1, source_target_pairs={{0,1},{1,2},{2,3},{3,0},{4,5},{5,6},{6,7},{7,4},{8,9},{9,10},{10,1... | collective-permute-start | bytes 3145736 | tf_op jit(solution)/shard_map/ppermute | solution.py:733
  446.1 36.2 %collective-permute-start.27 = (bf16[256,1024]{1,0:T(8,128)(2,1)S(1)}, bf16[256,1024]{1,0:T(8,128)(2,1)}, u32[]{:S(2)}, u32[]{:S(2)}) collective-permute-start(bf16[256,1024]{1,0:T(8,128)(2,1)S(1)} %add_convert_fusion.7), channel_id=1, source_target_pairs={{0,1},{1,2},{2,3},{3,0},{4,5},{5,6},{6,7},{7,4},{8,9},{9,10},{10,1... | collective-permute-start | bytes 1572872 | tf_op jit(solution)/shard_map/ppermute | solution.py:733
  448.6 33.7 %collective-permute-start.28 = (bf16[2,2,512,128]{3,2,1,0:T(8,128)(2,1)S(1)}, bf16[2,2,512,128]{3,2,1,0:T(8,128)(2,1)}, u32[]{:S(2)}, u32[]{:S(2)}) collective-permute-start(bf16[2,2,512,128]{3,2,1,0:T(8,128)(2,1)S(1)} %get-tuple-element.412), channel_id=1, source_target_pairs={{0,8},{4,12},{8,0},{12,4},{16,24},{20,28},{24,16},{28,20},{1,9},{5... | collective-permute-start | bytes 1572872 | tf_op jit(solution)/shard_map/ppermute | solution.py:607
  450.2 32.1 %collective-permute-start.29 = (bf16[2,2,512,128]{3,2,1,0:T(8,128)(2,1)S(1)}, bf16[2,2,512,128]{3,2,1,0:T(8,128)(2,1)}, u32[]{:S(2)}, u32[]{:S(2)}) collective-permute-start(bf16[2,2,512,128]{3,2,1,0:T(8,128)(2,1)S(1)} %get-tuple-element.410), channel_id=1, source_target_pairs={{0,16},{4,20},{8,24},{12,28},{16,0},{20,4},{24,8},{28,12},{1,17},{... | collective-permute-start | bytes 1572872 | tf_op jit(solution)/shard_map/ppermute | solution.py:607
  482.3 31.1 %collective-permute-start.30 = (bf16[256,2048]{1,0:T(8,128)(2,1)}, bf16[256,2048]{1,0:T(8,128)(2,1)}, u32[]{:S(2)}, u32[]{:S(2)}) collective-permute-start(bf16[256,2048]{1,0:T(8,128)(2,1)} %add_convert_fusion.4), channel_id=1, source_target_pairs={{0,1},{1,2},{2,3},{3,0},{4,5},{5,6},{6,7},{7,4},{8,9},{9,10},{10,1... | collective-permute-start | bytes 3145736 | tf_op jit(solution)/shard_map/ppermute | solution.py:733
  484.4 31.6 %collective-permute-start.33 = (bf16[4,256,1024]{2,1,0:T(8,128)(2,1)}, bf16[4,256,1024]{2,1,0:T(8,128)(2,1)S(1)}, u32[]{:S(2)}, u32[]{:S(2)}) collective-permute-start(bf16[4,256,1024]{2,1,0:T(8,128)(2,1)} %get-tuple-element.339), channel_id=1, source_target_pairs={{0,4},{4,0},{1,5},{5,1},{2,6},{6,2},{3,7},{7,3},{8,12},{12,8},{9,1... | collective-permute-start | bytes 6291464 | tf_op jit(solution)/shard_map/ppermute | solution.py:607
  486.5 29.5 %collective-permute-start.31 = (bf16[2,2,512,128]{3,2,1,0:T(8,128)(2,1)S(1)}, bf16[2,2,512,128]{3,2,1,0:T(8,128)(2,1)S(1)}, u32[]{:S(2)}, u32[]{:S(2)}) collective-permute-start(bf16[2,2,512,128]{3,2,1,0:T(8,128)(2,1)S(1)} %get-tuple-element.408), channel_id=1, source_target_pairs={{0,8},{4,12},{8,0},{12,4},{16,24},{20,28},{24,16},{28,20},{1,9},{5... | collective-permute-start | bytes 1572872 | tf_op jit(solution)/shard_map/ppermute | solution.py:607
  487.0 29.0 %collective-permute-start.32 = (bf16[2,2,512,128]{3,2,1,0:T(8,128)(2,1)S(1)}, bf16[2,2,512,128]{3,2,1,0:T(8,128)(2,1)S(1)}, u32[]{:S(2)}, u32[]{:S(2)}) collective-permute-start(bf16[2,2,512,128]{3,2,1,0:T(8,128)(2,1)S(1)} %get-tuple-element.406), channel_id=1, source_target_pairs={{0,16},{4,20},{8,24},{12,28},{16,0},{20,4},{24,8},{28,12},{1,17},{... | collective-permute-start | bytes 1572872 | tf_op jit(solution)/shard_map/ppermute | solution.py:607
  489.0 24.4 %collective-permute-start.36 = (f32[1,4352]{1,0:T(1,128)S(1)}, f32[1,4352]{1,0:T(1,128)S(1)}, u32[]{:S(2)}, u32[]{:S(2)}) collective-permute-start(f32[1,4352]{1,0:T(1,128)S(1)} %add.226), channel_id=1, source_target_pairs={{0,16},{4,20},{8,24},{12,28},{16,0},{20,4},{24,8},{28,12},{1,17},{... | collective-permute-start | bytes 52232 | tf_op jit(solution)/shard_map/ppermute | solution.py:607
  518.8 13.2 %collective-permute-start.38 = (bf16[4,512,128]{2,1,0:T(8,128)(2,1)}, bf16[4,512,128]{2,1,0:T(8,128)(2,1)S(1)}, u32[]{:S(2)}, u32[]{:S(2)}) collective-permute-start(bf16[4,512,128]{2,1,0:T(8,128)(2,1)} %fusion.20), channel_id=1, source_target_pairs={{0,16},{4,20},{8,24},{12,28},{16,0},{20,4},{24,8},{28,12},{1,17},{... | collective-permute-start | bytes 1572872 | tf_op jit(solution)/shard_map/ppermute | solution.py:607
  522.3 12.8 %collective-permute-start.39 = (bf16[4,512,128]{2,1,0:T(8,128)(2,1)S(1)}, bf16[4,512,128]{2,1,0:T(8,128)(2,1)S(1)}, u32[]{:S(2)}, u32[]{:S(2)}) collective-permute-start(bf16[4,512,128]{2,1,0:T(8,128)(2,1)S(1)} %fusion.21), channel_id=1, source_target_pairs={{0,8},{4,12},{8,0},{12,4},{16,24},{20,28},{24,16},{28,20},{1,9},{5... | collective-permute-start | bytes 1572872 | tf_op jit(solution)/shard_map/ppermute | solution.py:607
  524.7 28.2 %collective-permute-start.37 = (bf16[256,2048]{1,0:T(8,128)(2,1)}, bf16[256,2048]{1,0:T(8,128)(2,1)S(1)}, u32[]{:S(2)}, u32[]{:S(2)}) collective-permute-start(bf16[256,2048]{1,0:T(8,128)(2,1)} %add_convert_fusion.3), channel_id=1, source_target_pairs={{0,1},{1,2},{2,3},{3,0},{4,5},{5,6},{6,7},{7,4},{8,9},{9,10},{10,1... | collective-permute-start | bytes 3145736 | tf_op jit(solution)/shard_map/ppermute | solution.py:733
  536.0 11.9 %collective-permute-start.43 = (bf16[2,256,512]{2,1,0:T(8,128)(2,1)S(1)}, bf16[2,256,512]{2,1,0:T(8,128)(2,1)S(1)}, u32[]{:S(2)}, u32[]{:S(2)}) collective-permute-start(bf16[2,256,512]{2,1,0:T(8,128)(2,1)S(1)} %dynamic-slice_bitcast_fusion.1), channel_id=1, source_target_pairs={{0,8},{4,12},{8,0},{12,4},{16,24},{20,28},{24,16},{28,20},{1,9},{5... | collective-permute-start | bytes 1572872 | tf_op jit(solution)/shard_map/ppermute | solution.py:607
  537.7 11.6 %collective-permute-start.45 = (bf16[2,256,512]{2,1,0:T(8,128)(2,1)S(1)}, bf16[2,256,512]{2,1,0:T(8,128)(2,1)S(1)}, u32[]{:S(2)}, u32[]{:S(2)}) collective-permute-start(bf16[2,256,512]{2,1,0:T(8,128)(2,1)S(1)} %dynamic-slice_bitcast_fusion), channel_id=1, source_target_pairs={{0,16},{4,20},{8,24},{12,28},{16,0},{20,4},{24,8},{28,12},{1,17},{... | collective-permute-start | bytes 1572872 | tf_op jit(solution)/shard_map/ppermute | solution.py:607
  539.5 21.1 %collective-permute-start.40 = (bf16[512,256]{1,0:T(8,128)(2,1)S(1)}, bf16[512,256]{1,0:T(8,128)(2,1)}, u32[]{:S(2)}, u32[]{:S(2)}) collective-permute-start(bf16[512,256]{1,0:T(8,128)(2,1)S(1)} %fusion.29), channel_id=1, source_target_pairs={{0,1},{1,2},{2,3},{3,0},{4,5},{5,6},{6,7},{7,4},{8,9},{9,10},{10,1... | collective-permute-start | bytes 786440 | tf_op jit(solution)/shard_map/ppermute | solution.py:733
  548.8 18.1 %collective-permute-start.44 = (bf16[256,512]{1,0:T(8,128)(2,1)}, bf16[256,512]{1,0:T(8,128)(2,1)S(1)}, u32[]{:S(2)}, u32[]{:S(2)}) collective-permute-start(bf16[256,512]{1,0:T(8,128)(2,1)} %fusion.24), channel_id=1, source_target_pairs={{0,16},{4,20},{8,24},{12,28},{16,0},{20,4},{24,8},{28,12},{1,17},{... | collective-permute-start | bytes 786440 | tf_op jit(solution)/shard_map/ppermute | solution.py:607
  561.7 9.3 %collective-permute-start.47 = (bf16[512,256]{1,0:T(8,128)(2,1)S(1)}, bf16[512,256]{1,0:T(8,128)(2,1)}, u32[]{:S(2)}, u32[]{:S(2)}) collective-permute-start(bf16[512,256]{1,0:T(8,128)(2,1)S(1)} %fusion.23), channel_id=1, source_target_pairs={{0,1},{1,2},{2,3},{3,0},{4,5},{5,6},{6,7},{7,4},{8,9},{9,10},{10,1... | collective-permute-start | bytes 786440 | tf_op jit(solution)/shard_map/ppermute | solution.py:733
  563.5 7.4 %collective-permute-start.42 = (f32[1,4352]{1,0:T(1,128)S(1)}, f32[1,4352]{1,0:T(1,128)S(1)}, u32[]{:S(2)}, u32[]{:S(2)}) collective-permute-start(f32[1,4352]{1,0:T(1,128)S(1)} %add.241), channel_id=1, source_target_pairs={{0,2},{1,3},{2,0},{3,1},{4,6},{5,7},{6,4},{7,5},{8,10},{9,11},{10,... | collective-permute-start | bytes 52232 | tf_op jit(solution)/shard_map/ppermute | solution.py:607
  572.0 8.2 %collective-permute-start.48 = (bf16[512,256]{1,0:T(8,128)(2,1)S(1)}, bf16[512,256]{1,0:T(8,128)(2,1)S(1)}, u32[]{:S(2)}, u32[]{:S(2)}) collective-permute-start(bf16[512,256]{1,0:T(8,128)(2,1)S(1)} %fusion.22), channel_id=1, source_target_pairs={{0,1},{1,2},{2,3},{3,0},{4,5},{5,6},{6,7},{7,4},{8,9},{9,10},{10,1... | collective-permute-start | bytes 786440 | tf_op jit(solution)/shard_map/ppermute | solution.py:733
  (48 other events, 506.2 us)
Sparse Core Ops, SparseCore 0:
  10.2 45.1 all-gather.5
  113.9 122.4 all-gather.3
  373.5 148.9 reduce-scatter.1
